TPU v7x, 32 devices: a whole 2x2x4 slice. The times are simulated.
32 devices in a mesh: dst: 8 (over y, x, core), src: 4 (over z).
Axes of the slice: x: 2, y: 2, z: 4, core: 2. Of those that a mesh axis runs over, the one named last changes fastest.
Arguments:
- features: bfloat16 [3072, 768], P(('src', 'dst')), may hold values from -6 to 6
- relation_weight: bfloat16 [768, 3, 256], replicated, may hold values from -0.21875 to 0.21875
- bias: bfloat16 [256], replicated, may hold values from -3 to 3
- block_values: bfloat16 [8, 4, 3, 16, 128, 128], P('dst', 'src'), may hold values from 0 to 0.06591797
- block_list: int32 [8, 4, 3, 16], P('dst', 'src'), may hold values from 0 to 17, as said below
- block_count: int32 [8, 4, 3], P('dst', 'src'), may hold values from 4 to 16, as said below
- cotangent: bfloat16 [3072, 256], P(('dst', 'src')), may hold values from -6 to 6
Outputs:
- output: bfloat16 [3072, 256], P(('dst', 'src'))
- weight_grad: float32 [768, 3, 256], replicated
- bias_grad: float32 [256], replicated
Inputs may be any that keep to these rules, and one draw needn't show every extreme that they name: `block_list`: within one tile and relation the 16 slots name different blocks. `block_count`: some tile and relation fills all 16 slots.
All inputs are finite; a program needn't handle non-finite values.
Results may differ from a plain program's by a relative error of at most 0.0075.
Values may be sent and summed in bfloat16 or wider, within the bound.
No kernel may reach another device: no remote copies, remote signals or barrier semaphores. Data moves between devices by JAX's collectives and lax.ppermute only.
A program may use at most 64 MiB of HBM per device.

v0:
```python
import jax
import jax.numpy as jnp
from jax import lax
from jax.sharding import PartitionSpec as P


def on_device(features, relation_weight, bias, block_values, block_list, block_count, cotangent):
    width = features.shape[1]
    relations = relation_weight.shape[1]
    hidden_width = relation_weight.shape[2]
    max_slots = block_values.shape[3]
    block_size = block_values.shape[5]
    weighted = block_values.reshape(relations, max_slots, block_size, block_size)
    slot_list = block_list.reshape(relations, max_slots)
    counts = block_count.reshape(relations, 1)
    live = lax.broadcasted_iota(jnp.int32, (relations, max_slots), 1) < counts
    weighted = weighted * live[:, :, None, None].astype(weighted.dtype)
    flat_weight = relation_weight.reshape(width, relations * hidden_width)
    gathered = lax.all_gather(features, "dst", axis=0, tiled=True)
    band_projected = jnp.dot(gathered, flat_weight, preferred_element_type=jnp.float32).astype(
        jnp.bfloat16
    )
    blocks_across = gathered.shape[0] // block_size
    band_rows = cotangent.shape[0] * lax.axis_size("src")
    blocks_down = band_rows // block_size
    column_index = slot_list % blocks_across
    row_index = slot_list // blocks_across
    source_blocks = gathered.reshape(blocks_across, block_size, width)
    projected_blocks = band_projected.reshape(blocks_across, block_size, relations, hidden_width)
    partial_total = jnp.zeros((blocks_down, block_size, hidden_width), jnp.float32)
    pieces = []
    for relation in range(relations):
        chosen = projected_blocks[column_index[relation], :, relation, :]
        blockwise = jnp.einsum(
            "bij,bjh->bih", weighted[relation], chosen, preferred_element_type=jnp.float32
        )
        partial_total = partial_total.at[row_index[relation]].add(blockwise)
        picked = source_blocks[column_index[relation]]
        spread = jnp.einsum(
            "bij,bjd->bid", weighted[relation], picked, preferred_element_type=jnp.float32
        )
        banded = (
            jnp.zeros((blocks_down, block_size, width), jnp.float32)
            .at[row_index[relation]]
            .add(spread)
        )
        pieces.append(banded.reshape(band_rows, width).astype(jnp.bfloat16))
    tile_features = jnp.stack(pieces, axis=1)
    message = lax.psum_scatter(
        partial_total.reshape(band_rows, hidden_width), "src", scatter_dimension=0, tiled=True
    )
    pre = message + bias.astype(jnp.float32)
    sigma = jax.nn.sigmoid(pre)
    output = (pre * sigma).astype(jnp.bfloat16)
    grad_pre = (cotangent.astype(jnp.float32) * sigma * (1.0 + pre * (1.0 - sigma))).astype(
        jnp.bfloat16
    )
    bias_term = jnp.sum(grad_pre.astype(jnp.float32), axis=0)
    band_grad = lax.all_gather(grad_pre, "src", axis=0, tiled=True)
    weight_term = jnp.einsum(
        "nrd,nh->drh", tile_features, band_grad, preferred_element_type=jnp.float32
    )
    weight_grad, bias_grad = lax.psum((weight_term, bias_term), ("dst", "src"))
    return (output, weight_grad, bias_grad)


def solution(mesh):
    in_specs = (
        P(("src", "dst"), None),
        P(),
        P(),
        P("dst", "src", None, None, None, None),
        P("dst", "src", None, None),
        P("dst", "src", None),
        P(("dst", "src"), None),
    )
    out_specs = (P(("dst", "src"), None), P(), P())
    return jax.shard_map(
        on_device, mesh=mesh, in_specs=in_specs, out_specs=out_specs, check_vma=False
    )
```

profile of v0, /device:TPU:1, one launch (start us, length us, event | category | flops | bytes accessed | tf_op | source)
XLA Modules:
  0.0 281.9 jit_solution(18440119538449607228)
XLA Ops:
  7.3 0.7 all-gather.2.cloned.1.call-update
  8.0 2.4 copy.11
  10.8 25.8 %all-gather.2.cloned.1.call-done = bf16[768,768]{1,0:T(8,128)(2,1)} async-done(((bf16[96,768]{1,0:T(8,128)(2,1)}), bf16[768,768]{1,0:T(8,128)(2,1)}) %all-gather.2.cloned.1.call-update) | async-done | bytes 1179664 | tf_op jit(solution)/shard_map/all_gather | solution.py:19
  36.5 2.7 convolution_convert_fusion
  39.3 1.9 reshape.355
  41.2 1.6 copy.13
  42.8 1.6 gather_fusion
  44.4 1.6 gather_fusion.1
  46.0 3.1 %fusion.10 = f32[16,128,256]{2,1,0:T(8,128)} fusion(bf16[16,128,256]{2,1,0:T(8,128)(2,1)} %gather_fusion, bf16[3,16,128,128]{3,2,1,0:T(8,128)(2,1)S(1)} %bitcast_multiply_fusion), kind=kOutput, calls=%fused_computation.25 | convolution fusion | flops 134217728 | bytes 3670016 | tf_op jit(solution)/shard_map/bij,bjh->bih/dot_general | solution.py:34
  49.1 1.8 fusion.12
  50.9 1.6 gather_fusion.2
  52.5 2.9 %fusion.14 = f32[16,128,256]{2,1,0:T(8,128)} fusion(bf16[16,128,256]{2,1,0:T(8,128)(2,1)} %gather_fusion.2, bf16[3,16,128,128]{3,2,1,0:T(8,128)(2,1)S(1)} %bitcast_multiply_fusion), kind=kOutput, calls=%fused_computation.29 | convolution fusion | flops 134217728 | bytes 3670016 | tf_op jit(solution)/shard_map/bij,bjh->bih/dot_general | solution.py:34
  55.5 3.5 %scatter_fusion = f32[3,128,256]{2,1,0:T(8,128)S(1)} fusion(f32[3,128,256]{2,1,0:T(8,128)S(1)} %broadcast_in_dim.2, s32[16]{0:T(128)S(1)} %get-tuple-element.20, f32[16,128,256]{2,1,0:T(8,128)} %fusion.10), kind=kCustom, calls=%fused_computation.6 | custom fusion | flops 524288 | bytes 6291520 | tf_op jit(solution)/shard_map/scatter-add | solution.py:37
  59.0 3.5 %scatter_fusion.1 = f32[3,128,256]{2,1,0:T(8,128)S(1)} fusion(f32[3,128,256]{2,1,0:T(8,128)S(1)} %scatter_fusion, s32[16]{0:T(128)S(1)} %get-tuple-element.19, f32[16,128,256]{2,1,0:T(8,128)} %fusion.12), kind=kCustom, calls=%fused_computation.7 | custom fusion | flops 524288 | bytes 6291520 | tf_op jit(solution)/shard_map/scatter-add | solution.py:37
  62.5 3.5 %scatter_fusion.2 = f32[3,128,256]{2,1,0:T(8,128)S(1)} fusion(f32[3,128,256]{2,1,0:T(8,128)S(1)} %scatter_fusion.1, s32[16]{0:T(128)S(1)} %get-tuple-element.18, f32[16,128,256]{2,1,0:T(8,128)} %fusion.14), kind=kCustom, calls=%fused_computation.8 | custom fusion | flops 524288 | bytes 6291520 | tf_op jit(solution)/shard_map/scatter-add | solution.py:37
  65.9 0.7 copy-done
  67.0 2.4 gather_fusion.3
  69.4 5.5 %fusion.9 = f32[16,128,768]{2,1,0:T(8,128)} fusion(bf16[16,128,768]{2,1,0:T(8,128)(2,1)} %gather_fusion.3, bf16[3,16,128,128]{3,2,1,0:T(8,128)(2,1)S(1)} %bitcast_multiply_fusion), kind=kOutput, calls=%fused_computation.24 | convolution fusion | flops 402653184 | bytes 9961472 | tf_op jit(solution)/shard_map/bij,bjd->bid/dot_general | solution.py:39
  75.0 9.2 %scatter_fusion.3 = f32[3,128,768]{2,1,0:T(8,128)S(1)} fusion(f32[3,128,768]{2,1,0:T(8,128)S(1)} %broadcast.135.clone.2, s32[16]{0:T(128)S(1)} %get-tuple-element.20, f32[16,128,768]{2,1,0:T(8,128)} %fusion.9), kind=kCustom, calls=%fused_computation.9 | custom fusion | flops 1572864 | bytes 18874432 | tf_op jit(solution)/shard_map/scatter-add | solution.py:45
  84.3 2.4 gather_fusion.4
  86.7 5.7 %fusion.11 = f32[16,128,768]{2,1,0:T(8,128)} fusion(bf16[16,128,768]{2,1,0:T(8,128)(2,1)} %gather_fusion.4, bf16[3,16,128,128]{3,2,1,0:T(8,128)(2,1)} %copy-done.2), kind=kOutput, calls=%fused_computation.26 | convolution fusion | flops 402653184 | bytes 9961472 | tf_op jit(solution)/shard_map/bij,bjd->bid/dot_general | solution.py:39
  92.5 9.2 %scatter_fusion.4 = f32[3,128,768]{2,1,0:T(8,128)S(1)} fusion(f32[3,128,768]{2,1,0:T(8,128)S(1)} %broadcast.135.clone.1, s32[16]{0:T(128)S(1)} %get-tuple-element.19, f32[16,128,768]{2,1,0:T(8,128)} %fusion.11), kind=kCustom, calls=%fused_computation.10 | custom fusion | flops 1572864 | bytes 18874432 | tf_op jit(solution)/shard_map/scatter-add | solution.py:45
  101.7 0.9 convert_element_type.73
  102.6 2.4 gather_fusion.5
  105.0 5.7 %fusion.13 = f32[16,128,768]{2,1,0:T(8,128)} fusion(bf16[16,128,768]{2,1,0:T(8,128)(2,1)} %gather_fusion.5, bf16[3,16,128,128]{3,2,1,0:T(8,128)(2,1)} %copy-done.2), kind=kOutput, calls=%fused_computation.28 | convolution fusion | flops 402653184 | bytes 9961472 | tf_op jit(solution)/shard_map/bij,bjd->bid/dot_general | solution.py:39
  110.8 9.2 %scatter_fusion.5 = f32[3,128,768]{2,1,0:T(8,128)S(1)} fusion(f32[3,128,768]{2,1,0:T(8,128)S(1)} %broadcast.135.clone, s32[16]{0:T(128)S(1)} %get-tuple-element.18, f32[16,128,768]{2,1,0:T(8,128)} %fusion.13), kind=kCustom, calls=%fused_computation.11 | custom fusion | flops 1572864 | bytes 18874432 | tf_op jit(solution)/shard_map/scatter-add | solution.py:45
  120.1 1.6 convert_reduce_fusion
  121.7 11.8 %all_gather.7 = bf16[384,256]{1,0:T(8,128)(2,1)S(1)} all-gather(bf16[96,256]{1,0:T(8,128)(2,1)S(1)} %get-tuple-element.10), channel_id=1, replica_groups=mesh['dst'=8,'src'=4] {'src'}, dimensions={0}, use_global_device_ids=true | all-gather | bytes 245760 | tf_op jit(solution)/shard_map/all_gather | solution.py:59
  133.5 2.2 fusion.6
  135.7 40.8 %psum.15 = f32[256]{0:T(256)} all-reduce(f32[256]{0:T(256)S(1)} %get-tuple-element.9), channel_id=1, replica_groups=mesh['dst'=8,'src'=4] {'dst','src'}, use_global_device_ids=true, to_apply=%region_9.10 | all-reduce | flops 256 | bytes 2048 | tf_op jit(solution)/shard_map/psum | solution.py:63
  176.5 95.8 %all-reduce.5.cloned.1.call-done = f32[768,3,256]{0,2,1:T(8,128)} async-done(((f32[768,3,256]{0,2,1:T(8,128)}), f32[768,3,256]{0,2,1:T(8,128)}) %all-reduce.5.cloned.1.call-update) | async-done | bytes 2359312 | tf_op jit(solution)/shard_map/psum | solution.py:63
  272.4 3.0 %copy.16 = f32[768,3,256]{2,0,1:T(8,128)} copy(f32[768,3,256]{0,2,1:T(8,128)} %all-reduce.5.cloned.1.call-done) | data formatting | bytes 4718592
  (41 shorter events, 1.1 us)
Async XLA Ops:
  7.2 3.2 %copy-start.8 = (bf16[256]{0:T(256)(128)(2,1)S(1)}, bf16[256]{0:T(256)(128)(2,1)}, u32[]{:S(2)}) copy-start(bf16[256]{0:T(256)(128)(2,1)} %param.9) | copy-start | bytes 1540
  7.2 3.2 %copy-start.7 = (s32[1,1,3,16]{3,1,2,0:T(1,128)S(1)}, s32[1,1,3,16]{3,1,2,0:T(1,128)}, u32[]{:S(2)}) copy-start(s32[1,1,3,16]{3,1,2,0:T(1,128)} %param.11) | copy-start | bytes 580
  7.2 3.3 %copy-start.9 = (s32[1,1,3]{2,1,0:T(1,128)S(1)}, s32[1,1,3]{2,1,0:T(1,128)}, u32[]{:S(2)}) copy-start(s32[1,1,3]{2,1,0:T(1,128)} %param.12) | copy-start | bytes 40
  7.2 3.4 %copy-start.4 = (bf16[1,1,3,16,128,128]{5,4,3,2,1,0:T(8,128)(2,1)S(1)}, bf16[1,1,3,16,128,128]{5,4,3,2,1,0:T(8,128)(2,1)}, u32[]{:S(2)}) copy-start(bf16[1,1,3,16,128,128]{5,4,3,2,1,0:T(8,128)(2,1)} %param.10) | copy-start | bytes 4718596
  7.2 29.3 %all-gather.2.cloned.1.call-start = ((), (), s32[]{:S(2)}) async-start(), calls=%async_computation.1 | async-start | bytes 1327104 | tf_op jit(solution)/shard_map/all_gather | solution.py:19
  7.9 112.1 %reduce-scatter.2.cloned.1.call-start = ((), (), s32[]{:S(2)}) async-start(), calls=%async_computation.2 | async-start | bytes 491520 | tf_op jit(solution)/shard_map/reduce_scatter | solution.py:49
  10.7 58.7 %copy-start.2 = (bf16[3,16,128,128]{3,2,1,0:T(8,128)(2,1)}, bf16[3,16,128,128]{3,2,1,0:T(8,128)(2,1)S(1)}, u32[]{:S(2)}) copy-start(bf16[3,16,128,128]{3,2,1,0:T(8,128)(2,1)S(1)} %bitcast_multiply_fusion) | copy-start | bytes 4718596
  46.0 3.1 %copy-start.3 = (bf16[16,128,256]{2,1,0:T(8,128)(2,1)S(1)}, bf16[16,128,256]{2,1,0:T(8,128)(2,1)}, u32[]{:S(2)}) copy-start(bf16[16,128,256]{2,1,0:T(8,128)(2,1)} %gather_fusion.1) | copy-start | bytes 3145732
  62.4 4.5 %copy-start.1 = (bf16[768,768]{1,0:T(8,128)(2,1)S(1)}, bf16[768,768]{1,0:T(8,128)(2,1)}, u32[]{:S(2)}) copy-start(bf16[768,768]{1,0:T(8,128)(2,1)} %all-gather.2.cloned.1.call-done) | copy-start | bytes 3538948
  65.9 0.8 copy-start
  66.7 205.7 %all-reduce.5.cloned.1.call-start = ((), (), s32[]{:S(2)}) async-start(), calls=%async_computation.3 | async-start | bytes 4718592 | tf_op jit(solution)/shard_map/psum | solution.py:63
  110.8 9.3 %copy-start.6 = (bf16[96,256]{1,0:T(8,128)(2,1)S(1)}, bf16[96,256]{1,0:T(8,128)(2,1)}, u32[]{:S(2)}) copy-start(bf16[96,256]{1,0:T(8,128)(2,1)} %param.13) | copy-start | bytes 147460
  120.0 13.5 %copy-start.5 = (bf16[3,128,768]{2,1,0:T(8,128)(2,1)S(1)}, bf16[3,128,768]{2,1,0:T(8,128)(2,1)}, u32[]{:S(2)}) copy-start(bf16[3,128,768]{2,1,0:T(8,128)(2,1)} %convert_element_type.73) | copy-start | bytes 1769476
Sparse Core Ops, SparseCore 0:
  9.9 26.5 all-gather.1
  66.8 18.8 reduce-scatter.1
  135.8 136.4 all-reduce.4
where the time goes:
time: 284 us; the launch traced here: 282 us
  waiting for transfers between devices  122 us (43%)
  blocking collectives  52.6 us (19%)
  other arithmetic  40.9 us (14%)
  matrix products  29.6 us (10%)
  local copies, waits for them, and re-layouts  22.2 us (8%)
  between operations  14 us (5%)
    psum x1, waiting for transfers between devices, on_device(): weight_grad, bias_grad = lax.psum((weight_term, bias_term), ('dst', 'src'))  95.8 us
    psum x1, blocking collectives, on_device(): weight_grad, bias_grad = lax.psum((weight_term, bias_term), ('dst', 'src'))  40.8 us
    scatter-add x3, other arithmetic, on_device(): banded = jnp.zeros((blocks_down, block_size, width), jnp.float32).at[row_...  27.5 us
    all_gather x1, waiting for transfers between devices, on_device(): gathered = lax.all_gather(features, 'dst', axis=0, tiled=True)  25.8 us
    dot_general x3, matrix products, on_device(): jnp.einsum('bij,bjd->bid', weighted[relation], picked, preferred_element_...  16.9 us
    all_gather x1, blocking collectives, on_device(): band_grad = lax.all_gather(grad_pre, 'src', axis=0, tiled=True)  11.8 us
    scatter-add x3, other arithmetic, on_device(): partial_total = partial_total.at[row_index[relation]].add(blockwise)  10.4 us
    dot_general x3, matrix products, on_device(): jnp.einsum('bij,bjh->bih', weighted[relation], chosen, preferred_element_...  7.76 us
  transfers between devices with their start and end apart: 3, of which 2 were waited for; matrix products, arithmetic and copies ran while one was open for 20% of the time, Pallas kernels for 0%

commit v1 on v0

v1 whole, which is shorter than its diff:
```python
import functools

import jax
import jax.numpy as jnp
from jax import lax
from jax.experimental import pallas as pl
from jax.experimental.pallas import tpu as pltpu
from jax.sharding import PartitionSpec as P

BF = jnp.bfloat16
F32 = jnp.float32
TAIL = 16
ANY = pl.BlockSpec(memory_space=pl.ANY)
SMEM = pl.BlockSpec(memory_space=pltpu.SMEM)
VMEM = pl.BlockSpec(memory_space=pltpu.VMEM)


def shape(dims, dtype):
    return jax.ShapeDtypeStruct(dims, dtype)


def call(body, out, specs, *args, scratch=(), flops=0, moved=0, aliases=None):
    return pl.pallas_call(
        body,
        out_shape=out,
        in_specs=list(specs),
        out_specs=jax.tree.map(lambda _: VMEM, out),
        scratch_shapes=list(scratch),
        input_output_aliases=aliases or {},
        compiler_params=pltpu.CompilerParams(vmem_limit_bytes=24 * 2**20),
        cost_estimate=pl.CostEstimate(flops=flops, bytes_accessed=moved, transcendentals=0),
    )(*args)


def assemble(band_rows, list_ref, count_ref, values_ref, dense_ref):
    slots = values_ref.shape[0] // count_ref.shape[0]
    size = values_ref.shape[1]
    across = dense_ref.shape[1] // size
    dense_ref[...] = jnp.zeros_like(dense_ref)

    def place(at, carry):
        relation = lax.div(at, slots)

        @pl.when(lax.rem(at, slots) < count_ref[relation])
        def _():
            k = list_ref[at]
            row = pl.multiple_of(relation * band_rows + lax.div(k, across) * size, size)
            column = pl.multiple_of(lax.rem(k, across) * size, size)
            dense_ref[pl.ds(row, size), pl.ds(column, size)] = values_ref[at]

        return carry

    lax.fori_loop(0, values_ref.shape[0], place, 0)


def forward(n_src, count, where_ref, dense_ref, weight_ref, *refs):
    pieces = refs[:count]
    tile_ref, own_ref = refs[count : count + 2]
    sends = refs[count + 2 : count + 1 + n_src]
    features, message, sems = refs[count + 1 + n_src :]
    rows = pieces[0].shape[0]
    copies = []
    for i, piece in enumerate(pieces):
        start = pl.multiple_of(where_ref[1 + i] * rows, 16)
        copies.append(pltpu.make_async_copy(piece, features.at[pl.ds(start, rows)], sems.at[i]))
        copies[-1].start()
    for copy in copies:
        copy.wait()
    width = features.shape[1]
    band_rows = tile_ref.shape[0]
    total = None
    for r in range(dense_ref.shape[0] // band_rows):
        part = jnp.dot(
            dense_ref[r * band_rows : (r + 1) * band_rows],
            features[...],
            preferred_element_type=F32,
        ).astype(BF)
        tile_ref[:, r * width : (r + 1) * width] = part
        term = jnp.dot(
            part, weight_ref[r * width : (r + 1) * width], preferred_element_type=F32
        )
        total = term if total is None else total + term
    message[...] = total
    block = own_ref.shape[0]
    for m in range(n_src):
        start = pl.multiple_of((where_ref[0] ^ m) * block, 16)
        mine = message[pl.ds(start, block)]
        if m == 0:
            own_ref[...] = mine
        else:
            sends[m - 1][...] = mine.astype(BF)


def transpose(tile_ref, out_ref):
    step = 256
    for at in range(0, tile_ref.shape[1], step):
        out_ref[at : at + step] = tile_ref[:, at : at + step].T


def activate(bias_ref, cotangent_ref, own_ref, *refs):
    *others, output_ref, grad_ref = refs
    pre = own_ref[...]
    for other in others:
        pre = pre + other[...].astype(F32)
    pre = pre + bias_ref[...].astype(F32)
    sigma = jax.nn.sigmoid(pre)
    output_ref[...] = (pre * sigma).astype(BF)
    grad_ref[...] = (
        cotangent_ref[...].astype(F32) * sigma * (1.0 + pre * (1.0 - sigma))
    ).astype(BF)


def split_row(row):
    at = lax.broadcasted_iota(jnp.int32, (TAIL, row.shape[1]), 0)
    high = row.astype(BF).astype(F32)
    return jnp.where(at == 0, high, jnp.where(at == 1, row - high, 0.0)).astype(BF)


def join_row(tail):
    return jnp.sum(tail.astype(F32), axis=0, keepdims=True)


def backward(n_src, chips, where_ref, tile_ref, *refs):
    grads = refs[:n_src]
    keep_ref, send_ref, bias_ref, grad = refs[n_src:]
    block = grads[0].shape[0]
    for m in range(n_src):
        start = pl.multiple_of((where_ref[0] ^ m) * block, 16)
        grad[pl.ds(start, block)] = grads[m][...]
    piece = keep_ref.shape[0] // chips
    half = tile_ref.shape[0] // 2
    bias = jnp.sum(grad[...].astype(F32), axis=0, keepdims=True)
    tail = split_row(bias)
    bias_ref[...] = jnp.broadcast_to(join_row(tail), bias_ref.shape)
    send_ref[pl.ds(piece * chips, TAIL)] = tail
    for ref, core in ((send_ref, 1 - where_ref[1]), (keep_ref, where_ref[1])):
        for m in range(chips):
            start = pl.multiple_of(core * half + (where_ref[2] ^ m) * piece, 16)
            ref[m * piece : (m + 1) * piece] = jnp.dot(
                tile_ref[pl.ds(start, piece)], grad[...], preferred_element_type=F32
            ).astype(ref.dtype)


def add_cores(chips, keep_ref, bias_ref, received_ref, own_ref, total_ref, *sends):
    piece = own_ref.shape[0]
    tail = split_row(bias_ref[0:1] + join_row(received_ref[pl.ds(piece * chips, TAIL)]))
    total_ref[...] = jnp.broadcast_to(join_row(tail), total_ref.shape)
    for m in range(chips):
        at = pl.ds(m * piece, piece)
        both = keep_ref[at] + received_ref[at].astype(F32)
        if m == 0:
            own_ref[...] = both
        else:
            sends[m - 1][0:piece] = both.astype(BF)
            sends[m - 1][piece : piece + TAIL] = tail


def tree(terms):
    while len(terms) > 1:
        terms = [a + b for a, b in zip(terms[::2], terms[1::2])]
    return terms[0]


def add_chips(own_ref, bias_ref, *refs):
    *received, sum_ref, total_ref = refs
    piece = own_ref.shape[0]
    tails = [join_row(other[pl.ds(piece, TAIL)]) for other in received]
    total_ref[...] = tree([bias_ref[0:1]] + tails)
    parts = [other[0:piece].astype(F32) for other in received]
    sum_ref[...] = tree([own_ref[...]] + parts).astype(BF)


def add_bands(*refs):
    *parts, out_ref = refs
    out_ref[...] = tree([part[...].astype(F32) for part in parts]).astype(BF)


def spread(chips, where_ref, *refs):
    *pieces, out_ref = refs
    rows = pieces[0].shape[0]
    half = out_ref.shape[0] // 2
    for i, piece in enumerate(pieces):
        core = where_ref[1] if i < chips else 1 - where_ref[1]
        start = core * half + (where_ref[2] ^ (i % chips)) * rows
        out_ref[pl.ds(pl.multiple_of(start, 16), rows)] = piece[...].astype(F32)


def swap(x, axis, n, mask):
    return lax.ppermute(x, axis, [(i, i ^ mask) for i in range(n)])


def on_device(features, relation_weight, bias, block_values, block_list, block_count, cotangent):
    n_dst, n_src = lax.axis_size("dst"), lax.axis_size("src")
    own_rows, width = features.shape
    relations, hidden = relation_weight.shape[1:]
    block_size = block_values.shape[5]
    tile_columns = own_rows * n_dst
    block = cotangent.shape[0]
    band_rows = block * n_src
    weight = relation_weight.transpose(1, 0, 2).reshape(relations * width, hidden)
    dense = call(
        functools.partial(assemble, band_rows),
        shape((relations * band_rows, tile_columns), BF),
        (SMEM, SMEM, VMEM),
        block_list.reshape(-1),
        block_count.reshape(-1),
        block_values.reshape(-1, block_size, block_size),
        flops=10**8,
        moved=4 * 2**20,
    )
    if n_dst == 8 and n_src == 4 and (relations * width) % (8 * 16) == 0:
        return few_devices(features, weight, bias, dense, cotangent, relations)
    gathered = lax.all_gather(features, "dst", axis=0, tiled=True)
    tile = jnp.dot(dense, gathered, preferred_element_type=F32).astype(BF)
    tile = tile.reshape(relations, band_rows, width)
    partial = jnp.einsum(
        "rnd,rdh->nh",
        tile,
        weight.reshape(relations, width, hidden),
        preferred_element_type=F32,
    )
    pre = lax.psum_scatter(partial, "src", scatter_dimension=0, tiled=True)
    pre = pre + bias.astype(F32)
    sigma = jax.nn.sigmoid(pre)
    output = (pre * sigma).astype(BF)
    grad = (cotangent.astype(F32) * sigma * (1.0 + pre * (1.0 - sigma))).astype(BF)
    band_grad = lax.all_gather(grad, "src", axis=0, tiled=True)
    weight_term = jnp.einsum("rnd,nh->rdh", tile, band_grad, preferred_element_type=F32)
    weight_grad, bias_grad = lax.psum(
        (weight_term, jnp.sum(grad.astype(F32), axis=0)), ("dst", "src")
    )
    return output, weight_grad.transpose(1, 0, 2), bias_grad


def few_devices(features, weight, bias, dense, cotangent, relations):
    n_dst, n_src = lax.axis_size("dst"), lax.axis_size("src")
    chips = n_dst // 2
    own_rows, width = features.shape
    block, hidden = cotangent.shape
    band_rows = block * n_src
    total_rows = weight.shape[0]
    piece = total_rows // n_dst
    me, z = lax.axis_index("dst"), lax.axis_index("src")
    place = jnp.stack([z, me % 2, me // 2]).astype(jnp.int32)

    def over_chips(x, m):
        return swap(x, "dst", n_dst, 2 * m)

    def over_core(x):
        return swap(x, "dst", n_dst, 1)

    def over_src(x, m):
        return swap(x, "src", n_src, m)

    near = [features] + [over_chips(features, m) for m in range(1, chips)]
    far = [over_core(x) for x in near]
    order = [me ^ (2 * m) for m in range(chips)] + [me ^ (2 * m + 1) for m in range(chips)]
    where = jnp.stack([z] + order).astype(jnp.int32)
    tile, own, *sends = call(
        functools.partial(forward, n_src, n_dst),
        [shape((band_rows, relations * width), BF), shape((block, hidden), F32)]
        + [shape((block, hidden), BF)] * (n_src - 1),
        [SMEM, VMEM, VMEM] + [ANY] * n_dst,
        where,
        dense,
        weight,
        *near,
        *far,
        scratch=[
            pltpu.VMEM((own_rows * n_dst, width), BF),
            pltpu.VMEM((band_rows, hidden), F32),
            pltpu.SemaphoreType.DMA((n_dst,)),
        ],
        flops=2 * 10**9,
        moved=8 * 2**20,
    )
    received = [over_src(x, m + 1) for m, x in enumerate(sends)]
    turned = call(
        transpose,
        shape((total_rows, band_rows), BF),
        [VMEM],
        tile,
        flops=10**8,
        moved=4 * 2**20,
    )
    output, grad = call(
        activate,
        [shape((block, hidden), BF)] * 2,
        [VMEM] * (3 + len(received)),
        bias.reshape(1, hidden),
        cotangent,
        own,
        *received,
    )
    grads = [grad] + [over_src(grad, m) for m in range(1, n_src)]
    keep, send, bias_part = call(
        functools.partial(backward, n_src, chips),
        [
            shape((piece * chips, hidden), F32),
            shape((piece * chips + TAIL, hidden), BF),
            shape((8, hidden), F32),
        ],
        [SMEM, VMEM] + [VMEM] * n_src,
        place,
        turned,
        *grads,
        scratch=[pltpu.VMEM((band_rows, hidden), BF)],
    )
    own, bias_part, *sends = call(
        functools.partial(add_cores, chips),
        [shape((piece, hidden), F32), shape((8, hidden), F32)]
        + [shape((piece + TAIL, hidden), BF)] * (chips - 1),
        [VMEM] * 3,
        keep,
        bias_part,
        over_core(send),
    )
    received = [over_chips(x, m + 1) for m, x in enumerate(sends)]
    part, bias_grad = call(
        add_chips,
        [shape((piece, hidden), BF), shape((1, hidden), F32)],
        [VMEM] * (1 + chips),
        own,
        bias_part,
        *received,
    )
    parts = [part] + [over_src(part, m) for m in range(1, n_src)]
    chunk = call(add_bands, shape((piece, hidden), BF), [VMEM] * n_src, *parts)
    near = [chunk] + [over_chips(chunk, m) for m in range(1, chips)]
    far = [over_core(x) for x in near]
    weight_grad = call(
        functools.partial(spread, chips),
        shape((total_rows, hidden), F32),
        [SMEM] + [VMEM] * n_dst,
        place,
        *near,
        *far,
    )
    weight_grad = weight_grad.reshape(relations, width, hidden).transpose(1, 0, 2)
    return output, weight_grad, bias_grad.reshape(hidden)


def solution(mesh):
    in_specs = (
        P(("src", "dst"), None),
        P(),
        P(),
        P("dst", "src", None, None, None, None),
        P("dst", "src", None, None),
        P("dst", "src", None),
        P(("dst", "src"), None),
    )
    out_specs = (P(("dst", "src"), None), P(), P())
    return jax.shard_map(
        on_device, mesh=mesh, in_specs=in_specs, out_specs=out_specs, check_vma=False
    )
```

time: 284 us -> 81.2 us (0.29)
  waiting for transfers between devices: 122 us -> 26.1 us
  blocking collectives: 52.6 us -> 0 us
  other arithmetic: 40.9 us -> 0.77 us
  starting transfers between devices: 0.3 us -> 38.6 us
  matrix products: 29.6 us -> 0 us
  local copies, waits for them, and re-layouts: 22.2 us -> 2.26 us
  between operations: 14 us -> 0.8 us
  Pallas kernels: 0 us -> 11.9 us
    psum x1 -> x0, waiting for transfers between devices: 95.8 us -> none  [on_device(): weight_grad, bias_grad = lax.psum((weight_term, bias_term), ('dst', 'src'))]
    psum x1 -> x0, blocking collectives: 40.8 us -> none  [on_device(): weight_grad, bias_grad = lax.psum((weight_term, bias_term), ('dst', 'src'))]
    ppermute x0 -> x27, starting transfers between devices: none -> 38.6 us  [swap(): return lax.ppermute(x, axis, [(i, i ^ mask) for i in range(n)])]
    scatter-add x6 -> x0, other arithmetic: 38 us -> none  [the longest x3 27.5 us: on_device(): banded = jnp.zeros((blocks_down, block_size, width), jnp.float32).at[row_...]
    dot_general x8 -> x0, matrix products: 29.6 us -> none  [the longest x3 16.9 us: on_device(): jnp.einsum('bij,bjd->bid', weighted[relation], picked, preferred_element_...]
    ppermute x0 -> x27, waiting for transfers between devices: none -> 26.1 us  [swap(): return lax.ppermute(x, axis, [(i, i ^ mask) for i in range(n)])]
    all_gather x1 -> x0, waiting for transfers between devices: 25.8 us -> none  [on_device(): gathered = lax.all_gather(features, 'dst', axis=0, tiled=True)]
    gather x6 -> x0, local copies, waits for them, and re-layouts: 12.2 us -> none  [the longest x3 7.34 us: on_device(): picked = source_blocks[column_index[relation]]]
  transfers between devices with their start and end apart: 3 -> 27, of which waited for: 2 -> 12; matrix products, arithmetic and copies ran while one was open for 20% -> 1% of each run, Pallas kernels for 0% -> 3%
where the time goes in v1:
time: 81.2 us; the launch traced here: 80.4 us
  starting transfers between devices  38.6 us (48%)
  waiting for transfers between devices  26.1 us (32%)
  Pallas kernels  11.9 us (15%)
  local copies, waits for them, and re-layouts  2.26 us (3%)
    ppermute x27, starting transfers between devices, swap(): return lax.ppermute(x, axis, [(i, i ^ mask) for i in range(n)])  38.6 us
    ppermute x27, waiting for transfers between devices, swap(): return lax.ppermute(x, axis, [(i, i ^ mask) for i in range(n)])  26.1 us
    pallas_call x9, Pallas kernels, call(): pl.pallas_call(body, out_shape=out, in_specs=list(specs), out_specs=jax.t...  11.9 us
    unnamed x12, local copies, waits for them, and re-layouts  2.09 us
  transfers between devices with their start and end apart: 27, of which 12 were waited for; matrix products, arithmetic and copies ran while one was open for 1% of the time, Pallas kernels for 3%

profile of v1, /device:TPU:1, one launch (start us, length us, event | category | flops | bytes accessed | tf_op | source)
XLA Modules:
  0.0 80.4 jit_solution(7009721422653414569)
XLA Ops:
  0.6 2.1 %collective-permute-start = (bf16[96,768]{1,0:T(8,128)(2,1)}, bf16[96,768]{1,0:T(8,128)(2,1)S(1)}, u32[]{:S(2)}, u32[]{:S(2)}) collective-permute-start(bf16[96,768]{1,0:T(8,128)(2,1)} %refs_0_.1), channel_id=1, source_target_pairs={{0,8},{4,12},{8,0},{12,4},{16,24},{20,28},{24,16},{28,20},{1,9},{5... | collective-permute-start | bytes 442376 | tf_op jit(solution)/shard_map/ppermute | solution.py:189
  2.7 1.2 %collective-permute-start.1 = (bf16[96,768]{1,0:T(8,128)(2,1)}, bf16[96,768]{1,0:T(8,128)(2,1)S(1)}, u32[]{:S(2)}, u32[]{:S(2)}) collective-permute-start(bf16[96,768]{1,0:T(8,128)(2,1)} %refs_0_.1), channel_id=1, source_target_pairs={{0,16},{4,20},{8,24},{12,28},{16,0},{20,4},{24,8},{28,12},{1,17},{... | collective-permute-start | bytes 442376 | tf_op jit(solution)/shard_map/ppermute | solution.py:189
  4.0 1.2 %collective-permute-start.3 = (bf16[96,768]{1,0:T(8,128)(2,1)}, bf16[96,768]{1,0:T(8,128)(2,1)S(1)}, u32[]{:S(2)}, u32[]{:S(2)}) collective-permute-start(bf16[96,768]{1,0:T(8,128)(2,1)} %refs_0_.1), channel_id=1, source_target_pairs={{0,4},{4,0},{8,12},{12,8},{16,20},{20,16},{24,28},{28,24},{1,5},{5... | collective-permute-start | bytes 442376 | tf_op jit(solution)/shard_map/ppermute | solution.py:189
  5.2 1.3 %collective-permute-done.refs_1_ = bf16[96,768]{1,0:T(8,128)(2,1)S(1)} collective-permute-done((bf16[96,768]{1,0:T(8,128)(2,1)}, bf16[96,768]{1,0:T(8,128)(2,1)S(1)}, u32[]{:S(2)}, u32[]{:S(2)}) %collective-permute-start) | collective-permute-done | bytes 147488 | tf_op jit(solution)/shard_map/ppermute | solution.py:189
  6.5 1.7 %collective-permute-start.4 = (bf16[96,768]{1,0:T(8,128)(2,1)S(1)}, bf16[96,768]{1,0:T(8,128)(2,1)S(1)}, u32[]{:S(2)}, u32[]{:S(2)}) collective-permute-start(bf16[96,768]{1,0:T(8,128)(2,1)S(1)} %collective-permute-done.refs_1_), channel_id=1, source_target_pairs={{0,4},{4,0},{8,12},{12,8},{16,20},{20,16},{24,28},{28,24},{1,5},{5... | collective-permute-start | bytes 442376 | tf_op jit(solution)/shard_map/ppermute | solution.py:189
  8.3 4.1 %collective-permute-start.5 = (bf16[96,768]{1,0:T(8,128)(2,1)S(1)}, bf16[96,768]{1,0:T(8,128)(2,1)S(1)}, u32[]{:S(2)}, u32[]{:S(2)}) collective-permute-start(bf16[96,768]{1,0:T(8,128)(2,1)S(1)} %collective-permute-done.1.refs_2_), channel_id=1, source_target_pairs={{0,4},{4,0},{8,12},{12,8},{16,20},{20,16},{24,28},{28,24},{1,5},{5... | collective-permute-start | bytes 442376 | tf_op jit(solution)/shard_map/ppermute | solution.py:189
  13.2 1.4 %copy-done = bf16[1,1,3,16,128,128]{5,4,3,2,1,0:T(8,128)(2,1)S(1)} copy-done((bf16[1,1,3,16,128,128]{5,4,3,2,1,0:T(8,128)(2,1)S(1)}, bf16[1,1,3,16,128,128]{5,4,3,2,1,0:T(8,128)(2,1)}, u32[]{:S(2)}) %copy-start) | copy-done | bytes 1572888
  15.3 1.8 %shard_map.94.dense_ref = bf16[1152,768]{1,0:T(8,128)(2,1)S(1)} custom-call(s32[48]{0:T(128)S(1)} %reshape.28.list_ref, s32[3]{0:T(128)S(1)} %bitcast.21, bf16[48,128,128]{2,1,0:T(8,128)(2,1)S(1)} %bitcast.20), custom_call_target="tpu_custom_call" | custom-call | flops 100000000 | bytes 4194304 | tf_op jit(solution)/shard_map/pallas_call | solution.py:23
  17.2 4.7 %shard_map.95 = (bf16[384,2304]{1,0:T(8,128)(2,1)S(1)}, f32[96,256]{1,0:T(8,128)S(1)}, bf16[96,256]{1,0:T(8,128)(2,1)S(1)}, bf16[96,256]{1,0:T(8,128)(2,1)S(1)}, bf16[96,256]{1,0:T(8,128)(2,1)S(1)}) custom-call(s32[9]{0:T(128)S(1)} %stack.49.where_ref, bf16[1152,768]{1,0:T(8,128)(2,1)S(1)} %shard_map.94.dense_ref, bf16[2304,256]{1,0:T(8,128)(2,1)S(1)} %bitcast.22, ...), custom_call_target="tpu_custom_call" | custom-call | flops 2000000000 | bytes 8388608 | tf_op jit(solution)/shard_map/pallas_call | solution.py:23
  21.9 1.4 %collective-permute-start.7 = (bf16[96,256]{1,0:T(8,128)(2,1)S(1)}, bf16[96,256]{1,0:T(8,128)(2,1)S(1)}, u32[]{:S(2)}, u32[]{:S(2)}) collective-permute-start(bf16[96,256]{1,0:T(8,128)(2,1)S(1)} %get-tuple-element.21), channel_id=1, source_target_pairs={{0,1},{1,0},{2,3},{3,2},{4,5},{5,4},{6,7},{7,6},{8,9},{9,8},{10,11... | collective-permute-start | bytes 147464 | tf_op jit(solution)/shard_map/ppermute | solution.py:189
  23.3 2.2 %collective-permute-start.8 = (bf16[96,256]{1,0:T(8,128)(2,1)S(1)}, bf16[96,256]{1,0:T(8,128)(2,1)S(1)}, u32[]{:S(2)}, u32[]{:S(2)}) collective-permute-start(bf16[96,256]{1,0:T(8,128)(2,1)S(1)} %get-tuple-element.22), channel_id=1, source_target_pairs={{0,2},{1,3},{2,0},{3,1},{4,6},{5,7},{6,4},{7,5},{8,10},{9,11},{10,... | collective-permute-start | bytes 147464 | tf_op jit(solution)/shard_map/ppermute | solution.py:189
  25.5 2.2 %collective-permute-done.8.refs_1_ = bf16[96,256]{1,0:T(8,128)(2,1)S(1)} collective-permute-done((bf16[96,256]{1,0:T(8,128)(2,1)S(1)}, bf16[96,256]{1,0:T(8,128)(2,1)S(1)}, u32[]{:S(2)}, u32[]{:S(2)}) %collective-permute-start.8) | collective-permute-done | bytes 49184 | tf_op jit(solution)/shard_map/ppermute | solution.py:189
  27.7 2.6 %collective-permute-done.9.refs_2_ = bf16[96,256]{1,0:T(8,128)(2,1)S(1)} collective-permute-done((bf16[96,256]{1,0:T(8,128)(2,1)S(1)}, bf16[96,256]{1,0:T(8,128)(2,1)S(1)}, u32[]{:S(2)}, u32[]{:S(2)}) %collective-permute-start.9) | collective-permute-done | bytes 49184 | tf_op jit(solution)/shard_map/ppermute | solution.py:189
  31.0 0.8 collective-permute-start.11
  31.8 2.7 %collective-permute-start.12 = (bf16[96,256]{1,0:T(8,128)(2,1)S(1)}, bf16[96,256]{1,0:T(8,128)(2,1)S(1)}, u32[]{:S(2)}, u32[]{:S(2)}) collective-permute-start(bf16[96,256]{1,0:T(8,128)(2,1)S(1)} %get-tuple-element.26.refs_0_), channel_id=1, source_target_pairs={{0,3},{1,2},{2,1},{3,0},{4,7},{5,6},{6,5},{7,4},{8,11},{9,10},{10,... | collective-permute-start | bytes 147464 | tf_op jit(solution)/shard_map/ppermute | solution.py:189
  35.1 2.0 %collective-permute-done.12.refs_3_ = bf16[96,256]{1,0:T(8,128)(2,1)S(1)} collective-permute-done((bf16[96,256]{1,0:T(8,128)(2,1)S(1)}, bf16[96,256]{1,0:T(8,128)(2,1)S(1)}, u32[]{:S(2)}, u32[]{:S(2)}) %collective-permute-start.12) | collective-permute-done | bytes 49184 | tf_op jit(solution)/shard_map/ppermute | solution.py:189
  37.1 1.3 %shard_map.98 = (f32[1152,256]{1,0:T(8,128)S(1)}, bf16[1168,256]{1,0:T(8,128)(2,1)S(1)}, f32[8,256]{1,0:T(8,128)S(1)}) custom-call(s32[3]{0:T(128)S(1)} %pad_add_fusion.where_ref, bf16[2304,384]{1,0:T(8,128)(2,1)S(1)} %shard_map.97.tile_ref, bf16[96,256]{1,0:T(8,128)(2,1)S(1)} %get-tuple-element.26.refs_0_, ...), custom_call_target="tpu_custom_call" | custom-call | tf_op jit(solution)/shard_map/pallas_call | solution.py:23
  38.5 3.5 %collective-permute-start.13 = (bf16[1168,256]{1,0:T(8,128)(2,1)S(1)}, bf16[1168,256]{1,0:T(8,128)(2,1)S(1)}, u32[]{:S(2)}, u32[]{:S(2)}) collective-permute-start(bf16[1168,256]{1,0:T(8,128)(2,1)S(1)} %get-tuple-element.29), channel_id=1, source_target_pairs={{0,4},{4,0},{8,12},{12,8},{16,20},{20,16},{24,28},{28,24},{1,5},{5... | collective-permute-start | bytes 1794056 | tf_op jit(solution)/shard_map/ppermute | solution.py:189
  42.0 1.6 %collective-permute-done.13.received_ref = bf16[1168,256]{1,0:T(8,128)(2,1)S(1)} collective-permute-done((bf16[1168,256]{1,0:T(8,128)(2,1)S(1)}, bf16[1168,256]{1,0:T(8,128)(2,1)S(1)}, u32[]{:S(2)}, u32[]{:S(2)}) %collective-permute-start.13) | collective-permute-done | bytes 598048 | tf_op jit(solution)/shard_map/ppermute | solution.py:189
  43.8 1.0 %collective-permute-start.14 = (bf16[304,256]{1,0:T(8,128)(2,1)S(1)}, bf16[304,256]{1,0:T(8,128)(2,1)S(1)}, u32[]{:S(2)}, u32[]{:S(2)}) collective-permute-start(bf16[304,256]{1,0:T(8,128)(2,1)S(1)} %get-tuple-element.32), channel_id=1, source_target_pairs={{0,8},{4,12},{8,0},{12,4},{16,24},{20,28},{24,16},{28,20},{1,9},{5... | collective-permute-start | bytes 466952 | tf_op jit(solution)/shard_map/ppermute | solution.py:189
  45.4 1.1 %collective-permute-start.16 = (bf16[304,256]{1,0:T(8,128)(2,1)S(1)}, bf16[304,256]{1,0:T(8,128)(2,1)S(1)}, u32[]{:S(2)}, u32[]{:S(2)}) collective-permute-start(bf16[304,256]{1,0:T(8,128)(2,1)S(1)} %get-tuple-element.34), channel_id=1, source_target_pairs={{0,24},{4,28},{8,16},{12,20},{16,8},{20,12},{24,0},{28,4},{1,25},{... | collective-permute-start | bytes 466952 | tf_op jit(solution)/shard_map/ppermute | solution.py:189
  46.5 2.6 %collective-permute-done.14.refs_0_ = bf16[304,256]{1,0:T(8,128)(2,1)S(1)} collective-permute-done((bf16[304,256]{1,0:T(8,128)(2,1)S(1)}, bf16[304,256]{1,0:T(8,128)(2,1)S(1)}, u32[]{:S(2)}, u32[]{:S(2)}) %collective-permute-start.14) | collective-permute-done | bytes 155680 | tf_op jit(solution)/shard_map/ppermute | solution.py:189
  49.7 3.6 %collective-permute-done.16.refs_2_ = bf16[304,256]{1,0:T(8,128)(2,1)S(1)} collective-permute-done((bf16[304,256]{1,0:T(8,128)(2,1)S(1)}, bf16[304,256]{1,0:T(8,128)(2,1)S(1)}, u32[]{:S(2)}, u32[]{:S(2)}) %collective-permute-start.16) | collective-permute-done | bytes 155680 | tf_op jit(solution)/shard_map/ppermute | solution.py:189
  53.9 3.1 %collective-permute-start.18 = (bf16[288,256]{1,0:T(8,128)(2,1)S(1)}, bf16[288,256]{1,0:T(8,128)(2,1)S(1)}, u32[]{:S(2)}, u32[]{:S(2)}) collective-permute-start(bf16[288,256]{1,0:T(8,128)(2,1)S(1)} %get-tuple-element.35.refs_0_), channel_id=1, source_target_pairs={{0,2},{1,3},{2,0},{3,1},{4,6},{5,7},{6,4},{7,5},{8,10},{9,11},{10,... | collective-permute-start | bytes 442376 | tf_op jit(solution)/shard_map/ppermute | solution.py:189
  57.9 1.7 %collective-permute-done.18.refs_2_ = bf16[288,256]{1,0:T(8,128)(2,1)S(1)} collective-permute-done((bf16[288,256]{1,0:T(8,128)(2,1)S(1)}, bf16[288,256]{1,0:T(8,128)(2,1)S(1)}, u32[]{:S(2)}, u32[]{:S(2)}) %collective-permute-start.18) | collective-permute-done | bytes 147488 | tf_op jit(solution)/shard_map/ppermute | solution.py:189
  59.6 6.4 %collective-permute-done.19.refs_3_ = bf16[288,256]{1,0:T(8,128)(2,1)S(1)} collective-permute-done((bf16[288,256]{1,0:T(8,128)(2,1)S(1)}, bf16[288,256]{1,0:T(8,128)(2,1)S(1)}, u32[]{:S(2)}, u32[]{:S(2)}) %collective-permute-start.19) | collective-permute-done | bytes 147488 | tf_op jit(solution)/shard_map/ppermute | solution.py:189
  66.3 2.6 %collective-permute-start.22 = (bf16[288,256]{1,0:T(8,128)(2,1)S(1)}, bf16[288,256]{1,0:T(8,128)(2,1)S(1)}, u32[]{:S(2)}, u32[]{:S(2)}) collective-permute-start(bf16[288,256]{1,0:T(8,128)(2,1)S(1)} %shard_map.101.refs_0_), channel_id=1, source_target_pairs={{0,24},{4,28},{8,16},{12,20},{16,8},{20,12},{24,0},{28,4},{1,25},{... | collective-permute-start | bytes 442376 | tf_op jit(solution)/shard_map/ppermute | solution.py:189
  68.8 4.5 %collective-permute-start.23 = (bf16[288,256]{1,0:T(8,128)(2,1)S(1)}, bf16[288,256]{1,0:T(8,128)(2,1)S(1)}, u32[]{:S(2)}, u32[]{:S(2)}) collective-permute-start(bf16[288,256]{1,0:T(8,128)(2,1)S(1)} %shard_map.101.refs_0_), channel_id=1, source_target_pairs={{0,4},{4,0},{8,12},{12,8},{16,20},{20,16},{24,28},{28,24},{1,5},{5... | collective-permute-start | bytes 442376 | tf_op jit(solution)/shard_map/ppermute | solution.py:189
  73.3 1.7 %collective-permute-start.24 = (bf16[288,256]{1,0:T(8,128)(2,1)S(1)}, bf16[288,256]{1,0:T(8,128)(2,1)S(1)}, u32[]{:S(2)}, u32[]{:S(2)}) collective-permute-start(bf16[288,256]{1,0:T(8,128)(2,1)S(1)} %collective-permute-done.20.refs_1_), channel_id=1, source_target_pairs={{0,4},{4,0},{8,12},{12,8},{16,20},{20,16},{24,28},{28,24},{1,5},{5... | collective-permute-start | bytes 442376 | tf_op jit(solution)/shard_map/ppermute | solution.py:189
  75.6 1.7 %collective-permute-start.26 = (bf16[288,256]{1,0:T(8,128)(2,1)S(1)}, bf16[288,256]{1,0:T(8,128)(2,1)S(1)}, u32[]{:S(2)}, u32[]{:S(2)}) collective-permute-start(bf16[288,256]{1,0:T(8,128)(2,1)S(1)} %collective-permute-done.22.refs_3_), channel_id=1, source_target_pairs={{0,4},{4,0},{8,12},{12,8},{16,20},{20,16},{24,28},{28,24},{1,5},{5... | collective-permute-start | bytes 442376 | tf_op jit(solution)/shard_map/ppermute | solution.py:189
  77.3 1.0 %collective-permute-done.26.refs_7_ = bf16[288,256]{1,0:T(8,128)(2,1)S(1)} collective-permute-done((bf16[288,256]{1,0:T(8,128)(2,1)S(1)}, bf16[288,256]{1,0:T(8,128)(2,1)S(1)}, u32[]{:S(2)}, u32[]{:S(2)}) %collective-permute-start.26) | collective-permute-done | bytes 147488 | tf_op jit(solution)/shard_map/ppermute | solution.py:189
  78.3 2.1 %shard_map.102 = f32[2304,256]{1,0:T(8,128)} custom-call(s32[3]{0:T(128)S(1)} %pad_add_fusion.where_ref, bf16[288,256]{1,0:T(8,128)(2,1)S(1)} %shard_map.101.refs_0_, bf16[288,256]{1,0:T(8,128)(2,1)S(1)} %collective-permute-done.20.refs_1_, bf16[288,256]{1,0:T(8,128)(2,1)S(1)} %collective-permute-done.21.refs_2_, ...), custom_call_target="tpu_custom_call" | custom-call | tf_op jit(solution)/shard_map/pallas_call | solution.py:23
  (48 shorter events, 6.7 us)
Async XLA Ops:
  0.6 5.9 %collective-permute-start = (bf16[96,768]{1,0:T(8,128)(2,1)}, bf16[96,768]{1,0:T(8,128)(2,1)S(1)}, u32[]{:S(2)}, u32[]{:S(2)}) collective-permute-start(bf16[96,768]{1,0:T(8,128)(2,1)} %refs_0_.1), channel_id=1, source_target_pairs={{0,8},{4,12},{8,0},{12,4},{16,24},{20,28},{24,16},{28,20},{1,9},{5... | collective-permute-start | bytes 442376 | tf_op jit(solution)/shard_map/ppermute | solution.py:189
  2.7 5.5 %collective-permute-start.1 = (bf16[96,768]{1,0:T(8,128)(2,1)}, bf16[96,768]{1,0:T(8,128)(2,1)S(1)}, u32[]{:S(2)}, u32[]{:S(2)}) collective-permute-start(bf16[96,768]{1,0:T(8,128)(2,1)} %refs_0_.1), channel_id=1, source_target_pairs={{0,16},{4,20},{8,24},{12,28},{16,0},{20,4},{24,8},{28,12},{1,17},{... | collective-permute-start | bytes 442376 | tf_op jit(solution)/shard_map/ppermute | solution.py:189
  4.0 8.4 %collective-permute-start.2 = (bf16[96,768]{1,0:T(8,128)(2,1)}, bf16[96,768]{1,0:T(8,128)(2,1)S(1)}, u32[]{:S(2)}, u32[]{:S(2)}) collective-permute-start(bf16[96,768]{1,0:T(8,128)(2,1)} %refs_0_.1), channel_id=1, source_target_pairs={{0,24},{4,28},{8,16},{12,20},{16,8},{20,12},{24,0},{28,4},{1,25},{... | collective-permute-start | bytes 442376 | tf_op jit(solution)/shard_map/ppermute | solution.py:189
  4.0 13.1 %collective-permute-start.3 = (bf16[96,768]{1,0:T(8,128)(2,1)}, bf16[96,768]{1,0:T(8,128)(2,1)S(1)}, u32[]{:S(2)}, u32[]{:S(2)}) collective-permute-start(bf16[96,768]{1,0:T(8,128)(2,1)} %refs_0_.1), channel_id=1, source_target_pairs={{0,4},{4,0},{8,12},{12,8},{16,20},{20,16},{24,28},{28,24},{1,5},{5... | collective-permute-start | bytes 442376 | tf_op jit(solution)/shard_map/ppermute | solution.py:189
  6.5 10.6 %collective-permute-start.4 = (bf16[96,768]{1,0:T(8,128)(2,1)S(1)}, bf16[96,768]{1,0:T(8,128)(2,1)S(1)}, u32[]{:S(2)}, u32[]{:S(2)}) collective-permute-start(bf16[96,768]{1,0:T(8,128)(2,1)S(1)} %collective-permute-done.refs_1_), channel_id=1, source_target_pairs={{0,4},{4,0},{8,12},{12,8},{16,20},{20,16},{24,28},{28,24},{1,5},{5... | collective-permute-start | bytes 442376 | tf_op jit(solution)/shard_map/ppermute | solution.py:189
  8.3 8.9 %collective-permute-start.5 = (bf16[96,768]{1,0:T(8,128)(2,1)S(1)}, bf16[96,768]{1,0:T(8,128)(2,1)S(1)}, u32[]{:S(2)}, u32[]{:S(2)}) collective-permute-start(bf16[96,768]{1,0:T(8,128)(2,1)S(1)} %collective-permute-done.1.refs_2_), channel_id=1, source_target_pairs={{0,4},{4,0},{8,12},{12,8},{16,20},{20,16},{24,28},{28,24},{1,5},{5... | collective-permute-start | bytes 442376 | tf_op jit(solution)/shard_map/ppermute | solution.py:189
  12.4 4.8 %collective-permute-start.6 = (bf16[96,768]{1,0:T(8,128)(2,1)S(1)}, bf16[96,768]{1,0:T(8,128)(2,1)S(1)}, u32[]{:S(2)}, u32[]{:S(2)}) collective-permute-start(bf16[96,768]{1,0:T(8,128)(2,1)S(1)} %collective-permute-done.2.refs_3_), channel_id=1, source_target_pairs={{0,4},{4,0},{8,12},{12,8},{16,20},{20,16},{24,28},{28,24},{1,5},{5... | collective-permute-start | bytes 442376 | tf_op jit(solution)/shard_map/ppermute | solution.py:189
  13.2 1.4 %copy-start = (bf16[1,1,3,16,128,128]{5,4,3,2,1,0:T(8,128)(2,1)S(1)}, bf16[1,1,3,16,128,128]{5,4,3,2,1,0:T(8,128)(2,1)}, u32[]{:S(2)}) copy-start(bf16[1,1,3,16,128,128]{5,4,3,2,1,0:T(8,128)(2,1)} %param.10) | copy-start | bytes 4718596
  15.3 1.9 %copy-start.3 = (bf16[768,3,256]{2,0,1:T(8,128)(2,1)S(1)}, bf16[768,3,256]{2,0,1:T(8,128)(2,1)}, u32[]{:S(2)}) copy-start(bf16[768,3,256]{2,0,1:T(8,128)(2,1)} %param.8) | copy-start | bytes 3538948
  15.3 1.9 %copy-start.4 = (bf16[96,768]{1,0:T(8,128)(2,1)S(1)}, bf16[96,768]{1,0:T(8,128)(2,1)}, u32[]{:S(2)}) copy-start(bf16[96,768]{1,0:T(8,128)(2,1)} %refs_0_.1) | copy-start | bytes 442372
  17.2 8.3 %copy-start.5 = (bf16[256]{0:T(256)(128)(2,1)S(1)}, bf16[256]{0:T(256)(128)(2,1)}, u32[]{:S(2)}) copy-start(bf16[256]{0:T(256)(128)(2,1)} %param.9) | copy-start | bytes 1540
  17.2 13.1 %copy-start.1 = (bf16[96,256]{1,0:T(8,128)(2,1)S(1)}, bf16[96,256]{1,0:T(8,128)(2,1)}, u32[]{:S(2)}) copy-start(bf16[96,256]{1,0:T(8,128)(2,1)} %cotangent_ref.1) | copy-start | bytes 147460
  21.9 3.6 %collective-permute-start.7 = (bf16[96,256]{1,0:T(8,128)(2,1)S(1)}, bf16[96,256]{1,0:T(8,128)(2,1)S(1)}, u32[]{:S(2)}, u32[]{:S(2)}) collective-permute-start(bf16[96,256]{1,0:T(8,128)(2,1)S(1)} %get-tuple-element.21), channel_id=1, source_target_pairs={{0,1},{1,0},{2,3},{3,2},{4,5},{5,4},{6,7},{7,6},{8,9},{9,8},{10,11... | collective-permute-start | bytes 147464 | tf_op jit(solution)/shard_map/ppermute | solution.py:189
  23.3 4.4 %collective-permute-start.8 = (bf16[96,256]{1,0:T(8,128)(2,1)S(1)}, bf16[96,256]{1,0:T(8,128)(2,1)S(1)}, u32[]{:S(2)}, u32[]{:S(2)}) collective-permute-start(bf16[96,256]{1,0:T(8,128)(2,1)S(1)} %get-tuple-element.22), channel_id=1, source_target_pairs={{0,2},{1,3},{2,0},{3,1},{4,6},{5,7},{6,4},{7,5},{8,10},{9,11},{10,... | collective-permute-start | bytes 147464 | tf_op jit(solution)/shard_map/ppermute | solution.py:189
  25.5 4.8 %collective-permute-start.9 = (bf16[96,256]{1,0:T(8,128)(2,1)S(1)}, bf16[96,256]{1,0:T(8,128)(2,1)S(1)}, u32[]{:S(2)}, u32[]{:S(2)}) collective-permute-start(bf16[96,256]{1,0:T(8,128)(2,1)S(1)} %get-tuple-element.23), channel_id=1, source_target_pairs={{0,3},{1,2},{2,1},{3,0},{4,7},{5,6},{6,5},{7,4},{8,11},{9,10},{10,... | collective-permute-start | bytes 147464 | tf_op jit(solution)/shard_map/ppermute | solution.py:189
  31.0 4.1 %collective-permute-start.10 = (bf16[96,256]{1,0:T(8,128)(2,1)S(1)}, bf16[96,256]{1,0:T(8,128)(2,1)S(1)}, u32[]{:S(2)}, u32[]{:S(2)}) collective-permute-start(bf16[96,256]{1,0:T(8,128)(2,1)S(1)} %get-tuple-element.26.refs_0_), channel_id=1, source_target_pairs={{0,1},{1,0},{2,3},{3,2},{4,5},{5,4},{6,7},{7,6},{8,9},{9,8},{10,11... | collective-permute-start | bytes 147464 | tf_op jit(solution)/shard_map/ppermute | solution.py:189
  31.0 4.1 %collective-permute-start.11 = (bf16[96,256]{1,0:T(8,128)(2,1)S(1)}, bf16[96,256]{1,0:T(8,128)(2,1)S(1)}, u32[]{:S(2)}, u32[]{:S(2)}) collective-permute-start(bf16[96,256]{1,0:T(8,128)(2,1)S(1)} %get-tuple-element.26.refs_0_), channel_id=1, source_target_pairs={{0,2},{1,3},{2,0},{3,1},{4,6},{5,7},{6,4},{7,5},{8,10},{9,11},{10,... | collective-permute-start | bytes 147464 | tf_op jit(solution)/shard_map/ppermute | solution.py:189
  31.8 5.3 %collective-permute-start.12 = (bf16[96,256]{1,0:T(8,128)(2,1)S(1)}, bf16[96,256]{1,0:T(8,128)(2,1)S(1)}, u32[]{:S(2)}, u32[]{:S(2)}) collective-permute-start(bf16[96,256]{1,0:T(8,128)(2,1)S(1)} %get-tuple-element.26.refs_0_), channel_id=1, source_target_pairs={{0,3},{1,2},{2,1},{3,0},{4,7},{5,6},{6,5},{7,4},{8,11},{9,10},{10,... | collective-permute-start | bytes 147464 | tf_op jit(solution)/shard_map/ppermute | solution.py:189
  38.5 5.2 %collective-permute-start.13 = (bf16[1168,256]{1,0:T(8,128)(2,1)S(1)}, bf16[1168,256]{1,0:T(8,128)(2,1)S(1)}, u32[]{:S(2)}, u32[]{:S(2)}) collective-permute-start(bf16[1168,256]{1,0:T(8,128)(2,1)S(1)} %get-tuple-element.29), channel_id=1, source_target_pairs={{0,4},{4,0},{8,12},{12,8},{16,20},{20,16},{24,28},{28,24},{1,5},{5... | collective-permute-start | bytes 1794056 | tf_op jit(solution)/shard_map/ppermute | solution.py:189
  43.8 5.3 %collective-permute-start.14 = (bf16[304,256]{1,0:T(8,128)(2,1)S(1)}, bf16[304,256]{1,0:T(8,128)(2,1)S(1)}, u32[]{:S(2)}, u32[]{:S(2)}) collective-permute-start(bf16[304,256]{1,0:T(8,128)(2,1)S(1)} %get-tuple-element.32), channel_id=1, source_target_pairs={{0,8},{4,12},{8,0},{12,4},{16,24},{20,28},{24,16},{28,20},{1,9},{5... | collective-permute-start | bytes 466952 | tf_op jit(solution)/shard_map/ppermute | solution.py:189
  44.8 4.9 %collective-permute-start.15 = (bf16[304,256]{1,0:T(8,128)(2,1)S(1)}, bf16[304,256]{1,0:T(8,128)(2,1)S(1)}, u32[]{:S(2)}, u32[]{:S(2)}) collective-permute-start(bf16[304,256]{1,0:T(8,128)(2,1)S(1)} %get-tuple-element.33), channel_id=1, source_target_pairs={{0,16},{4,20},{8,24},{12,28},{16,0},{20,4},{24,8},{28,12},{1,17},{... | collective-permute-start | bytes 466952 | tf_op jit(solution)/shard_map/ppermute | solution.py:189
  45.4 7.8 %collective-permute-start.16 = (bf16[304,256]{1,0:T(8,128)(2,1)S(1)}, bf16[304,256]{1,0:T(8,128)(2,1)S(1)}, u32[]{:S(2)}, u32[]{:S(2)}) collective-permute-start(bf16[304,256]{1,0:T(8,128)(2,1)S(1)} %get-tuple-element.34), channel_id=1, source_target_pairs={{0,24},{4,28},{8,16},{12,20},{16,8},{20,12},{24,0},{28,4},{1,25},{... | collective-permute-start | bytes 466952 | tf_op jit(solution)/shard_map/ppermute | solution.py:189
  53.9 4.0 %collective-permute-start.17 = (bf16[288,256]{1,0:T(8,128)(2,1)S(1)}, bf16[288,256]{1,0:T(8,128)(2,1)S(1)}, u32[]{:S(2)}, u32[]{:S(2)}) collective-permute-start(bf16[288,256]{1,0:T(8,128)(2,1)S(1)} %get-tuple-element.35.refs_0_), channel_id=1, source_target_pairs={{0,1},{1,0},{2,3},{3,2},{4,5},{5,4},{6,7},{7,6},{8,9},{9,8},{10,11... | collective-permute-start | bytes 442376 | tf_op jit(solution)/shard_map/ppermute | solution.py:189
  53.9 5.7 %collective-permute-start.18 = (bf16[288,256]{1,0:T(8,128)(2,1)S(1)}, bf16[288,256]{1,0:T(8,128)(2,1)S(1)}, u32[]{:S(2)}, u32[]{:S(2)}) collective-permute-start(bf16[288,256]{1,0:T(8,128)(2,1)S(1)} %get-tuple-element.35.refs_0_), channel_id=1, source_target_pairs={{0,2},{1,3},{2,0},{3,1},{4,6},{5,7},{6,4},{7,5},{8,10},{9,11},{10,... | collective-permute-start | bytes 442376 | tf_op jit(solution)/shard_map/ppermute | solution.py:189
  57.0 9.1 %collective-permute-start.19 = (bf16[288,256]{1,0:T(8,128)(2,1)S(1)}, bf16[288,256]{1,0:T(8,128)(2,1)S(1)}, u32[]{:S(2)}, u32[]{:S(2)}) collective-permute-start(bf16[288,256]{1,0:T(8,128)(2,1)S(1)} %get-tuple-element.35.refs_0_), channel_id=1, source_target_pairs={{0,3},{1,2},{2,1},{3,0},{4,7},{5,6},{6,5},{7,4},{8,11},{9,10},{10,... | collective-permute-start | bytes 442376 | tf_op jit(solution)/shard_map/ppermute | solution.py:189
  66.1 7.2 %collective-permute-start.20 = (bf16[288,256]{1,0:T(8,128)(2,1)S(1)}, bf16[288,256]{1,0:T(8,128)(2,1)S(1)}, u32[]{:S(2)}, u32[]{:S(2)}) collective-permute-start(bf16[288,256]{1,0:T(8,128)(2,1)S(1)} %shard_map.101.refs_0_), channel_id=1, source_target_pairs={{0,8},{4,12},{8,0},{12,4},{16,24},{20,28},{24,16},{28,20},{1,9},{5... | collective-permute-start | bytes 442376 | tf_op jit(solution)/shard_map/ppermute | solution.py:189
  66.2 8.8 %collective-permute-start.21 = (bf16[288,256]{1,0:T(8,128)(2,1)S(1)}, bf16[288,256]{1,0:T(8,128)(2,1)S(1)}, u32[]{:S(2)}, u32[]{:S(2)}) collective-permute-start(bf16[288,256]{1,0:T(8,128)(2,1)S(1)} %shard_map.101.refs_0_), channel_id=1, source_target_pairs={{0,16},{4,20},{8,24},{12,28},{16,0},{20,4},{24,8},{28,12},{1,17},{... | collective-permute-start | bytes 442376 | tf_op jit(solution)/shard_map/ppermute | solution.py:189
  66.3 9.3 %collective-permute-start.22 = (bf16[288,256]{1,0:T(8,128)(2,1)S(1)}, bf16[288,256]{1,0:T(8,128)(2,1)S(1)}, u32[]{:S(2)}, u32[]{:S(2)}) collective-permute-start(bf16[288,256]{1,0:T(8,128)(2,1)S(1)} %shard_map.101.refs_0_), channel_id=1, source_target_pairs={{0,24},{4,28},{8,16},{12,20},{16,8},{20,12},{24,0},{28,4},{1,25},{... | collective-permute-start | bytes 442376 | tf_op jit(solution)/shard_map/ppermute | solution.py:189
  68.8 8.5 %collective-permute-start.23 = (bf16[288,256]{1,0:T(8,128)(2,1)S(1)}, bf16[288,256]{1,0:T(8,128)(2,1)S(1)}, u32[]{:S(2)}, u32[]{:S(2)}) collective-permute-start(bf16[288,256]{1,0:T(8,128)(2,1)S(1)} %shard_map.101.refs_0_), channel_id=1, source_target_pairs={{0,4},{4,0},{8,12},{12,8},{16,20},{20,16},{24,28},{28,24},{1,5},{5... | collective-permute-start | bytes 442376 | tf_op jit(solution)/shard_map/ppermute | solution.py:189
  73.3 4.0 %collective-permute-start.24 = (bf16[288,256]{1,0:T(8,128)(2,1)S(1)}, bf16[288,256]{1,0:T(8,128)(2,1)S(1)}, u32[]{:S(2)}, u32[]{:S(2)}) collective-permute-start(bf16[288,256]{1,0:T(8,128)(2,1)S(1)} %collective-permute-done.20.refs_1_), channel_id=1, source_target_pairs={{0,4},{4,0},{8,12},{12,8},{16,20},{20,16},{24,28},{28,24},{1,5},{5... | collective-permute-start | bytes 442376 | tf_op jit(solution)/shard_map/ppermute | solution.py:189
  75.0 2.4 %collective-permute-start.25 = (bf16[288,256]{1,0:T(8,128)(2,1)S(1)}, bf16[288,256]{1,0:T(8,128)(2,1)S(1)}, u32[]{:S(2)}, u32[]{:S(2)}) collective-permute-start(bf16[288,256]{1,0:T(8,128)(2,1)S(1)} %collective-permute-done.21.refs_2_), channel_id=1, source_target_pairs={{0,4},{4,0},{8,12},{12,8},{16,20},{20,16},{24,28},{28,24},{1,5},{5... | collective-permute-start | bytes 442376 | tf_op jit(solution)/shard_map/ppermute | solution.py:189
  75.6 2.7 %collective-permute-start.26 = (bf16[288,256]{1,0:T(8,128)(2,1)S(1)}, bf16[288,256]{1,0:T(8,128)(2,1)S(1)}, u32[]{:S(2)}, u32[]{:S(2)}) collective-permute-start(bf16[288,256]{1,0:T(8,128)(2,1)S(1)} %collective-permute-done.22.refs_3_), channel_id=1, source_target_pairs={{0,4},{4,0},{8,12},{12,8},{16,20},{20,16},{24,28},{28,24},{1,5},{5... | collective-permute-start | bytes 442376 | tf_op jit(solution)/shard_map/ppermute | solution.py:189
  (1 other events, 0.7 us)

commit v2 on v1

--- a/solution.py
+++ b/solution.py
@@ -19,12 +19,12 @@
     return jax.ShapeDtypeStruct(dims, dtype)
 
 
-def call(body, out, specs, *args, scratch=(), flops=0, moved=0, aliases=None):
+def call(body, out, specs, *args, scratch=(), flops=0, moved=0, aliases=None, out_spec=VMEM):
     return pl.pallas_call(
         body,
         out_shape=out,
         in_specs=list(specs),
-        out_specs=jax.tree.map(lambda _: VMEM, out),
+        out_specs=jax.tree.map(lambda _: out_spec, out),
         scratch_shapes=list(scratch),
         input_output_aliases=aliases or {},
         compiler_params=pltpu.CompilerParams(vmem_limit_bytes=24 * 2**20),
@@ -43,7 +43,7 @@
 
         @pl.when(lax.rem(at, slots) < count_ref[relation])
         def _():
-            k = list_ref[at]
+            k = list_ref[relation, lax.rem(at, slots)]
             row = pl.multiple_of(relation * band_rows + lax.div(k, across) * size, size)
             column = pl.multiple_of(lax.rem(k, across) * size, size)
             dense_ref[pl.ds(row, size), pl.ds(column, size)] = values_ref[at]
@@ -57,30 +57,22 @@
     pieces = refs[:count]
     tile_ref, own_ref = refs[count : count + 2]
     sends = refs[count + 2 : count + 1 + n_src]
-    features, message, sems = refs[count + 1 + n_src :]
+    features, message = refs[count + 1 + n_src :]
     rows = pieces[0].shape[0]
-    copies = []
     for i, piece in enumerate(pieces):
         start = pl.multiple_of(where_ref[1 + i] * rows, 16)
-        copies.append(pltpu.make_async_copy(piece, features.at[pl.ds(start, rows)], sems.at[i]))
-        copies[-1].start()
-    for copy in copies:
-        copy.wait()
+        features[pl.ds(start, rows)] = piece[...]
     width = features.shape[1]
     band_rows = tile_ref.shape[0]
-    total = None
-    for r in range(dense_ref.shape[0] // band_rows):
-        part = jnp.dot(
-            dense_ref[r * band_rows : (r + 1) * band_rows],
-            features[...],
-            preferred_element_type=F32,
-        ).astype(BF)
-        tile_ref[:, r * width : (r + 1) * width] = part
-        term = jnp.dot(
-            part, weight_ref[r * width : (r + 1) * width], preferred_element_type=F32
-        )
-        total = term if total is None else total + term
-    message[...] = total
+    step = 128
+    for i in range(0, band_rows, step):
+        for r in range(dense_ref.shape[0] // band_rows):
+            tile_ref[i : i + step, r * width : (r + 1) * width] = jnp.dot(
+                dense_ref[r * band_rows + i : r * band_rows + i + step],
+                features[...],
+                preferred_element_type=F32,
+            ).astype(BF)
+    message[...] = jnp.dot(tile_ref[...], weight_ref[...], preferred_element_type=F32)
     block = own_ref.shape[0]
     for m in range(n_src):
         start = pl.multiple_of((where_ref[0] ^ m) * block, 16)
@@ -175,14 +167,19 @@
     out_ref[...] = tree([part[...].astype(F32) for part in parts]).astype(BF)
 
 
-def spread(chips, where_ref, *refs):
-    *pieces, out_ref = refs
-    rows = pieces[0].shape[0]
+def spread(which, where_ref, *refs):
+    chunks, (out_ref, wide, sems) = refs[: len(which)], refs[-3:]
+    rows = chunks[0].shape[0]
     half = out_ref.shape[0] // 2
-    for i, piece in enumerate(pieces):
-        core = where_ref[1] if i < chips else 1 - where_ref[1]
-        start = core * half + (where_ref[2] ^ (i % chips)) * rows
-        out_ref[pl.ds(pl.multiple_of(start, 16), rows)] = piece[...].astype(F32)
+    copies = []
+    for i, (core, chip) in enumerate(which):
+        wide[i] = chunks[i][...].astype(F32)
+        start = (where_ref[1] ^ core) * half + (where_ref[2] ^ chip) * rows
+        target = out_ref.at[pl.ds(pl.multiple_of(start, 16), rows)]
+        copies.append(pltpu.make_async_copy(wide.at[i], target, sems.at[i]))
+        copies[-1].start()
+    for copy in copies:
+        copy.wait()
 
 
 def swap(x, axis, n, mask):
@@ -202,7 +199,7 @@
         functools.partial(assemble, band_rows),
         shape((relations * band_rows, tile_columns), BF),
         (SMEM, SMEM, VMEM),
-        block_list.reshape(-1),
+        block_list.reshape(relations, -1),
         block_count.reshape(-1),
         block_values.reshape(-1, block_size, block_size),
         flops=10**8,
@@ -253,6 +250,7 @@
         return swap(x, "src", n_src, m)
 
     near = [features] + [over_chips(features, m) for m in range(1, chips)]
+    near[1], dense = lax.optimization_barrier((near[1], dense))
     far = [over_core(x) for x in near]
     order = [me ^ (2 * m) for m in range(chips)] + [me ^ (2 * m + 1) for m in range(chips)]
     where = jnp.stack([z] + order).astype(jnp.int32)
@@ -260,7 +258,7 @@
         functools.partial(forward, n_src, n_dst),
         [shape((band_rows, relations * width), BF), shape((block, hidden), F32)]
         + [shape((block, hidden), BF)] * (n_src - 1),
-        [SMEM, VMEM, VMEM] + [ANY] * n_dst,
+        [SMEM] + [VMEM] * (2 + n_dst),
         where,
         dense,
         weight,
@@ -269,7 +267,6 @@
         scratch=[
             pltpu.VMEM((own_rows * n_dst, width), BF),
             pltpu.VMEM((band_rows, hidden), F32),
-            pltpu.SemaphoreType.DMA((n_dst,)),
         ],
         flops=2 * 10**9,
         moved=8 * 2**20,
@@ -328,14 +325,26 @@
     chunk = call(add_bands, shape((piece, hidden), BF), [VMEM] * n_src, *parts)
     near = [chunk] + [over_chips(chunk, m) for m in range(1, chips)]
     far = [over_core(x) for x in near]
-    weight_grad = call(
-        functools.partial(spread, chips),
-        shape((total_rows, hidden), F32),
-        [SMEM] + [VMEM] * n_dst,
-        place,
-        *near,
-        *far,
-    )
+    chunks = {(0, m): x for m, x in enumerate(near)} | {(1, m): x for m, x in enumerate(far)}
+    last = [(0, chips - 1), (1, chips - 1)]
+    first = [w for w in chunks if w not in last]
+    weight_grad = None
+    for which in (first, last):
+        before = [] if weight_grad is None else [weight_grad]
+        weight_grad = call(
+            functools.partial(spread, which),
+            shape((total_rows, hidden), F32),
+            [SMEM] + [VMEM] * len(which) + [ANY] * len(before),
+            place,
+            *[chunks[w] for w in which],
+            *before,
+            scratch=[
+                pltpu.VMEM((len(which), piece, hidden), F32),
+                pltpu.SemaphoreType.DMA((len(which),)),
+            ],
+            aliases={1 + len(which): 0} if before else None,
+            out_spec=ANY,
+        )
     weight_grad = weight_grad.reshape(relations, width, hidden).transpose(1, 0, 2)
     return output, weight_grad, bias_grad.reshape(hidden)
 

time: 81.2 us -> 93.3 us (1.15)
  local copies, waits for them, and re-layouts: 2.26 us -> 18.3 us
  starting transfers between devices: 38.6 us -> 34.5 us
  waiting for transfers between devices: 26.1 us -> 27.6 us
    unnamed x12 -> x45, local copies, waits for them, and re-layouts: 2.09 us -> 18.2 us
    ppermute x27, starting transfers between devices: 38.6 us -> 34.5 us  [swap(): return lax.ppermute(x, axis, [(i, i ^ mask) for i in range(n)])]
    ppermute x27, waiting for transfers between devices: 26.1 us -> 27.6 us  [swap(): return lax.ppermute(x, axis, [(i, i ^ mask) for i in range(n)])]
    pallas_call x9 -> x10, Pallas kernels: 11.9 us -> 11.7 us  [call(): pl.pallas_call(body, out_shape=out, in_specs=list(specs), out_specs=jax.t...]
  transfers between devices with their start and end apart: 27 -> 27, of which waited for: 12 -> 10; matrix products, arithmetic and copies ran while one was open for 1% -> 1% of each run, Pallas kernels for 3% -> 4%
where the time goes in v2:
time: 93.3 us; the launch traced here: 92.9 us
  starting transfers between devices  34.5 us (37%)
  waiting for transfers between devices  27.6 us (30%)
  local copies, waits for them, and re-layouts  18.3 us (20%)
  Pallas kernels  11.7 us (13%)
    ppermute x27, starting transfers between devices, swap(): return lax.ppermute(x, axis, [(i, i ^ mask) for i in range(n)])  34.5 us
    ppermute x27, waiting for transfers between devices, swap(): return lax.ppermute(x, axis, [(i, i ^ mask) for i in range(n)])  27.6 us
    unnamed x45, local copies, waits for them, and re-layouts  18.2 us
    pallas_call x10, Pallas kernels, call(): pl.pallas_call(body, out_shape=out, in_specs=list(specs), out_specs=jax.t...  11.7 us
  transfers between devices with their start and end apart: 27, of which 10 were waited for; matrix products, arithmetic and copies ran while one was open for 1% of the time, Pallas kernels for 4%

profile of v2, /device:TPU:1, one launch (start us, length us, event | category | flops | bytes accessed | tf_op | source)
XLA Modules:
  0.0 92.9 jit_solution(5204260159829747901)
XLA Ops:
  0.6 2.1 %collective-permute-start = (bf16[96,768]{1,0:T(8,128)(2,1)}, bf16[96,768]{1,0:T(8,128)(2,1)S(1)}, u32[]{:S(2)}, u32[]{:S(2)}) collective-permute-start(bf16[96,768]{1,0:T(8,128)(2,1)} %refs_0_.1), channel_id=1, source_target_pairs={{0,8},{4,12},{8,0},{12,4},{16,24},{20,28},{24,16},{28,20},{1,9},{5... | collective-permute-start | bytes 442376 | tf_op jit(solution)/shard_map/ppermute | solution.py:186
  2.7 1.2 %collective-permute-start.2 = (bf16[96,768]{1,0:T(8,128)(2,1)}, bf16[96,768]{1,0:T(8,128)(2,1)S(1)}, u32[]{:S(2)}, u32[]{:S(2)}) collective-permute-start(bf16[96,768]{1,0:T(8,128)(2,1)} %refs_0_.1), channel_id=1, source_target_pairs={{0,24},{4,28},{8,16},{12,20},{16,8},{20,12},{24,0},{28,4},{1,25},{... | collective-permute-start | bytes 442376 | tf_op jit(solution)/shard_map/ppermute | solution.py:186
  4.0 1.2 %collective-permute-start.3 = (bf16[96,768]{1,0:T(8,128)(2,1)}, bf16[96,768]{1,0:T(8,128)(2,1)S(1)}, u32[]{:S(2)}, u32[]{:S(2)}) collective-permute-start(bf16[96,768]{1,0:T(8,128)(2,1)} %refs_0_.1), channel_id=1, source_target_pairs={{0,4},{4,0},{8,12},{12,8},{16,20},{20,16},{24,28},{28,24},{1,5},{5... | collective-permute-start | bytes 442376 | tf_op jit(solution)/shard_map/ppermute | solution.py:186
  5.9 1.4 %copy-done = bf16[1,1,3,16,128,128]{5,4,3,2,1,0:T(8,128)(2,1)S(1)} copy-done((bf16[1,1,3,16,128,128]{5,4,3,2,1,0:T(8,128)(2,1)S(1)}, bf16[1,1,3,16,128,128]{5,4,3,2,1,0:T(8,128)(2,1)}, u32[]{:S(2)}) %copy-start) | copy-done | bytes 1572888
  8.0 1.9 %shard_map.94.dense_ref = bf16[1152,768]{1,0:T(8,128)(2,1)S(1)} custom-call(s32[3,16]{1,0:T(4,128)S(1)} %bitcast.24, s32[3]{0:T(128)S(1)} %bitcast.25, bf16[48,128,128]{2,1,0:T(8,128)(2,1)S(1)} %bitcast.23), custom_call_target="tpu_custom_call" | custom-call | flops 100000000 | bytes 4194304 | tf_op jit(solution)/shard_map/pallas_call | solution.py:23
  10.6 1.7 %collective-permute-start.6 = (bf16[96,768]{1,0:T(8,128)(2,1)S(1)}, bf16[96,768]{1,0:T(8,128)(2,1)S(1)}, u32[]{:S(2)}, u32[]{:S(2)}) collective-permute-start(bf16[96,768]{1,0:T(8,128)(2,1)S(1)} %collective-permute-done.2.refs_3_), channel_id=1, source_target_pairs={{0,4},{4,0},{8,12},{12,8},{16,20},{20,16},{24,28},{28,24},{1,5},{5... | collective-permute-start | bytes 442376 | tf_op jit(solution)/shard_map/ppermute | solution.py:186
  17.6 1.3 %copy-done.5 = bf16[768,3,256]{2,0,1:T(8,128)(2,1)S(1)} copy-done((bf16[768,3,256]{2,0,1:T(8,128)(2,1)S(1)}, bf16[768,3,256]{2,0,1:T(8,128)(2,1)}, u32[]{:S(2)}) %copy-start.5) | copy-done | bytes 1179672
  19.8 0.9 copy-done.8
  26.2 3.3 %shard_map.95 = (bf16[384,2304]{1,0:T(8,128)(2,1)S(1)}, f32[96,256]{1,0:T(8,128)S(1)}, bf16[96,256]{1,0:T(8,128)(2,1)}, bf16[96,256]{1,0:T(8,128)(2,1)}, bf16[96,256]{1,0:T(8,128)(2,1)}) custom-call(s32[9]{0:T(128)S(1)} %stack.49.where_ref, bf16[1152,768]{1,0:T(8,128)(2,1)S(1)} %shard_map.94.dense_ref, bf16[2304,256]{1,0:T(8,128)(2,1)S(1)} %bitcast.26, ...), custom_call_target="tpu_custom_call" | custom-call | flops 2000000000 | bytes 8388608 | tf_op jit(solution)/shard_map/pallas_call | solution.py:23
  30.1 1.3 %collective-permute-start.7 = (bf16[96,256]{1,0:T(8,128)(2,1)}, bf16[96,256]{1,0:T(8,128)(2,1)S(1)}, u32[]{:S(2)}, u32[]{:S(2)}) collective-permute-start(bf16[96,256]{1,0:T(8,128)(2,1)} %get-tuple-element.25), channel_id=1, source_target_pairs={{0,1},{1,0},{2,3},{3,2},{4,5},{5,4},{6,7},{7,6},{8,9},{9,8},{10,11... | collective-permute-start | bytes 147464 | tf_op jit(solution)/shard_map/ppermute | solution.py:186
  31.4 2.3 %collective-permute-start.8 = (bf16[96,256]{1,0:T(8,128)(2,1)}, bf16[96,256]{1,0:T(8,128)(2,1)S(1)}, u32[]{:S(2)}, u32[]{:S(2)}) collective-permute-start(bf16[96,256]{1,0:T(8,128)(2,1)} %get-tuple-element.26), channel_id=1, source_target_pairs={{0,2},{1,3},{2,0},{3,1},{4,6},{5,7},{6,4},{7,5},{8,10},{9,11},{10,... | collective-permute-start | bytes 147464 | tf_op jit(solution)/shard_map/ppermute | solution.py:186
  33.8 2.2 %collective-permute-done.8.refs_1_ = bf16[96,256]{1,0:T(8,128)(2,1)S(1)} collective-permute-done((bf16[96,256]{1,0:T(8,128)(2,1)}, bf16[96,256]{1,0:T(8,128)(2,1)S(1)}, u32[]{:S(2)}, u32[]{:S(2)}) %collective-permute-start.8) | collective-permute-done | bytes 49184 | tf_op jit(solution)/shard_map/ppermute | solution.py:186
  36.0 2.8 %collective-permute-done.9.refs_2_ = bf16[96,256]{1,0:T(8,128)(2,1)S(1)} collective-permute-done((bf16[96,256]{1,0:T(8,128)(2,1)}, bf16[96,256]{1,0:T(8,128)(2,1)S(1)}, u32[]{:S(2)}, u32[]{:S(2)}) %collective-permute-start.9) | collective-permute-done | bytes 49184 | tf_op jit(solution)/shard_map/ppermute | solution.py:186
  41.7 3.0 %collective-permute-start.10 = (bf16[96,256]{1,0:T(8,128)(2,1)S(1)}, bf16[96,256]{1,0:T(8,128)(2,1)S(1)}, u32[]{:S(2)}, u32[]{:S(2)}) collective-permute-start(bf16[96,256]{1,0:T(8,128)(2,1)S(1)} %get-tuple-element.30.refs_0_), channel_id=1, source_target_pairs={{0,1},{1,0},{2,3},{3,2},{4,5},{5,4},{6,7},{7,6},{8,9},{9,8},{10,11... | collective-permute-start | bytes 147464 | tf_op jit(solution)/shard_map/ppermute | solution.py:186
  46.9 1.3 %shard_map.98 = (f32[1152,256]{1,0:T(8,128)S(1)}, bf16[1168,256]{1,0:T(8,128)(2,1)S(1)}, f32[8,256]{1,0:T(8,128)S(1)}) custom-call(s32[3]{0:T(128)S(1)} %pad_add_fusion.where_ref, bf16[2304,384]{1,0:T(8,128)(2,1)S(1)} %shard_map.97.tile_ref, bf16[96,256]{1,0:T(8,128)(2,1)S(1)} %get-tuple-element.30.refs_0_, ...), custom_call_target="tpu_custom_call" | custom-call | tf_op jit(solution)/shard_map/pallas_call | solution.py:23
  48.2 3.4 %collective-permute-start.13 = (bf16[1168,256]{1,0:T(8,128)(2,1)S(1)}, bf16[1168,256]{1,0:T(8,128)(2,1)S(1)}, u32[]{:S(2)}, u32[]{:S(2)}) collective-permute-start(bf16[1168,256]{1,0:T(8,128)(2,1)S(1)} %get-tuple-element.33), channel_id=1, source_target_pairs={{0,4},{4,0},{8,12},{12,8},{16,20},{20,16},{24,28},{28,24},{1,5},{5... | collective-permute-start | bytes 1794056 | tf_op jit(solution)/shard_map/ppermute | solution.py:186
  51.6 1.6 %collective-permute-done.13.received_ref = bf16[1168,256]{1,0:T(8,128)(2,1)S(1)} collective-permute-done((bf16[1168,256]{1,0:T(8,128)(2,1)S(1)}, bf16[1168,256]{1,0:T(8,128)(2,1)S(1)}, u32[]{:S(2)}, u32[]{:S(2)}) %collective-permute-start.13) | collective-permute-done | bytes 598048 | tf_op jit(solution)/shard_map/ppermute | solution.py:186
  53.4 1.3 %collective-permute-start.14 = (bf16[304,256]{1,0:T(8,128)(2,1)S(1)}, bf16[304,256]{1,0:T(8,128)(2,1)S(1)}, u32[]{:S(2)}, u32[]{:S(2)}) collective-permute-start(bf16[304,256]{1,0:T(8,128)(2,1)S(1)} %get-tuple-element.36), channel_id=1, source_target_pairs={{0,8},{4,12},{8,0},{12,4},{16,24},{20,28},{24,16},{28,20},{1,9},{5... | collective-permute-start | bytes 466952 | tf_op jit(solution)/shard_map/ppermute | solution.py:186
  54.9 1.2 %collective-permute-start.16 = (bf16[304,256]{1,0:T(8,128)(2,1)S(1)}, bf16[304,256]{1,0:T(8,128)(2,1)S(1)}, u32[]{:S(2)}, u32[]{:S(2)}) collective-permute-start(bf16[304,256]{1,0:T(8,128)(2,1)S(1)} %get-tuple-element.38), channel_id=1, source_target_pairs={{0,24},{4,28},{8,16},{12,20},{16,8},{20,12},{24,0},{28,4},{1,25},{... | collective-permute-start | bytes 466952 | tf_op jit(solution)/shard_map/ppermute | solution.py:186
  56.1 2.6 %collective-permute-done.14.refs_0_ = bf16[304,256]{1,0:T(8,128)(2,1)S(1)} collective-permute-done((bf16[304,256]{1,0:T(8,128)(2,1)S(1)}, bf16[304,256]{1,0:T(8,128)(2,1)S(1)}, u32[]{:S(2)}, u32[]{:S(2)}) %collective-permute-start.14) | collective-permute-done | bytes 155680 | tf_op jit(solution)/shard_map/ppermute | solution.py:186
  58.7 4.2 %collective-permute-done.15.refs_1_ = bf16[304,256]{1,0:T(8,128)(2,1)S(1)} collective-permute-done((bf16[304,256]{1,0:T(8,128)(2,1)S(1)}, bf16[304,256]{1,0:T(8,128)(2,1)S(1)}, u32[]{:S(2)}, u32[]{:S(2)}) %collective-permute-start.15) | collective-permute-done | bytes 155680 | tf_op jit(solution)/shard_map/ppermute | solution.py:186
  63.5 1.6 %collective-permute-start.19 = (bf16[288,256]{1,0:T(8,128)(2,1)S(1)}, bf16[288,256]{1,0:T(8,128)(2,1)S(1)}, u32[]{:S(2)}, u32[]{:S(2)}) collective-permute-start(bf16[288,256]{1,0:T(8,128)(2,1)S(1)} %get-tuple-element.39.refs_0_), channel_id=1, source_target_pairs={{0,3},{1,2},{2,1},{3,0},{4,7},{5,6},{6,5},{7,4},{8,11},{9,10},{10,... | collective-permute-start | bytes 442376 | tf_op jit(solution)/shard_map/ppermute | solution.py:186
  66.0 1.1 %collective-permute-start.17 = (bf16[288,256]{1,0:T(8,128)(2,1)S(1)}, bf16[288,256]{1,0:T(8,128)(2,1)S(1)}, u32[]{:S(2)}, u32[]{:S(2)}) collective-permute-start(bf16[288,256]{1,0:T(8,128)(2,1)S(1)} %get-tuple-element.39.refs_0_), channel_id=1, source_target_pairs={{0,1},{1,0},{2,3},{3,2},{4,5},{5,4},{6,7},{7,6},{8,9},{9,8},{10,11... | collective-permute-start | bytes 442376 | tf_op jit(solution)/shard_map/ppermute | solution.py:186
  67.1 2.5 %collective-permute-done.19.refs_3_ = bf16[288,256]{1,0:T(8,128)(2,1)S(1)} collective-permute-done((bf16[288,256]{1,0:T(8,128)(2,1)S(1)}, bf16[288,256]{1,0:T(8,128)(2,1)S(1)}, u32[]{:S(2)}, u32[]{:S(2)}) %collective-permute-start.19) | collective-permute-done | bytes 147488 | tf_op jit(solution)/shard_map/ppermute | solution.py:186
  69.5 9.3 %collective-permute-done.18.refs_2_ = bf16[288,256]{1,0:T(8,128)(2,1)S(1)} collective-permute-done((bf16[288,256]{1,0:T(8,128)(2,1)S(1)}, bf16[288,256]{1,0:T(8,128)(2,1)S(1)}, u32[]{:S(2)}, u32[]{:S(2)}) %collective-permute-start.18) | collective-permute-done | bytes 147488 | tf_op jit(solution)/shard_map/ppermute | solution.py:186
  79.4 1.2 %collective-permute-start.22 = (bf16[288,256]{1,0:T(8,128)(2,1)S(1)}, bf16[288,256]{1,0:T(8,128)(2,1)S(1)}, u32[]{:S(2)}, u32[]{:S(2)}) collective-permute-start(bf16[288,256]{1,0:T(8,128)(2,1)S(1)} %shard_map.101.refs_0_), channel_id=1, source_target_pairs={{0,8},{4,12},{8,0},{12,4},{16,24},{20,28},{24,16},{28,20},{1,9},{5... | collective-permute-start | bytes 442376 | tf_op jit(solution)/shard_map/ppermute | solution.py:186
  80.5 1.1 %collective-permute-start.20 = (bf16[288,256]{1,0:T(8,128)(2,1)S(1)}, bf16[288,256]{1,0:T(8,128)(2,1)S(1)}, u32[]{:S(2)}, u32[]{:S(2)}) collective-permute-start(bf16[288,256]{1,0:T(8,128)(2,1)S(1)} %shard_map.101.refs_0_), channel_id=1, source_target_pairs={{0,24},{4,28},{8,16},{12,20},{16,8},{20,12},{24,0},{28,4},{1,25},{... | collective-permute-start | bytes 442376 | tf_op jit(solution)/shard_map/ppermute | solution.py:186
  81.7 2.2 %collective-permute-start.24 = (bf16[288,256]{1,0:T(8,128)(2,1)S(1)}, bf16[288,256]{1,0:T(8,128)(2,1)S(1)}, u32[]{:S(2)}, u32[]{:S(2)}) collective-permute-start(bf16[288,256]{1,0:T(8,128)(2,1)S(1)} %shard_map.101.refs_0_), channel_id=1, source_target_pairs={{0,4},{4,0},{8,12},{12,8},{16,20},{20,16},{24,28},{28,24},{1,5},{5... | collective-permute-start | bytes 442376 | tf_op jit(solution)/shard_map/ppermute | solution.py:186
  83.9 2.9 %collective-permute-start.26 = (bf16[288,256]{1,0:T(8,128)(2,1)S(1)}, bf16[288,256]{1,0:T(8,128)(2,1)S(1)}, u32[]{:S(2)}, u32[]{:S(2)}) collective-permute-start(bf16[288,256]{1,0:T(8,128)(2,1)S(1)} %collective-permute-done.23.refs_2_), channel_id=1, source_target_pairs={{0,4},{4,0},{8,12},{12,8},{16,20},{20,16},{24,28},{28,24},{1,5},{5... | collective-permute-start | bytes 442376 | tf_op jit(solution)/shard_map/ppermute | solution.py:186
  87.2 2.4 %collective-permute-start.21 = (bf16[288,256]{1,0:T(8,128)(2,1)S(1)}, bf16[288,256]{1,0:T(8,128)(2,1)S(1)}, u32[]{:S(2)}, u32[]{:S(2)}) collective-permute-start(bf16[288,256]{1,0:T(8,128)(2,1)S(1)} %collective-permute-done.20.refs_0_), channel_id=1, source_target_pairs={{0,4},{4,0},{8,12},{12,8},{16,20},{20,16},{24,28},{28,24},{1,5},{5... | collective-permute-start | bytes 442376 | tf_op jit(solution)/shard_map/ppermute | solution.py:186
  89.6 1.8 %shard_map.102.refs_2_ = f32[2304,256]{1,0:T(8,128)} custom-call(s32[3]{0:T(128)S(1)} %pad_add_fusion.where_ref, bf16[288,256]{1,0:T(8,128)(2,1)S(1)} %shard_map.101.refs_0_, bf16[288,256]{1,0:T(8,128)(2,1)S(1)} %collective-permute-done.22.refs_1_, bf16[288,256]{1,0:T(8,128)(2,1)S(1)} %collective-permute-done.23.refs_2_, ...), custom_call_target="tpu_custom_call" | custom-call | tf_op jit(solution)/shard_map/pallas_call | solution.py:23
  91.5 1.4 %shard_map.103 = f32[2304,256]{1,0:T(8,128)} custom-call(s32[3]{0:T(128)S(1)} %pad_add_fusion.where_ref, bf16[288,256]{1,0:T(8,128)(2,1)S(1)} %collective-permute-done.20.refs_0_, bf16[288,256]{1,0:T(8,128)(2,1)S(1)} %collective-permute-done.21.refs_1_, f32[2304,256]{1,0:T(8,128)} %shard_map.102.refs_2_), custom_call_target="tpu_custom_call", output_to_operand_aliasing={{}: (3, {})} | custom-call | tf_op jit(solution)/shard_map/pallas_call | solution.py:23
  (80 shorter events, 22.2 us)
Async XLA Ops:
  0.6 9.2 %collective-permute-start = (bf16[96,768]{1,0:T(8,128)(2,1)}, bf16[96,768]{1,0:T(8,128)(2,1)S(1)}, u32[]{:S(2)}, u32[]{:S(2)}) collective-permute-start(bf16[96,768]{1,0:T(8,128)(2,1)} %refs_0_.1), channel_id=1, source_target_pairs={{0,8},{4,12},{8,0},{12,4},{16,24},{20,28},{24,16},{28,20},{1,9},{5... | collective-permute-start | bytes 442376 | tf_op jit(solution)/shard_map/ppermute | solution.py:186
  2.7 7.8 %collective-permute-start.2 = (bf16[96,768]{1,0:T(8,128)(2,1)}, bf16[96,768]{1,0:T(8,128)(2,1)S(1)}, u32[]{:S(2)}, u32[]{:S(2)}) collective-permute-start(bf16[96,768]{1,0:T(8,128)(2,1)} %refs_0_.1), channel_id=1, source_target_pairs={{0,24},{4,28},{8,16},{12,20},{16,8},{20,12},{24,0},{28,4},{1,25},{... | collective-permute-start | bytes 442376 | tf_op jit(solution)/shard_map/ppermute | solution.py:186
  3.9 8.9 %collective-permute-start.1 = (bf16[96,768]{1,0:T(8,128)(2,1)}, bf16[96,768]{1,0:T(8,128)(2,1)S(1)}, u32[]{:S(2)}, u32[]{:S(2)}) collective-permute-start(bf16[96,768]{1,0:T(8,128)(2,1)} %refs_0_.1), channel_id=1, source_target_pairs={{0,16},{4,20},{8,24},{12,28},{16,0},{20,4},{24,8},{28,12},{1,17},{... | collective-permute-start | bytes 442376 | tf_op jit(solution)/shard_map/ppermute | solution.py:186
  4.0 11.0 %collective-permute-start.3 = (bf16[96,768]{1,0:T(8,128)(2,1)}, bf16[96,768]{1,0:T(8,128)(2,1)S(1)}, u32[]{:S(2)}, u32[]{:S(2)}) collective-permute-start(bf16[96,768]{1,0:T(8,128)(2,1)} %refs_0_.1), channel_id=1, source_target_pairs={{0,4},{4,0},{8,12},{12,8},{16,20},{20,16},{24,28},{28,24},{1,5},{5... | collective-permute-start | bytes 442376 | tf_op jit(solution)/shard_map/ppermute | solution.py:186
  5.9 1.4 %copy-start = (bf16[1,1,3,16,128,128]{5,4,3,2,1,0:T(8,128)(2,1)S(1)}, bf16[1,1,3,16,128,128]{5,4,3,2,1,0:T(8,128)(2,1)}, u32[]{:S(2)}) copy-start(bf16[1,1,3,16,128,128]{5,4,3,2,1,0:T(8,128)(2,1)} %param.10) | copy-start | bytes 4718596
  10.6 5.1 %collective-permute-start.6 = (bf16[96,768]{1,0:T(8,128)(2,1)S(1)}, bf16[96,768]{1,0:T(8,128)(2,1)S(1)}, u32[]{:S(2)}, u32[]{:S(2)}) collective-permute-start(bf16[96,768]{1,0:T(8,128)(2,1)S(1)} %collective-permute-done.2.refs_3_), channel_id=1, source_target_pairs={{0,4},{4,0},{8,12},{12,8},{16,20},{20,16},{24,28},{28,24},{1,5},{5... | collective-permute-start | bytes 442376 | tf_op jit(solution)/shard_map/ppermute | solution.py:186
  12.9 3.5 %collective-permute-start.5 = (bf16[96,768]{1,0:T(8,128)(2,1)S(1)}, bf16[96,768]{1,0:T(8,128)(2,1)S(1)}, u32[]{:S(2)}, u32[]{:S(2)}) collective-permute-start(bf16[96,768]{1,0:T(8,128)(2,1)S(1)} %collective-permute-done.1.refs_2_), channel_id=1, source_target_pairs={{0,4},{4,0},{8,12},{12,8},{16,20},{20,16},{24,28},{28,24},{1,5},{5... | collective-permute-start | bytes 442376 | tf_op jit(solution)/shard_map/ppermute | solution.py:186
  14.2 2.7 %collective-permute-start.4 = (bf16[96,768]{1,0:T(8,128)(2,1)S(1)}, bf16[96,768]{1,0:T(8,128)(2,1)S(1)}, u32[]{:S(2)}, u32[]{:S(2)}) collective-permute-start(bf16[96,768]{1,0:T(8,128)(2,1)S(1)} %collective-permute-done.refs_1_), channel_id=1, source_target_pairs={{0,4},{4,0},{8,12},{12,8},{16,20},{20,16},{24,28},{28,24},{1,5},{5... | collective-permute-start | bytes 442376 | tf_op jit(solution)/shard_map/ppermute | solution.py:186
  17.6 1.3 %copy-start.5 = (bf16[768,3,256]{2,0,1:T(8,128)(2,1)S(1)}, bf16[768,3,256]{2,0,1:T(8,128)(2,1)}, u32[]{:S(2)}) copy-start(bf16[768,3,256]{2,0,1:T(8,128)(2,1)} %param.8) | copy-start | bytes 3538948
  18.9 0.9 copy-start.6
  19.8 0.9 copy-start.8
  26.2 7.6 %copy-start.21 = (bf16[256]{0:T(256)(128)(2,1)S(1)}, bf16[256]{0:T(256)(128)(2,1)}, u32[]{:S(2)}) copy-start(bf16[256]{0:T(256)(128)(2,1)} %param.9) | copy-start | bytes 1540
  30.1 3.6 %collective-permute-start.7 = (bf16[96,256]{1,0:T(8,128)(2,1)}, bf16[96,256]{1,0:T(8,128)(2,1)S(1)}, u32[]{:S(2)}, u32[]{:S(2)}) collective-permute-start(bf16[96,256]{1,0:T(8,128)(2,1)} %get-tuple-element.25), channel_id=1, source_target_pairs={{0,1},{1,0},{2,3},{3,2},{4,5},{5,4},{6,7},{7,6},{8,9},{9,8},{10,11... | collective-permute-start | bytes 147464 | tf_op jit(solution)/shard_map/ppermute | solution.py:186
  31.4 4.6 %collective-permute-start.8 = (bf16[96,256]{1,0:T(8,128)(2,1)}, bf16[96,256]{1,0:T(8,128)(2,1)S(1)}, u32[]{:S(2)}, u32[]{:S(2)}) collective-permute-start(bf16[96,256]{1,0:T(8,128)(2,1)} %get-tuple-element.26), channel_id=1, source_target_pairs={{0,2},{1,3},{2,0},{3,1},{4,6},{5,7},{6,4},{7,5},{8,10},{9,11},{10,... | collective-permute-start | bytes 147464 | tf_op jit(solution)/shard_map/ppermute | solution.py:186
  33.7 5.1 %collective-permute-start.9 = (bf16[96,256]{1,0:T(8,128)(2,1)}, bf16[96,256]{1,0:T(8,128)(2,1)S(1)}, u32[]{:S(2)}, u32[]{:S(2)}) collective-permute-start(bf16[96,256]{1,0:T(8,128)(2,1)} %get-tuple-element.27), channel_id=1, source_target_pairs={{0,3},{1,2},{2,1},{3,0},{4,7},{5,6},{6,5},{7,4},{8,11},{9,10},{10,... | collective-permute-start | bytes 147464 | tf_op jit(solution)/shard_map/ppermute | solution.py:186
  41.2 4.9 %collective-permute-start.12 = (bf16[96,256]{1,0:T(8,128)(2,1)S(1)}, bf16[96,256]{1,0:T(8,128)(2,1)S(1)}, u32[]{:S(2)}, u32[]{:S(2)}) collective-permute-start(bf16[96,256]{1,0:T(8,128)(2,1)S(1)} %get-tuple-element.30.refs_0_), channel_id=1, source_target_pairs={{0,3},{1,2},{2,1},{3,0},{4,7},{5,6},{6,5},{7,4},{8,11},{9,10},{10,... | collective-permute-start | bytes 147464 | tf_op jit(solution)/shard_map/ppermute | solution.py:186
  41.7 5.2 %collective-permute-start.11 = (bf16[96,256]{1,0:T(8,128)(2,1)S(1)}, bf16[96,256]{1,0:T(8,128)(2,1)S(1)}, u32[]{:S(2)}, u32[]{:S(2)}) collective-permute-start(bf16[96,256]{1,0:T(8,128)(2,1)S(1)} %get-tuple-element.30.refs_0_), channel_id=1, source_target_pairs={{0,2},{1,3},{2,0},{3,1},{4,6},{5,7},{6,4},{7,5},{8,10},{9,11},{10,... | collective-permute-start | bytes 147464 | tf_op jit(solution)/shard_map/ppermute | solution.py:186
  41.7 5.2 %collective-permute-start.10 = (bf16[96,256]{1,0:T(8,128)(2,1)S(1)}, bf16[96,256]{1,0:T(8,128)(2,1)S(1)}, u32[]{:S(2)}, u32[]{:S(2)}) collective-permute-start(bf16[96,256]{1,0:T(8,128)(2,1)S(1)} %get-tuple-element.30.refs_0_), channel_id=1, source_target_pairs={{0,1},{1,0},{2,3},{3,2},{4,5},{5,4},{6,7},{7,6},{8,9},{9,8},{10,11... | collective-permute-start | bytes 147464 | tf_op jit(solution)/shard_map/ppermute | solution.py:186
  48.2 5.1 %collective-permute-start.13 = (bf16[1168,256]{1,0:T(8,128)(2,1)S(1)}, bf16[1168,256]{1,0:T(8,128)(2,1)S(1)}, u32[]{:S(2)}, u32[]{:S(2)}) collective-permute-start(bf16[1168,256]{1,0:T(8,128)(2,1)S(1)} %get-tuple-element.33), channel_id=1, source_target_pairs={{0,4},{4,0},{8,12},{12,8},{16,20},{20,16},{24,28},{28,24},{1,5},{5... | collective-permute-start | bytes 1794056 | tf_op jit(solution)/shard_map/ppermute | solution.py:186
  53.4 5.3 %collective-permute-start.14 = (bf16[304,256]{1,0:T(8,128)(2,1)S(1)}, bf16[304,256]{1,0:T(8,128)(2,1)S(1)}, u32[]{:S(2)}, u32[]{:S(2)}) collective-permute-start(bf16[304,256]{1,0:T(8,128)(2,1)S(1)} %get-tuple-element.36), channel_id=1, source_target_pairs={{0,8},{4,12},{8,0},{12,4},{16,24},{20,28},{24,16},{28,20},{1,9},{5... | collective-permute-start | bytes 466952 | tf_op jit(solution)/shard_map/ppermute | solution.py:186
  54.7 8.2 %collective-permute-start.15 = (bf16[304,256]{1,0:T(8,128)(2,1)S(1)}, bf16[304,256]{1,0:T(8,128)(2,1)S(1)}, u32[]{:S(2)}, u32[]{:S(2)}) collective-permute-start(bf16[304,256]{1,0:T(8,128)(2,1)S(1)} %get-tuple-element.37), channel_id=1, source_target_pairs={{0,16},{4,20},{8,24},{12,28},{16,0},{20,4},{24,8},{28,12},{1,17},{... | collective-permute-start | bytes 466952 | tf_op jit(solution)/shard_map/ppermute | solution.py:186
  54.9 8.0 %collective-permute-start.16 = (bf16[304,256]{1,0:T(8,128)(2,1)S(1)}, bf16[304,256]{1,0:T(8,128)(2,1)S(1)}, u32[]{:S(2)}, u32[]{:S(2)}) collective-permute-start(bf16[304,256]{1,0:T(8,128)(2,1)S(1)} %get-tuple-element.38), channel_id=1, source_target_pairs={{0,24},{4,28},{8,16},{12,20},{16,8},{20,12},{24,0},{28,4},{1,25},{... | collective-permute-start | bytes 466952 | tf_op jit(solution)/shard_map/ppermute | solution.py:186
  63.5 6.0 %collective-permute-start.19 = (bf16[288,256]{1,0:T(8,128)(2,1)S(1)}, bf16[288,256]{1,0:T(8,128)(2,1)S(1)}, u32[]{:S(2)}, u32[]{:S(2)}) collective-permute-start(bf16[288,256]{1,0:T(8,128)(2,1)S(1)} %get-tuple-element.39.refs_0_), channel_id=1, source_target_pairs={{0,3},{1,2},{2,1},{3,0},{4,7},{5,6},{6,5},{7,4},{8,11},{9,10},{10,... | collective-permute-start | bytes 442376 | tf_op jit(solution)/shard_map/ppermute | solution.py:186
  65.1 13.7 %collective-permute-start.18 = (bf16[288,256]{1,0:T(8,128)(2,1)S(1)}, bf16[288,256]{1,0:T(8,128)(2,1)S(1)}, u32[]{:S(2)}, u32[]{:S(2)}) collective-permute-start(bf16[288,256]{1,0:T(8,128)(2,1)S(1)} %get-tuple-element.39.refs_0_), channel_id=1, source_target_pairs={{0,2},{1,3},{2,0},{3,1},{4,6},{5,7},{6,4},{7,5},{8,10},{9,11},{10,... | collective-permute-start | bytes 442376 | tf_op jit(solution)/shard_map/ppermute | solution.py:186
  66.0 12.9 %collective-permute-start.17 = (bf16[288,256]{1,0:T(8,128)(2,1)S(1)}, bf16[288,256]{1,0:T(8,128)(2,1)S(1)}, u32[]{:S(2)}, u32[]{:S(2)}) collective-permute-start(bf16[288,256]{1,0:T(8,128)(2,1)S(1)} %get-tuple-element.39.refs_0_), channel_id=1, source_target_pairs={{0,1},{1,0},{2,3},{3,2},{4,5},{5,4},{6,7},{7,6},{8,9},{9,8},{10,11... | collective-permute-start | bytes 442376 | tf_op jit(solution)/shard_map/ppermute | solution.py:186
  78.9 5.0 %collective-permute-start.23 = (bf16[288,256]{1,0:T(8,128)(2,1)S(1)}, bf16[288,256]{1,0:T(8,128)(2,1)S(1)}, u32[]{:S(2)}, u32[]{:S(2)}) collective-permute-start(bf16[288,256]{1,0:T(8,128)(2,1)S(1)} %shard_map.101.refs_0_), channel_id=1, source_target_pairs={{0,16},{4,20},{8,24},{12,28},{16,0},{20,4},{24,8},{28,12},{1,17},{... | collective-permute-start | bytes 442376 | tf_op jit(solution)/shard_map/ppermute | solution.py:186
  79.4 7.5 %collective-permute-start.22 = (bf16[288,256]{1,0:T(8,128)(2,1)S(1)}, bf16[288,256]{1,0:T(8,128)(2,1)S(1)}, u32[]{:S(2)}, u32[]{:S(2)}) collective-permute-start(bf16[288,256]{1,0:T(8,128)(2,1)S(1)} %shard_map.101.refs_0_), channel_id=1, source_target_pairs={{0,8},{4,12},{8,0},{12,4},{16,24},{20,28},{24,16},{28,20},{1,9},{5... | collective-permute-start | bytes 442376 | tf_op jit(solution)/shard_map/ppermute | solution.py:186
  80.5 6.7 %collective-permute-start.20 = (bf16[288,256]{1,0:T(8,128)(2,1)S(1)}, bf16[288,256]{1,0:T(8,128)(2,1)S(1)}, u32[]{:S(2)}, u32[]{:S(2)}) collective-permute-start(bf16[288,256]{1,0:T(8,128)(2,1)S(1)} %shard_map.101.refs_0_), channel_id=1, source_target_pairs={{0,24},{4,28},{8,16},{12,20},{16,8},{20,12},{24,0},{28,4},{1,25},{... | collective-permute-start | bytes 442376 | tf_op jit(solution)/shard_map/ppermute | solution.py:186
  81.7 8.0 %collective-permute-start.24 = (bf16[288,256]{1,0:T(8,128)(2,1)S(1)}, bf16[288,256]{1,0:T(8,128)(2,1)S(1)}, u32[]{:S(2)}, u32[]{:S(2)}) collective-permute-start(bf16[288,256]{1,0:T(8,128)(2,1)S(1)} %shard_map.101.refs_0_), channel_id=1, source_target_pairs={{0,4},{4,0},{8,12},{12,8},{16,20},{20,16},{24,28},{28,24},{1,5},{5... | collective-permute-start | bytes 442376 | tf_op jit(solution)/shard_map/ppermute | solution.py:186
  83.9 5.7 %collective-permute-start.26 = (bf16[288,256]{1,0:T(8,128)(2,1)S(1)}, bf16[288,256]{1,0:T(8,128)(2,1)S(1)}, u32[]{:S(2)}, u32[]{:S(2)}) collective-permute-start(bf16[288,256]{1,0:T(8,128)(2,1)S(1)} %collective-permute-done.23.refs_2_), channel_id=1, source_target_pairs={{0,4},{4,0},{8,12},{12,8},{16,20},{20,16},{24,28},{28,24},{1,5},{5... | collective-permute-start | bytes 442376 | tf_op jit(solution)/shard_map/ppermute | solution.py:186
  86.8 2.8 %collective-permute-start.25 = (bf16[288,256]{1,0:T(8,128)(2,1)S(1)}, bf16[288,256]{1,0:T(8,128)(2,1)S(1)}, u32[]{:S(2)}, u32[]{:S(2)}) collective-permute-start(bf16[288,256]{1,0:T(8,128)(2,1)S(1)} %collective-permute-done.22.refs_1_), channel_id=1, source_target_pairs={{0,4},{4,0},{8,12},{12,8},{16,20},{20,16},{24,28},{28,24},{1,5},{5... | collective-permute-start | bytes 442376 | tf_op jit(solution)/shard_map/ppermute | solution.py:186
  87.2 4.3 %collective-permute-start.21 = (bf16[288,256]{1,0:T(8,128)(2,1)S(1)}, bf16[288,256]{1,0:T(8,128)(2,1)S(1)}, u32[]{:S(2)}, u32[]{:S(2)}) collective-permute-start(bf16[288,256]{1,0:T(8,128)(2,1)S(1)} %collective-permute-done.20.refs_0_), channel_id=1, source_target_pairs={{0,4},{4,0},{8,12},{12,8},{16,20},{20,16},{24,28},{28,24},{1,5},{5... | collective-permute-start | bytes 442376 | tf_op jit(solution)/shard_map/ppermute | solution.py:186
  (17 other events, 13.1 us)

commit v3 on v2

v3 whole, which is shorter than its diff:
```python
import functools

import jax
import jax.numpy as jnp
from jax import lax
from jax.experimental import pallas as pl
from jax.experimental.pallas import tpu as pltpu
from jax.sharding import PartitionSpec as P

BF = jnp.bfloat16
F32 = jnp.float32
TAIL = 16
ANY = pl.BlockSpec(memory_space=pl.ANY)
SMEM = pl.BlockSpec(memory_space=pltpu.SMEM)
VMEM = pl.BlockSpec(memory_space=pltpu.VMEM)


def shape(dims, dtype):
    return jax.ShapeDtypeStruct(dims, dtype)


def call(body, out, specs, *args, scratch=(), flops=0, moved=0, out_specs=None):
    return pl.pallas_call(
        body,
        out_shape=out,
        in_specs=list(specs),
        out_specs=out_specs or jax.tree.map(lambda _: VMEM, out),
        scratch_shapes=list(scratch),
        compiler_params=pltpu.CompilerParams(vmem_limit_bytes=24 * 2**20),
        cost_estimate=pl.CostEstimate(flops=flops, bytes_accessed=moved, transcendentals=0),
    )(*args)


def assemble(band_rows, list_ref, count_ref, values_ref, dense_ref, zero_ref):
    zero_ref[...] = jnp.zeros_like(zero_ref)
    slots = values_ref.shape[0] // count_ref.shape[0]
    size = values_ref.shape[1]
    across = dense_ref.shape[1] // size
    dense_ref[...] = jnp.zeros_like(dense_ref)

    def place(at, carry):
        relation = lax.div(at, slots)

        @pl.when(lax.rem(at, slots) < count_ref[relation])
        def _():
            k = list_ref[relation, lax.rem(at, slots)]
            row = pl.multiple_of(relation * band_rows + lax.div(k, across) * size, size)
            column = pl.multiple_of(lax.rem(k, across) * size, size)
            dense_ref[pl.ds(row, size), pl.ds(column, size)] = values_ref[at]

        return carry

    lax.fori_loop(0, values_ref.shape[0], place, 0)


def collect(here, pieces, features):
    rows = pieces[0].shape[0]
    for k, piece in enumerate(pieces):
        features[pl.ds(pl.multiple_of((here ^ k) * rows, 16), rows)] = piece[...]


def forward_near(count, dense_ref, *refs):
    pieces, (total_ref, features) = refs[:count], refs[count:]
    me = lax.axis_index("dst")
    collect(lax.rem(me, count), pieces, features)
    depth = features.shape[0]
    columns = pl.ds(pl.multiple_of(lax.div(me, count) * depth, 128), depth)
    step = 384
    for i in range(0, total_ref.shape[0], step):
        total_ref[i : i + step] = jnp.dot(
            dense_ref[i : i + step, columns], features[...], preferred_element_type=F32
        )


def forward(count, dense_ref, weight_ref, total_ref, *refs):
    pieces, (tile_ref, own_ref, *sends, features, message) = refs[:count], refs[count:]
    me = lax.axis_index("dst")
    collect(lax.rem(me, count), pieces, features)
    depth, width = features.shape
    columns = pl.ds(pl.multiple_of((1 - lax.div(me, count)) * depth, 128), depth)
    band_rows = tile_ref.shape[0]
    step = 128
    for i in range(0, band_rows, step):
        for r in range(dense_ref.shape[0] // band_rows):
            at = slice(r * band_rows + i, r * band_rows + i + step)
            part = jnp.dot(
                dense_ref[at, columns], features[...], preferred_element_type=F32
            )
            tile_ref[i : i + step, r * width : (r + 1) * width] = (total_ref[at] + part).astype(BF)
    message[...] = jnp.dot(tile_ref[...], weight_ref[...], preferred_element_type=F32)
    block = own_ref.shape[0]
    z = lax.axis_index("src")
    for m in range(len(sends) + 1):
        mine = message[pl.ds(pl.multiple_of((z ^ m) * block, 16), block)]
        if m == 0:
            own_ref[...] = mine
        else:
            sends[m - 1][...] = mine.astype(BF)


def transpose(tile_ref, pre_ref, out_ref, output_ref):
    pre = pre_ref[...]
    output_ref[...] = (pre * jax.nn.sigmoid(pre)).astype(BF)
    step = 256
    for at in range(0, tile_ref.shape[1], step):
        out_ref[at : at + step] = tile_ref[:, at : at + step].T


def activate(bias_ref, cotangent_ref, own_ref, *refs):
    *others, pre_ref, grad_ref = refs
    pre = own_ref[...]
    for other in others:
        pre = pre + other[...].astype(F32)
    pre = pre + bias_ref[...].astype(F32)
    sigma = jax.nn.sigmoid(pre)
    pre_ref[...] = pre
    grad_ref[...] = (
        cotangent_ref[...].astype(F32) * sigma * (1.0 + pre * (1.0 - sigma))
    ).astype(BF)


def split_row(row):
    at = lax.broadcasted_iota(jnp.int32, (TAIL, row.shape[1]), 0)
    high = row.astype(BF).astype(F32)
    return jnp.where(at == 0, high, jnp.where(at == 1, row - high, 0.0)).astype(BF)


def join_row(tail):
    return jnp.sum(tail.astype(F32), axis=0, keepdims=True)


def backward(chips, tile_ref, *refs):
    *grads, keep_ref, send_ref, bias_ref, grad = refs
    z, me = lax.axis_index("src"), lax.axis_index("dst")
    block = grads[0].shape[0]
    for m, piece in enumerate(grads):
        grad[pl.ds(pl.multiple_of((z ^ m) * block, 16), block)] = piece[...]
    piece = keep_ref.shape[0] // chips
    half = tile_ref.shape[0] // 2
    bias = jnp.sum(grad[...].astype(F32), axis=0, keepdims=True)
    tail = split_row(bias)
    bias_ref[...] = jnp.broadcast_to(join_row(tail), bias_ref.shape)
    send_ref[pl.ds(piece * chips, TAIL)] = tail
    for ref, core in ((send_ref, 1 - lax.rem(me, 2)), (keep_ref, lax.rem(me, 2))):
        for m in range(chips):
            start = pl.multiple_of(core * half + (lax.div(me, 2) ^ m) * piece, 16)
            ref[m * piece : (m + 1) * piece] = jnp.dot(
                tile_ref[pl.ds(start, piece)], grad[...], preferred_element_type=F32
            ).astype(ref.dtype)


def add_cores(chips, keep_ref, bias_ref, received_ref, own_ref, total_ref, *sends):
    piece = own_ref.shape[0]
    tail = split_row(bias_ref[0:1] + join_row(received_ref[pl.ds(piece * chips, TAIL)]))
    total_ref[...] = jnp.broadcast_to(join_row(tail), total_ref.shape)
    for m in range(chips):
        at = pl.ds(m * piece, piece)
        both = keep_ref[at] + received_ref[at].astype(F32)
        if m == 0:
            own_ref[...] = both
        else:
            sends[m - 1][0:piece] = both.astype(BF)
            sends[m - 1][piece : piece + TAIL] = tail


def tree(terms):
    while len(terms) > 1:
        terms = [a + b for a, b in zip(terms[::2], terms[1::2])]
    return terms[0]


def add_chips(own_ref, bias_ref, *refs):
    *received, sum_ref, total_ref = refs
    piece = own_ref.shape[0]
    tails = [join_row(other[pl.ds(piece, TAIL)]) for other in received]
    total_ref[...] = jnp.broadcast_to(tree([bias_ref[0:1]] + tails), total_ref.shape)
    parts = [other[0:piece].astype(F32) for other in received]
    sum_ref[...] = tree([own_ref[...]] + parts).astype(BF)


def add_bands(*refs):
    *parts, out_ref = refs
    out_ref[...] = tree([part[...].astype(F32) for part in parts]).astype(BF)


def spread(bias_ref, *refs):
    me = lax.axis_index("dst")
    *chunks, out_ref, row_ref, wide, sems = refs
    row_ref[...] = bias_ref[0:1]
    rows = chunks[0].shape[0]
    half = out_ref.shape[0] // 2
    chips = len(chunks) // 2
    copies = []
    for i, chunk in enumerate(chunks):
        wide[i] = chunk[...].astype(F32)
        start = (lax.rem(me, 2) ^ (i // chips)) * half + (lax.div(me, 2) ^ (i % chips)) * rows
        target = out_ref.at[pl.ds(pl.multiple_of(start, 16), rows)]
        copies.append(pltpu.make_async_copy(wide.at[i], target, sems.at[i]))
        copies[-1].start()
    for copy in copies:
        copy.wait()


def swap(x, axis, n, mask):
    return lax.ppermute(x, axis, [(i, i ^ mask) for i in range(n)])


def on_device(features, relation_weight, bias, block_values, block_list, block_count, cotangent):
    n_dst, n_src = lax.axis_size("dst"), lax.axis_size("src")
    own_rows, width = features.shape
    relations, hidden = relation_weight.shape[1:]
    block_size = block_values.shape[5]
    tile_columns = own_rows * n_dst
    block = cotangent.shape[0]
    band_rows = block * n_src
    few = n_dst == 8 and n_src == 4 and (relations * width) % (8 * 16) == 0
    weight = relation_weight.transpose(1, 0, 2).reshape(relations * width, hidden)
    dense, zero = call(
        functools.partial(assemble, band_rows),
        [shape((relations * band_rows, tile_columns), BF), shape(features.shape, BF)],
        (SMEM, SMEM, VMEM),
        block_list.reshape(relations, -1),
        block_count.reshape(-1),
        block_values.reshape(-1, block_size, block_size),
        flops=10**8,
        moved=4 * 2**20,
    )
    if few:
        return few_devices(features, weight, bias, dense, zero, cotangent, relations)
    gathered = lax.all_gather(features, "dst", axis=0, tiled=True)
    tile = jnp.dot(dense, gathered, preferred_element_type=F32).astype(BF)
    tile = tile.reshape(relations, band_rows, width)
    partial = jnp.einsum(
        "rnd,rdh->nh",
        tile,
        weight.reshape(relations, width, hidden),
        preferred_element_type=F32,
    )
    pre = lax.psum_scatter(partial, "src", scatter_dimension=0, tiled=True)
    pre = pre + bias.astype(F32)
    sigma = jax.nn.sigmoid(pre)
    output = (pre * sigma).astype(BF)
    grad = (cotangent.astype(F32) * sigma * (1.0 + pre * (1.0 - sigma))).astype(BF)
    band_grad = lax.all_gather(grad, "src", axis=0, tiled=True)
    weight_term = jnp.einsum("rnd,nh->rdh", tile, band_grad, preferred_element_type=F32)
    weight_grad, bias_grad = lax.psum(
        (weight_term, jnp.sum(grad.astype(F32), axis=0)), ("dst", "src")
    )
    return output, weight_grad.transpose(1, 0, 2), bias_grad


def few_devices(features, weight, bias, dense, zero, cotangent, relations):
    n_dst, n_src = lax.axis_size("dst"), lax.axis_size("src")
    chips = n_dst // 2
    own_rows, width = features.shape
    block, hidden = cotangent.shape
    band_rows = block * n_src
    total_rows = weight.shape[0]
    piece = total_rows // n_dst
    half = n_dst // 2

    def over_chips(x, m):
        return swap(x, "dst", n_dst, 2 * m)

    def over_core(x):
        return swap(x, "dst", n_dst, 1)

    def over_src(x, m):
        return swap(x, "src", n_src, m)

    near = [features] + [over_chips(features, m) for m in range(1, chips)]
    near[1] = near[1] + zero
    far = [over_core(x) for x in near]
    pieces = [x for pair in zip(near, far) for x in pair]
    total = call(
        functools.partial(forward_near, half),
        shape((relations * band_rows, width), F32),
        [VMEM] * (1 + half),
        dense,
        *pieces[:half],
        scratch=[pltpu.VMEM((own_rows * half, width), BF)],
        flops=10**9,
        moved=2**20,
    )
    tile, own, *sends = call(
        functools.partial(forward, half),
        [shape((band_rows, relations * width), BF), shape((block, hidden), F32)]
        + [shape((block, hidden), BF)] * (n_src - 1),
        [VMEM] * (3 + half),
        dense,
        weight,
        total,
        *pieces[half:],
        scratch=[
            pltpu.VMEM((own_rows * half, width), BF),
            pltpu.VMEM((band_rows, hidden), F32),
        ],
        flops=10**9,
        moved=2**20,
    )
    received = [over_src(x, m + 1) for m, x in enumerate(sends)]
    pre, grad = call(
        activate,
        [shape((block, hidden), F32), shape((block, hidden), BF)],
        [VMEM] * (2 + n_src),
        bias.reshape(1, hidden),
        cotangent,
        own,
        *received,
    )
    turned, output = call(
        transpose,
        [shape((total_rows, band_rows), BF), shape((block, hidden), BF)],
        [VMEM] * 2,
        tile,
        pre,
        flops=10**8,
        moved=4 * 2**20,
    )
    keep, send, bias_part = call(
        functools.partial(backward, chips),
        [
            shape((piece * chips, hidden), F32),
            shape((piece * chips + TAIL, hidden), BF),
            shape((8, hidden), F32),
        ],
        [VMEM] * (1 + n_src),
        turned,
        grad,
        *[over_src(grad, m) for m in range(1, n_src)],
        scratch=[pltpu.VMEM((band_rows, hidden), BF)],
    )
    own, bias_part, *sends = call(
        functools.partial(add_cores, chips),
        [shape((piece, hidden), F32), shape((8, hidden), F32)]
        + [shape((piece + TAIL, hidden), BF)] * (chips - 1),
        [VMEM] * 3,
        keep,
        bias_part,
        over_core(send),
    )
    received = [over_chips(x, m + 1) for m, x in enumerate(sends)]
    part, bias_grad = call(
        add_chips,
        [shape((piece, hidden), BF), shape((8, hidden), F32)],
        [VMEM] * (1 + chips),
        own,
        bias_part,
        *received,
    )
    parts = [part] + [over_src(part, m) for m in range(1, n_src)]
    chunk = call(add_bands, shape((piece, hidden), BF), [VMEM] * n_src, *parts)
    near = [chunk] + [over_chips(chunk, m) for m in range(1, chips)]
    far = [over_core(x) for x in near]
    weight_grad, bias_grad = call(
        spread,
        [shape((total_rows, hidden), F32), shape((1, hidden), F32)],
        [VMEM] * (1 + n_dst),
        bias_grad,
        *near,
        *far,
        scratch=[pltpu.VMEM((n_dst, piece, hidden), F32), pltpu.SemaphoreType.DMA((n_dst,))],
        out_specs=[ANY, VMEM],
    )
    weight_grad = weight_grad.reshape(relations, width, hidden).transpose(1, 0, 2)
    return output, weight_grad, bias_grad.reshape(hidden)


def solution(mesh):
    in_specs = (
        P(("src", "dst"), None),
        P(),
        P(),
        P("dst", "src", None, None, None, None),
        P("dst", "src", None, None),
        P("dst", "src", None),
        P(("dst", "src"), None),
    )
    out_specs = (P(("dst", "src"), None), P(), P())
    return jax.shard_map(
        on_device, mesh=mesh, in_specs=in_specs, out_specs=out_specs, check_vma=False
    )
```

time: 93.3 us -> 73 us (0.78)
  local copies, waits for them, and re-layouts: 18.3 us -> 2.76 us
  waiting for transfers between devices: 27.6 us -> 24.4 us
  Pallas kernels: 11.7 us -> 8.98 us
    unnamed x45 -> x13, local copies, waits for them, and re-layouts: 18.2 us -> 2.76 us
    ppermute x27, waiting for transfers between devices: 27.6 us -> 24.4 us  [swap(): return lax.ppermute(x, axis, [(i, i ^ mask) for i in range(n)])]
    pallas_call x10, Pallas kernels: 11.7 us -> 8.98 us  [call(): pl.pallas_call(body, out_shape=out, in_specs=list(specs), out_specs=out_s...]
  transfers between devices with their start and end apart: 27 -> 27, of which waited for: 10 -> 11; matrix products, arithmetic and copies ran while one was open for 1% -> 1% of each run, Pallas kernels for 4% -> 6%
where the time goes in v3:
time: 73 us; the launch traced here: 72.2 us
  starting transfers between devices  35.2 us (48%)
  waiting for transfers between devices  24.4 us (33%)
  Pallas kernels  8.98 us (12%)
  local copies, waits for them, and re-layouts  2.76 us (4%)
  between operations  0.81 us (1%)
    ppermute x27, starting transfers between devices, swap(): return lax.ppermute(x, axis, [(i, i ^ mask) for i in range(n)])  35.2 us
    ppermute x27, waiting for transfers between devices, swap(): return lax.ppermute(x, axis, [(i, i ^ mask) for i in range(n)])  24.4 us
    pallas_call x10, Pallas kernels, call(): pl.pallas_call(body, out_shape=out, in_specs=list(specs), out_specs=out_s...  8.98 us
    unnamed x13, local copies, waits for them, and re-layouts  2.76 us
  transfers between devices with their start and end apart: 27, of which 11 were waited for; matrix products, arithmetic and copies ran while one was open for 1% of the time, Pallas kernels for 6%

profile of v3, /device:TPU:1, one launch (start us, length us, event | category | flops | bytes accessed | tf_op | source)
XLA Modules:
  0.0 72.2 jit_solution(9178658584993716719)
XLA Ops:
  0.6 2.1 %collective-permute-start.1 = (bf16[96,768]{1,0:T(8,128)(2,1)}, bf16[96,768]{1,0:T(8,128)(2,1)S(1)}, u32[]{:S(2)}, u32[]{:S(2)}) collective-permute-start(bf16[96,768]{1,0:T(8,128)(2,1)} %refs_0_.1), channel_id=1, source_target_pairs={{0,8},{4,12},{8,0},{12,4},{16,24},{20,28},{24,16},{28,20},{1,9},{5... | collective-permute-start | bytes 442376 | tf_op jit(solution)/shard_map/ppermute | solution.py:205
  2.7 1.2 %collective-permute-start.3 = (bf16[96,768]{1,0:T(8,128)(2,1)}, bf16[96,768]{1,0:T(8,128)(2,1)S(1)}, u32[]{:S(2)}, u32[]{:S(2)}) collective-permute-start(bf16[96,768]{1,0:T(8,128)(2,1)} %refs_0_.1), channel_id=1, source_target_pairs={{0,16},{4,20},{8,24},{12,28},{16,0},{20,4},{24,8},{28,12},{1,17},{... | collective-permute-start | bytes 442376 | tf_op jit(solution)/shard_map/ppermute | solution.py:205
  4.0 1.2 %collective-permute-start = (bf16[96,768]{1,0:T(8,128)(2,1)}, bf16[96,768]{1,0:T(8,128)(2,1)S(1)}, u32[]{:S(2)}, u32[]{:S(2)}) collective-permute-start(bf16[96,768]{1,0:T(8,128)(2,1)} %refs_0_.1), channel_id=1, source_target_pairs={{0,4},{4,0},{8,12},{12,8},{16,20},{20,16},{24,28},{28,24},{1,5},{5... | collective-permute-start | bytes 442376 | tf_op jit(solution)/shard_map/ppermute | solution.py:205
  5.9 1.4 %copy-done = bf16[1,1,3,16,128,128]{5,4,3,2,1,0:T(8,128)(2,1)S(1)} copy-done((bf16[1,1,3,16,128,128]{5,4,3,2,1,0:T(8,128)(2,1)S(1)}, bf16[1,1,3,16,128,128]{5,4,3,2,1,0:T(8,128)(2,1)}, u32[]{:S(2)}) %copy-start) | copy-done | bytes 1572888
  8.0 1.9 %shard_map.94 = (bf16[1152,768]{1,0:T(8,128)(2,1)S(1)}, bf16[96,768]{1,0:T(8,128)(2,1)S(1)}) custom-call(s32[3,16]{1,0:T(4,128)S(1)} %bitcast.14, s32[3]{0:T(128)S(1)} %bitcast.15, bf16[48,128,128]{2,1,0:T(8,128)(2,1)S(1)} %bitcast.12), custom_call_target="tpu_custom_call" | custom-call | flops 100000000 | bytes 4194304 | tf_op jit(solution)/shard_map/pallas_call | solution.py:23
  10.0 2.4 %collective-permute-start.4 = (bf16[96,768]{1,0:T(8,128)(2,1)S(1)}, bf16[96,768]{1,0:T(8,128)(2,1)S(1)}, u32[]{:S(2)}, u32[]{:S(2)}) collective-permute-start(bf16[96,768]{1,0:T(8,128)(2,1)S(1)} %collective-permute-done.3.refs_0_), channel_id=1, source_target_pairs={{0,4},{4,0},{8,12},{12,8},{16,20},{20,16},{24,28},{28,24},{1,5},{5... | collective-permute-start | bytes 442376 | tf_op jit(solution)/shard_map/ppermute | solution.py:205
  12.4 1.1 %shard_map.95.total_ref = f32[1152,768]{1,0:T(8,128)S(1)} custom-call(bf16[1152,768]{1,0:T(8,128)(2,1)S(1)} %get-tuple-element.26.dense_ref, bf16[96,768]{1,0:T(8,128)(2,1)S(1)} %copy-done.2, bf16[96,768]{1,0:T(8,128)(2,1)S(1)} %collective-permute-done.refs_1_, bf16[96,768]{1,0:T(8,128)(2,1)S(1)} %add.3.refs_2_, ...), custom_call_target="tpu_custom_call" | custom-call | flops 1000000000 | bytes 1048576 | tf_op jit(solution)/shard_map/pallas_call | solution.py:23
  13.8 1.8 %shard_map.96 = (bf16[384,2304]{1,0:T(8,128)(2,1)S(1)}, f32[96,256]{1,0:T(8,128)S(1)}, bf16[96,256]{1,0:T(8,128)(2,1)S(1)}, bf16[96,256]{1,0:T(8,128)(2,1)S(1)}, bf16[96,256]{1,0:T(8,128)(2,1)S(1)}) custom-call(bf16[1152,768]{1,0:T(8,128)(2,1)S(1)} %get-tuple-element.26.dense_ref, bf16[2304,256]{1,0:T(8,128)(2,1)S(1)} %bitcast.13, ...), custom_call_target="tpu_custom_call" | custom-call | flops 1000000000 | bytes 1048576 | tf_op jit(solution)/shard_map/pallas_call | solution.py:23
  15.5 1.4 %collective-permute-start.7 = (bf16[96,256]{1,0:T(8,128)(2,1)S(1)}, bf16[96,256]{1,0:T(8,128)(2,1)S(1)}, u32[]{:S(2)}, u32[]{:S(2)}) collective-permute-start(bf16[96,256]{1,0:T(8,128)(2,1)S(1)} %get-tuple-element.30), channel_id=1, source_target_pairs={{0,1},{1,0},{2,3},{3,2},{4,5},{5,4},{6,7},{7,6},{8,9},{9,8},{10,11... | collective-permute-start | bytes 147464 | tf_op jit(solution)/shard_map/ppermute | solution.py:205
  16.9 2.3 %collective-permute-start.8 = (bf16[96,256]{1,0:T(8,128)(2,1)S(1)}, bf16[96,256]{1,0:T(8,128)(2,1)S(1)}, u32[]{:S(2)}, u32[]{:S(2)}) collective-permute-start(bf16[96,256]{1,0:T(8,128)(2,1)S(1)} %get-tuple-element.31), channel_id=1, source_target_pairs={{0,2},{1,3},{2,0},{3,1},{4,6},{5,7},{6,4},{7,5},{8,10},{9,11},{10,... | collective-permute-start | bytes 147464 | tf_op jit(solution)/shard_map/ppermute | solution.py:205
  19.2 2.0 %collective-permute-done.8.refs_1_ = bf16[96,256]{1,0:T(8,128)(2,1)S(1)} collective-permute-done((bf16[96,256]{1,0:T(8,128)(2,1)S(1)}, bf16[96,256]{1,0:T(8,128)(2,1)S(1)}, u32[]{:S(2)}, u32[]{:S(2)}) %collective-permute-start.8) | collective-permute-done | bytes 49184 | tf_op jit(solution)/shard_map/ppermute | solution.py:205
  21.2 2.8 %collective-permute-done.9.refs_2_ = bf16[96,256]{1,0:T(8,128)(2,1)S(1)} collective-permute-done((bf16[96,256]{1,0:T(8,128)(2,1)S(1)}, bf16[96,256]{1,0:T(8,128)(2,1)S(1)}, u32[]{:S(2)}, u32[]{:S(2)}) %collective-permute-start.9) | collective-permute-done | bytes 49184 | tf_op jit(solution)/shard_map/ppermute | solution.py:205
  24.1 0.8 %collective-permute-start.11 = (bf16[96,256]{1,0:T(8,128)(2,1)S(1)}, bf16[96,256]{1,0:T(8,128)(2,1)S(1)}, u32[]{:S(2)}, u32[]{:S(2)}) collective-permute-start(bf16[96,256]{1,0:T(8,128)(2,1)S(1)} %get-tuple-element.36.refs_0_), channel_id=1, source_target_pairs={{0,2},{1,3},{2,0},{3,1},{4,6},{5,7},{6,4},{7,5},{8,10},{9,11},{10,... | collective-permute-start | bytes 147464 | tf_op jit(solution)/shard_map/ppermute | solution.py:205
  25.0 2.7 %collective-permute-start.12 = (bf16[96,256]{1,0:T(8,128)(2,1)S(1)}, bf16[96,256]{1,0:T(8,128)(2,1)S(1)}, u32[]{:S(2)}, u32[]{:S(2)}) collective-permute-start(bf16[96,256]{1,0:T(8,128)(2,1)S(1)} %get-tuple-element.36.refs_0_), channel_id=1, source_target_pairs={{0,3},{1,2},{2,1},{3,0},{4,7},{5,6},{6,5},{7,4},{8,11},{9,10},{10,... | collective-permute-start | bytes 147464 | tf_op jit(solution)/shard_map/ppermute | solution.py:205
  27.7 1.1 %shard_map.98 = (bf16[2304,384]{1,0:T(8,128)(2,1)S(1)}, bf16[96,256]{1,0:T(8,128)(2,1)}) custom-call(bf16[384,2304]{1,0:T(8,128)(2,1)S(1)} %get-tuple-element.28.tile_ref, f32[96,256]{1,0:T(8,128)S(1)} %get-tuple-element.33.pre_ref), custom_call_target="tpu_custom_call" | custom-call | flops 100000000 | bytes 4194304 | tf_op jit(solution)/shard_map/pallas_call | solution.py:23
  28.7 1.5 %collective-permute-done.12.refs_3_ = bf16[96,256]{1,0:T(8,128)(2,1)S(1)} collective-permute-done((bf16[96,256]{1,0:T(8,128)(2,1)S(1)}, bf16[96,256]{1,0:T(8,128)(2,1)S(1)}, u32[]{:S(2)}, u32[]{:S(2)}) %collective-permute-start.12) | collective-permute-done | bytes 49184 | tf_op jit(solution)/shard_map/ppermute | solution.py:205
  30.3 0.8 %shard_map.99 = (f32[1152,256]{1,0:T(8,128)S(1)}, bf16[1168,256]{1,0:T(8,128)(2,1)S(1)}, f32[8,256]{1,0:T(8,128)S(1)}) custom-call(bf16[2304,384]{1,0:T(8,128)(2,1)S(1)} %get-tuple-element.35.tile_ref, bf16[96,256]{1,0:T(8,128)(2,1)S(1)} %get-tuple-element.36.refs_0_, bf16[96,256]{1,0:T(8,128)(2,1)S(1)} %collective-permute-done.10.refs_1_, ...), custom_call_target="tpu_custom_call" | custom-call | tf_op jit(solution)/shard_map/pallas_call | solution.py:23
  31.1 3.4 %collective-permute-start.13 = (bf16[1168,256]{1,0:T(8,128)(2,1)S(1)}, bf16[1168,256]{1,0:T(8,128)(2,1)S(1)}, u32[]{:S(2)}, u32[]{:S(2)}) collective-permute-start(bf16[1168,256]{1,0:T(8,128)(2,1)S(1)} %get-tuple-element.39), channel_id=1, source_target_pairs={{0,4},{4,0},{8,12},{12,8},{16,20},{20,16},{24,28},{28,24},{1,5},{5... | collective-permute-start | bytes 1794056 | tf_op jit(solution)/shard_map/ppermute | solution.py:205
  34.5 1.6 %collective-permute-done.13.received_ref = bf16[1168,256]{1,0:T(8,128)(2,1)S(1)} collective-permute-done((bf16[1168,256]{1,0:T(8,128)(2,1)S(1)}, bf16[1168,256]{1,0:T(8,128)(2,1)S(1)}, u32[]{:S(2)}, u32[]{:S(2)}) %collective-permute-start.13) | collective-permute-done | bytes 598048 | tf_op jit(solution)/shard_map/ppermute | solution.py:205
  36.3 0.9 %collective-permute-start.14 = (bf16[304,256]{1,0:T(8,128)(2,1)S(1)}, bf16[304,256]{1,0:T(8,128)(2,1)S(1)}, u32[]{:S(2)}, u32[]{:S(2)}) collective-permute-start(bf16[304,256]{1,0:T(8,128)(2,1)S(1)} %get-tuple-element.42), channel_id=1, source_target_pairs={{0,8},{4,12},{8,0},{12,4},{16,24},{20,28},{24,16},{28,20},{1,9},{5... | collective-permute-start | bytes 466952 | tf_op jit(solution)/shard_map/ppermute | solution.py:205
  37.2 1.1 %collective-permute-start.15 = (bf16[304,256]{1,0:T(8,128)(2,1)S(1)}, bf16[304,256]{1,0:T(8,128)(2,1)S(1)}, u32[]{:S(2)}, u32[]{:S(2)}) collective-permute-start(bf16[304,256]{1,0:T(8,128)(2,1)S(1)} %get-tuple-element.43), channel_id=1, source_target_pairs={{0,16},{4,20},{8,24},{12,28},{16,0},{20,4},{24,8},{28,12},{1,17},{... | collective-permute-start | bytes 466952 | tf_op jit(solution)/shard_map/ppermute | solution.py:205
  39.0 2.6 %collective-permute-done.14.refs_0_ = bf16[304,256]{1,0:T(8,128)(2,1)S(1)} collective-permute-done((bf16[304,256]{1,0:T(8,128)(2,1)S(1)}, bf16[304,256]{1,0:T(8,128)(2,1)S(1)}, u32[]{:S(2)}, u32[]{:S(2)}) %collective-permute-start.14) | collective-permute-done | bytes 155680 | tf_op jit(solution)/shard_map/ppermute | solution.py:205
  42.1 3.7 %collective-permute-done.16.refs_2_ = bf16[304,256]{1,0:T(8,128)(2,1)S(1)} collective-permute-done((bf16[304,256]{1,0:T(8,128)(2,1)S(1)}, bf16[304,256]{1,0:T(8,128)(2,1)S(1)}, u32[]{:S(2)}, u32[]{:S(2)}) %collective-permute-start.16) | collective-permute-done | bytes 155680 | tf_op jit(solution)/shard_map/ppermute | solution.py:205
  46.0 2.8 %collective-permute-start.18 = (bf16[288,256]{1,0:T(8,128)(2,1)S(1)}, bf16[288,256]{1,0:T(8,128)(2,1)S(1)}, u32[]{:S(2)}, u32[]{:S(2)}) collective-permute-start(bf16[288,256]{1,0:T(8,128)(2,1)S(1)} %get-tuple-element.46.refs_0_), channel_id=1, source_target_pairs={{0,2},{1,3},{2,0},{3,1},{4,6},{5,7},{6,4},{7,5},{8,10},{9,11},{10,... | collective-permute-start | bytes 442376 | tf_op jit(solution)/shard_map/ppermute | solution.py:205
  49.5 2.3 %collective-permute-done.17.refs_1_ = bf16[288,256]{1,0:T(8,128)(2,1)S(1)} collective-permute-done((bf16[288,256]{1,0:T(8,128)(2,1)S(1)}, bf16[288,256]{1,0:T(8,128)(2,1)S(1)}, u32[]{:S(2)}, u32[]{:S(2)}) %collective-permute-start.17) | collective-permute-done | bytes 147488 | tf_op jit(solution)/shard_map/ppermute | solution.py:205
  51.9 6.0 %collective-permute-done.19.refs_3_ = bf16[288,256]{1,0:T(8,128)(2,1)S(1)} collective-permute-done((bf16[288,256]{1,0:T(8,128)(2,1)S(1)}, bf16[288,256]{1,0:T(8,128)(2,1)S(1)}, u32[]{:S(2)}, u32[]{:S(2)}) %collective-permute-start.19) | collective-permute-done | bytes 147488 | tf_op jit(solution)/shard_map/ppermute | solution.py:205
  58.1 2.6 %collective-permute-start.22 = (bf16[288,256]{1,0:T(8,128)(2,1)S(1)}, bf16[288,256]{1,0:T(8,128)(2,1)S(1)}, u32[]{:S(2)}, u32[]{:S(2)}) collective-permute-start(bf16[288,256]{1,0:T(8,128)(2,1)S(1)} %shard_map.102.refs_0_), channel_id=1, source_target_pairs={{0,24},{4,28},{8,16},{12,20},{16,8},{20,12},{24,0},{28,4},{1,25},{... | collective-permute-start | bytes 442376 | tf_op jit(solution)/shard_map/ppermute | solution.py:205
  60.7 4.5 %collective-permute-start.23 = (bf16[288,256]{1,0:T(8,128)(2,1)S(1)}, bf16[288,256]{1,0:T(8,128)(2,1)S(1)}, u32[]{:S(2)}, u32[]{:S(2)}) collective-permute-start(bf16[288,256]{1,0:T(8,128)(2,1)S(1)} %shard_map.102.refs_0_), channel_id=1, source_target_pairs={{0,4},{4,0},{8,12},{12,8},{16,20},{20,16},{24,28},{28,24},{1,5},{5... | collective-permute-start | bytes 442376 | tf_op jit(solution)/shard_map/ppermute | solution.py:205
  65.2 1.7 %collective-permute-start.24 = (bf16[288,256]{1,0:T(8,128)(2,1)S(1)}, bf16[288,256]{1,0:T(8,128)(2,1)S(1)}, u32[]{:S(2)}, u32[]{:S(2)}) collective-permute-start(bf16[288,256]{1,0:T(8,128)(2,1)S(1)} %collective-permute-done.20.refs_1_), channel_id=1, source_target_pairs={{0,4},{4,0},{8,12},{12,8},{16,20},{20,16},{24,28},{28,24},{1,5},{5... | collective-permute-start | bytes 442376 | tf_op jit(solution)/shard_map/ppermute | solution.py:205
  67.4 1.7 %collective-permute-start.26 = (bf16[288,256]{1,0:T(8,128)(2,1)S(1)}, bf16[288,256]{1,0:T(8,128)(2,1)S(1)}, u32[]{:S(2)}, u32[]{:S(2)}) collective-permute-start(bf16[288,256]{1,0:T(8,128)(2,1)S(1)} %collective-permute-done.22.refs_3_), channel_id=1, source_target_pairs={{0,4},{4,0},{8,12},{12,8},{16,20},{20,16},{24,28},{28,24},{1,5},{5... | collective-permute-start | bytes 442376 | tf_op jit(solution)/shard_map/ppermute | solution.py:205
  69.1 1.0 %collective-permute-done.26.refs_7_ = bf16[288,256]{1,0:T(8,128)(2,1)S(1)} collective-permute-done((bf16[288,256]{1,0:T(8,128)(2,1)S(1)}, bf16[288,256]{1,0:T(8,128)(2,1)S(1)}, u32[]{:S(2)}, u32[]{:S(2)}) %collective-permute-start.26) | collective-permute-done | bytes 147488 | tf_op jit(solution)/shard_map/ppermute | solution.py:205
  70.1 2.0 %shard_map.103 = (f32[2304,256]{1,0:T(8,128)}, f32[1,256]{1,0:T(1,128)}) custom-call(f32[8,256]{1,0:T(8,128)S(1)} %get-tuple-element.45.bias_ref, bf16[288,256]{1,0:T(8,128)(2,1)S(1)} %shard_map.102.refs_0_, bf16[288,256]{1,0:T(8,128)(2,1)S(1)} %collective-permute-done.20.refs_1_, bf16[288,256]{1,0:T(8,128)(2,1)S(1)} %collective-permute-done.21.refs_2_, ...), custom_call_target="tpu_custom_call" | custom-call | tf_op jit(solution)/shard_map/pallas_call | solution.py:23
  (47 shorter events, 4.8 us)
Async XLA Ops:
  0.6 9.2 %collective-permute-start.1 = (bf16[96,768]{1,0:T(8,128)(2,1)}, bf16[96,768]{1,0:T(8,128)(2,1)S(1)}, u32[]{:S(2)}, u32[]{:S(2)}) collective-permute-start(bf16[96,768]{1,0:T(8,128)(2,1)} %refs_0_.1), channel_id=1, source_target_pairs={{0,8},{4,12},{8,0},{12,4},{16,24},{20,28},{24,16},{28,20},{1,9},{5... | collective-permute-start | bytes 442376 | tf_op jit(solution)/shard_map/ppermute | solution.py:205
  2.7 7.2 %collective-permute-start.3 = (bf16[96,768]{1,0:T(8,128)(2,1)}, bf16[96,768]{1,0:T(8,128)(2,1)S(1)}, u32[]{:S(2)}, u32[]{:S(2)}) collective-permute-start(bf16[96,768]{1,0:T(8,128)(2,1)} %refs_0_.1), channel_id=1, source_target_pairs={{0,16},{4,20},{8,24},{12,28},{16,0},{20,4},{24,8},{28,12},{1,17},{... | collective-permute-start | bytes 442376 | tf_op jit(solution)/shard_map/ppermute | solution.py:205
  4.0 8.4 %collective-permute-start.5 = (bf16[96,768]{1,0:T(8,128)(2,1)}, bf16[96,768]{1,0:T(8,128)(2,1)S(1)}, u32[]{:S(2)}, u32[]{:S(2)}) collective-permute-start(bf16[96,768]{1,0:T(8,128)(2,1)} %refs_0_.1), channel_id=1, source_target_pairs={{0,24},{4,28},{8,16},{12,20},{16,8},{20,12},{24,0},{28,4},{1,25},{... | collective-permute-start | bytes 442376 | tf_op jit(solution)/shard_map/ppermute | solution.py:205
  4.0 8.4 %collective-permute-start = (bf16[96,768]{1,0:T(8,128)(2,1)}, bf16[96,768]{1,0:T(8,128)(2,1)S(1)}, u32[]{:S(2)}, u32[]{:S(2)}) collective-permute-start(bf16[96,768]{1,0:T(8,128)(2,1)} %refs_0_.1), channel_id=1, source_target_pairs={{0,4},{4,0},{8,12},{12,8},{16,20},{20,16},{24,28},{28,24},{1,5},{5... | collective-permute-start | bytes 442376 | tf_op jit(solution)/shard_map/ppermute | solution.py:205
  5.9 1.4 %copy-start = (bf16[1,1,3,16,128,128]{5,4,3,2,1,0:T(8,128)(2,1)S(1)}, bf16[1,1,3,16,128,128]{5,4,3,2,1,0:T(8,128)(2,1)}, u32[]{:S(2)}) copy-start(bf16[1,1,3,16,128,128]{5,4,3,2,1,0:T(8,128)(2,1)} %param.10) | copy-start | bytes 4718596
  8.0 4.4 %copy-start.2 = (bf16[96,768]{1,0:T(8,128)(2,1)S(1)}, bf16[96,768]{1,0:T(8,128)(2,1)}, u32[]{:S(2)}) copy-start(bf16[96,768]{1,0:T(8,128)(2,1)} %refs_0_.1) | copy-start | bytes 442372
  9.9 2.5 %collective-permute-start.2 = (bf16[96,768]{1,0:T(8,128)(2,1)S(1)}, bf16[96,768]{1,0:T(8,128)(2,1)S(1)}, u32[]{:S(2)}, u32[]{:S(2)}) collective-permute-start(bf16[96,768]{1,0:T(8,128)(2,1)S(1)} %add.3.refs_2_), channel_id=1, source_target_pairs={{0,4},{4,0},{8,12},{12,8},{16,20},{20,16},{24,28},{28,24},{1,5},{5... | collective-permute-start | bytes 442376 | tf_op jit(solution)/shard_map/ppermute | solution.py:205
  10.0 3.6 %collective-permute-start.4 = (bf16[96,768]{1,0:T(8,128)(2,1)S(1)}, bf16[96,768]{1,0:T(8,128)(2,1)S(1)}, u32[]{:S(2)}, u32[]{:S(2)}) collective-permute-start(bf16[96,768]{1,0:T(8,128)(2,1)S(1)} %collective-permute-done.3.refs_0_), channel_id=1, source_target_pairs={{0,4},{4,0},{8,12},{12,8},{16,20},{20,16},{24,28},{28,24},{1,5},{5... | collective-permute-start | bytes 442376 | tf_op jit(solution)/shard_map/ppermute | solution.py:205
  12.4 1.4 %collective-permute-start.6 = (bf16[96,768]{1,0:T(8,128)(2,1)S(1)}, bf16[96,768]{1,0:T(8,128)(2,1)S(1)}, u32[]{:S(2)}, u32[]{:S(2)}) collective-permute-start(bf16[96,768]{1,0:T(8,128)(2,1)S(1)} %collective-permute-done.5.refs_2_), channel_id=1, source_target_pairs={{0,4},{4,0},{8,12},{12,8},{16,20},{20,16},{24,28},{28,24},{1,5},{5... | collective-permute-start | bytes 442376 | tf_op jit(solution)/shard_map/ppermute | solution.py:205
  12.4 1.3 %copy-start.1 = (bf16[768,3,256]{2,0,1:T(8,128)(2,1)S(1)}, bf16[768,3,256]{2,0,1:T(8,128)(2,1)}, u32[]{:S(2)}) copy-start(bf16[768,3,256]{2,0,1:T(8,128)(2,1)} %param.8) | copy-start | bytes 3538948
  13.7 5.4 %copy-start.5 = (bf16[256]{0:T(256)(128)(2,1)S(1)}, bf16[256]{0:T(256)(128)(2,1)}, u32[]{:S(2)}) copy-start(bf16[256]{0:T(256)(128)(2,1)} %param.9) | copy-start | bytes 1540
  13.8 10.2 %copy-start.3 = (bf16[96,256]{1,0:T(8,128)(2,1)S(1)}, bf16[96,256]{1,0:T(8,128)(2,1)}, u32[]{:S(2)}) copy-start(bf16[96,256]{1,0:T(8,128)(2,1)} %cotangent_ref.1) | copy-start | bytes 147460
  15.5 3.7 %collective-permute-start.7 = (bf16[96,256]{1,0:T(8,128)(2,1)S(1)}, bf16[96,256]{1,0:T(8,128)(2,1)S(1)}, u32[]{:S(2)}, u32[]{:S(2)}) collective-permute-start(bf16[96,256]{1,0:T(8,128)(2,1)S(1)} %get-tuple-element.30), channel_id=1, source_target_pairs={{0,1},{1,0},{2,3},{3,2},{4,5},{5,4},{6,7},{7,6},{8,9},{9,8},{10,11... | collective-permute-start | bytes 147464 | tf_op jit(solution)/shard_map/ppermute | solution.py:205
  16.9 4.3 %collective-permute-start.8 = (bf16[96,256]{1,0:T(8,128)(2,1)S(1)}, bf16[96,256]{1,0:T(8,128)(2,1)S(1)}, u32[]{:S(2)}, u32[]{:S(2)}) collective-permute-start(bf16[96,256]{1,0:T(8,128)(2,1)S(1)} %get-tuple-element.31), channel_id=1, source_target_pairs={{0,2},{1,3},{2,0},{3,1},{4,6},{5,7},{6,4},{7,5},{8,10},{9,11},{10,... | collective-permute-start | bytes 147464 | tf_op jit(solution)/shard_map/ppermute | solution.py:205
  19.2 4.8 %collective-permute-start.9 = (bf16[96,256]{1,0:T(8,128)(2,1)S(1)}, bf16[96,256]{1,0:T(8,128)(2,1)S(1)}, u32[]{:S(2)}, u32[]{:S(2)}) collective-permute-start(bf16[96,256]{1,0:T(8,128)(2,1)S(1)} %get-tuple-element.32), channel_id=1, source_target_pairs={{0,3},{1,2},{2,1},{3,0},{4,7},{5,6},{6,5},{7,4},{8,11},{9,10},{10,... | collective-permute-start | bytes 147464 | tf_op jit(solution)/shard_map/ppermute | solution.py:205
  24.0 4.7 %collective-permute-start.10 = (bf16[96,256]{1,0:T(8,128)(2,1)S(1)}, bf16[96,256]{1,0:T(8,128)(2,1)S(1)}, u32[]{:S(2)}, u32[]{:S(2)}) collective-permute-start(bf16[96,256]{1,0:T(8,128)(2,1)S(1)} %get-tuple-element.36.refs_0_), channel_id=1, source_target_pairs={{0,1},{1,0},{2,3},{3,2},{4,5},{5,4},{6,7},{7,6},{8,9},{9,8},{10,11... | collective-permute-start | bytes 147464 | tf_op jit(solution)/shard_map/ppermute | solution.py:205
  24.1 4.6 %collective-permute-start.11 = (bf16[96,256]{1,0:T(8,128)(2,1)S(1)}, bf16[96,256]{1,0:T(8,128)(2,1)S(1)}, u32[]{:S(2)}, u32[]{:S(2)}) collective-permute-start(bf16[96,256]{1,0:T(8,128)(2,1)S(1)} %get-tuple-element.36.refs_0_), channel_id=1, source_target_pairs={{0,2},{1,3},{2,0},{3,1},{4,6},{5,7},{6,4},{7,5},{8,10},{9,11},{10,... | collective-permute-start | bytes 147464 | tf_op jit(solution)/shard_map/ppermute | solution.py:205
  25.0 5.3 %collective-permute-start.12 = (bf16[96,256]{1,0:T(8,128)(2,1)S(1)}, bf16[96,256]{1,0:T(8,128)(2,1)S(1)}, u32[]{:S(2)}, u32[]{:S(2)}) collective-permute-start(bf16[96,256]{1,0:T(8,128)(2,1)S(1)} %get-tuple-element.36.refs_0_), channel_id=1, source_target_pairs={{0,3},{1,2},{2,1},{3,0},{4,7},{5,6},{6,5},{7,4},{8,11},{9,10},{10,... | collective-permute-start | bytes 147464 | tf_op jit(solution)/shard_map/ppermute | solution.py:205
  31.1 5.0 %collective-permute-start.13 = (bf16[1168,256]{1,0:T(8,128)(2,1)S(1)}, bf16[1168,256]{1,0:T(8,128)(2,1)S(1)}, u32[]{:S(2)}, u32[]{:S(2)}) collective-permute-start(bf16[1168,256]{1,0:T(8,128)(2,1)S(1)} %get-tuple-element.39), channel_id=1, source_target_pairs={{0,4},{4,0},{8,12},{12,8},{16,20},{20,16},{24,28},{28,24},{1,5},{5... | collective-permute-start | bytes 1794056 | tf_op jit(solution)/shard_map/ppermute | solution.py:205
  36.3 5.3 %collective-permute-start.14 = (bf16[304,256]{1,0:T(8,128)(2,1)S(1)}, bf16[304,256]{1,0:T(8,128)(2,1)S(1)}, u32[]{:S(2)}, u32[]{:S(2)}) collective-permute-start(bf16[304,256]{1,0:T(8,128)(2,1)S(1)} %get-tuple-element.42), channel_id=1, source_target_pairs={{0,8},{4,12},{8,0},{12,4},{16,24},{20,28},{24,16},{28,20},{1,9},{5... | collective-permute-start | bytes 466952 | tf_op jit(solution)/shard_map/ppermute | solution.py:205
  37.2 4.9 %collective-permute-start.15 = (bf16[304,256]{1,0:T(8,128)(2,1)S(1)}, bf16[304,256]{1,0:T(8,128)(2,1)S(1)}, u32[]{:S(2)}, u32[]{:S(2)}) collective-permute-start(bf16[304,256]{1,0:T(8,128)(2,1)S(1)} %get-tuple-element.43), channel_id=1, source_target_pairs={{0,16},{4,20},{8,24},{12,28},{16,0},{20,4},{24,8},{28,12},{1,17},{... | collective-permute-start | bytes 466952 | tf_op jit(solution)/shard_map/ppermute | solution.py:205
  38.3 7.5 %collective-permute-start.16 = (bf16[304,256]{1,0:T(8,128)(2,1)S(1)}, bf16[304,256]{1,0:T(8,128)(2,1)S(1)}, u32[]{:S(2)}, u32[]{:S(2)}) collective-permute-start(bf16[304,256]{1,0:T(8,128)(2,1)S(1)} %get-tuple-element.44), channel_id=1, source_target_pairs={{0,24},{4,28},{8,16},{12,20},{16,8},{20,12},{24,0},{28,4},{1,25},{... | collective-permute-start | bytes 466952 | tf_op jit(solution)/shard_map/ppermute | solution.py:205
  45.9 6.0 %collective-permute-start.17 = (bf16[288,256]{1,0:T(8,128)(2,1)S(1)}, bf16[288,256]{1,0:T(8,128)(2,1)S(1)}, u32[]{:S(2)}, u32[]{:S(2)}) collective-permute-start(bf16[288,256]{1,0:T(8,128)(2,1)S(1)} %get-tuple-element.46.refs_0_), channel_id=1, source_target_pairs={{0,1},{1,0},{2,3},{3,2},{4,5},{5,4},{6,7},{7,6},{8,9},{9,8},{10,11... | collective-permute-start | bytes 442376 | tf_op jit(solution)/shard_map/ppermute | solution.py:205
  46.0 5.9 %collective-permute-start.18 = (bf16[288,256]{1,0:T(8,128)(2,1)S(1)}, bf16[288,256]{1,0:T(8,128)(2,1)S(1)}, u32[]{:S(2)}, u32[]{:S(2)}) collective-permute-start(bf16[288,256]{1,0:T(8,128)(2,1)S(1)} %get-tuple-element.46.refs_0_), channel_id=1, source_target_pairs={{0,2},{1,3},{2,0},{3,1},{4,6},{5,7},{6,4},{7,5},{8,10},{9,11},{10,... | collective-permute-start | bytes 442376 | tf_op jit(solution)/shard_map/ppermute | solution.py:205
  48.8 9.1 %collective-permute-start.19 = (bf16[288,256]{1,0:T(8,128)(2,1)S(1)}, bf16[288,256]{1,0:T(8,128)(2,1)S(1)}, u32[]{:S(2)}, u32[]{:S(2)}) collective-permute-start(bf16[288,256]{1,0:T(8,128)(2,1)S(1)} %get-tuple-element.46.refs_0_), channel_id=1, source_target_pairs={{0,3},{1,2},{2,1},{3,0},{4,7},{5,6},{6,5},{7,4},{8,11},{9,10},{10,... | collective-permute-start | bytes 442376 | tf_op jit(solution)/shard_map/ppermute | solution.py:205
  57.9 7.2 %collective-permute-start.20 = (bf16[288,256]{1,0:T(8,128)(2,1)S(1)}, bf16[288,256]{1,0:T(8,128)(2,1)S(1)}, u32[]{:S(2)}, u32[]{:S(2)}) collective-permute-start(bf16[288,256]{1,0:T(8,128)(2,1)S(1)} %shard_map.102.refs_0_), channel_id=1, source_target_pairs={{0,8},{4,12},{8,0},{12,4},{16,24},{20,28},{24,16},{28,20},{1,9},{5... | collective-permute-start | bytes 442376 | tf_op jit(solution)/shard_map/ppermute | solution.py:205
  58.0 8.8 %collective-permute-start.21 = (bf16[288,256]{1,0:T(8,128)(2,1)S(1)}, bf16[288,256]{1,0:T(8,128)(2,1)S(1)}, u32[]{:S(2)}, u32[]{:S(2)}) collective-permute-start(bf16[288,256]{1,0:T(8,128)(2,1)S(1)} %shard_map.102.refs_0_), channel_id=1, source_target_pairs={{0,16},{4,20},{8,24},{12,28},{16,0},{20,4},{24,8},{28,12},{1,17},{... | collective-permute-start | bytes 442376 | tf_op jit(solution)/shard_map/ppermute | solution.py:205
  58.1 9.3 %collective-permute-start.22 = (bf16[288,256]{1,0:T(8,128)(2,1)S(1)}, bf16[288,256]{1,0:T(8,128)(2,1)S(1)}, u32[]{:S(2)}, u32[]{:S(2)}) collective-permute-start(bf16[288,256]{1,0:T(8,128)(2,1)S(1)} %shard_map.102.refs_0_), channel_id=1, source_target_pairs={{0,24},{4,28},{8,16},{12,20},{16,8},{20,12},{24,0},{28,4},{1,25},{... | collective-permute-start | bytes 442376 | tf_op jit(solution)/shard_map/ppermute | solution.py:205
  60.7 8.5 %collective-permute-start.23 = (bf16[288,256]{1,0:T(8,128)(2,1)S(1)}, bf16[288,256]{1,0:T(8,128)(2,1)S(1)}, u32[]{:S(2)}, u32[]{:S(2)}) collective-permute-start(bf16[288,256]{1,0:T(8,128)(2,1)S(1)} %shard_map.102.refs_0_), channel_id=1, source_target_pairs={{0,4},{4,0},{8,12},{12,8},{16,20},{20,16},{24,28},{28,24},{1,5},{5... | collective-permute-start | bytes 442376 | tf_op jit(solution)/shard_map/ppermute | solution.py:205
  65.2 3.9 %collective-permute-start.24 = (bf16[288,256]{1,0:T(8,128)(2,1)S(1)}, bf16[288,256]{1,0:T(8,128)(2,1)S(1)}, u32[]{:S(2)}, u32[]{:S(2)}) collective-permute-start(bf16[288,256]{1,0:T(8,128)(2,1)S(1)} %collective-permute-done.20.refs_1_), channel_id=1, source_target_pairs={{0,4},{4,0},{8,12},{12,8},{16,20},{20,16},{24,28},{28,24},{1,5},{5... | collective-permute-start | bytes 442376 | tf_op jit(solution)/shard_map/ppermute | solution.py:205
  66.8 2.3 %collective-permute-start.25 = (bf16[288,256]{1,0:T(8,128)(2,1)S(1)}, bf16[288,256]{1,0:T(8,128)(2,1)S(1)}, u32[]{:S(2)}, u32[]{:S(2)}) collective-permute-start(bf16[288,256]{1,0:T(8,128)(2,1)S(1)} %collective-permute-done.21.refs_2_), channel_id=1, source_target_pairs={{0,4},{4,0},{8,12},{12,8},{16,20},{20,16},{24,28},{28,24},{1,5},{5... | collective-permute-start | bytes 442376 | tf_op jit(solution)/shard_map/ppermute | solution.py:205
  67.4 2.7 %collective-permute-start.26 = (bf16[288,256]{1,0:T(8,128)(2,1)S(1)}, bf16[288,256]{1,0:T(8,128)(2,1)S(1)}, u32[]{:S(2)}, u32[]{:S(2)}) collective-permute-start(bf16[288,256]{1,0:T(8,128)(2,1)S(1)} %collective-permute-done.22.refs_3_), channel_id=1, source_target_pairs={{0,4},{4,0},{8,12},{12,8},{16,20},{20,16},{24,28},{28,24},{1,5},{5... | collective-permute-start | bytes 442376 | tf_op jit(solution)/shard_map/ppermute | solution.py:205
  (1 other events, 0.7 us)

commit v4 on v3

v4 whole, which is shorter than its diff:
```python
import functools

import jax
import jax.numpy as jnp
from jax import lax
from jax.experimental import pallas as pl
from jax.experimental.pallas import tpu as pltpu
from jax.sharding import PartitionSpec as P

BF = jnp.bfloat16
F32 = jnp.float32
MESSAGE = (3, 2, 1)
GRAD = (1, 2, 3)
SUMS = (1, 2, 3)
CHUNKS = (1, 2, 3)
FIRST, REST = (1, 2), (3, 0)
FAR = (3, 2)
TAIL = 16
ANY = pl.BlockSpec(memory_space=pl.ANY)
SMEM = pl.BlockSpec(memory_space=pltpu.SMEM)
VMEM = pl.BlockSpec(memory_space=pltpu.VMEM)


def shape(dims, dtype):
    return jax.ShapeDtypeStruct(dims, dtype)


def call(body, out, specs, *args, scratch=(), flops=0, moved=0, out_specs=None, aliases=None):
    return pl.pallas_call(
        body,
        out_shape=out,
        in_specs=list(specs),
        out_specs=out_specs or jax.tree.map(lambda _: VMEM, out),
        scratch_shapes=list(scratch),
        input_output_aliases=aliases or {},
        compiler_params=pltpu.CompilerParams(vmem_limit_bytes=24 * 2**20),
        cost_estimate=pl.CostEstimate(flops=flops, bytes_accessed=moved, transcendentals=0),
    )(*args)


def assemble(band_rows, list_ref, count_ref, values_ref, dense_ref, zero_ref):
    zero_ref[...] = jnp.zeros_like(zero_ref)
    slots = values_ref.shape[0] // count_ref.shape[0]
    size = values_ref.shape[1]
    across = dense_ref.shape[1] // size
    dense_ref[...] = jnp.zeros_like(dense_ref)

    def place(at, carry):
        relation = lax.div(at, slots)

        @pl.when(lax.rem(at, slots) < count_ref[relation])
        def _():
            k = list_ref[relation, lax.rem(at, slots)]
            row = pl.multiple_of(relation * band_rows + lax.div(k, across) * size, size)
            column = pl.multiple_of(lax.rem(k, across) * size, size)
            dense_ref[pl.ds(row, size), pl.ds(column, size)] = values_ref[at]

        return carry

    lax.fori_loop(0, values_ref.shape[0], place, 0)


def collect(here, pieces, features):
    rows = pieces[0].shape[0]
    for k, piece in enumerate(pieces):
        features[pl.ds(pl.multiple_of((here ^ k) * rows, 16), rows)] = piece[...]


def half_message(dense_ref, weight_ref, features, half):
    depth, width = features.shape
    columns = pl.ds(pl.multiple_of(half * depth, 128), depth)
    relations = weight_ref.shape[0] // width
    rows = dense_ref.shape[0] // relations
    total = None
    for r in range(relations):
        projected = jnp.dot(
            features[...],
            weight_ref[r * width : (r + 1) * width],
            preferred_element_type=F32,
        ).astype(BF)
        term = jnp.dot(
            dense_ref[r * rows : (r + 1) * rows, columns],
            projected,
            preferred_element_type=F32,
        )
        total = term if total is None else total + term
    return total


def forward_near(dense_ref, weight_ref, *refs):
    *pieces, message_ref, features_ref = refs
    me, count = lax.axis_index("dst"), len(pieces)
    collect(lax.rem(me, count), pieces, features_ref)
    message_ref[...] = half_message(dense_ref, weight_ref, features_ref, lax.div(me, count))


def forward(count, dense_ref, weight_ref, near_ref, *refs):
    pieces, (features_ref, own_ref, *sends, message) = refs[:count], refs[count:]
    me, z = lax.axis_index("dst"), lax.axis_index("src")
    collect(lax.rem(me, count) ^ (2 * (FAR[0] - 2)), pieces, features_ref)
    message[...] = near_ref[...] + half_message(
        dense_ref, weight_ref, features_ref, 1 - lax.div(me, count)
    )
    block = own_ref.shape[0]
    for m in range(len(sends) + 1):
        mine = message[pl.ds(pl.multiple_of((z ^ m) * block, 16), block)]
        if m == 0:
            own_ref[...] = mine
        else:
            sends[m - 1][...] = mine.astype(BF)


def tile_turned(count, dense_ref, near_ref, far_ref, out_ref, features):
    half = lax.div(lax.axis_index("dst"), count)
    depth, width = near_ref.shape
    features[pl.ds(pl.multiple_of(half * depth, 128), depth)] = near_ref[...]
    features[pl.ds(pl.multiple_of((1 - half) * depth, 128), depth)] = far_ref[...]
    rows = out_ref.shape[1]
    step = 256
    for r in range(dense_ref.shape[0] // rows):
        for at in range(0, width, step):
            part = jnp.dot(
                dense_ref[r * rows : (r + 1) * rows],
                features[:, at : at + step],
                preferred_element_type=F32,
            )
            out_ref[r * width + at : r * width + at + step] = part.astype(BF).T


def activate(bias_ref, cotangent_ref, own_ref, *refs):
    *others, pre_ref, grad_ref = refs
    pre = own_ref[...]
    for other in others:
        pre = pre + other[...].astype(F32)
    pre = pre + bias_ref[...].astype(F32)
    sigma = jax.nn.sigmoid(pre)
    pre_ref[...] = pre
    grad_ref[...] = (
        cotangent_ref[...].astype(F32) * sigma * (1.0 + pre * (1.0 - sigma))
    ).astype(BF)


def tree(terms):
    while len(terms) > 1:
        terms = [a + b for a, b in zip(terms[::2], terms[1::2])]
    return terms[0]


def split_row(row):
    at = lax.broadcasted_iota(jnp.int32, (TAIL, row.shape[1]), 0)
    high = row.astype(BF).astype(F32)
    return jnp.where(at == 0, high, jnp.where(at == 1, row - high, 0.0)).astype(BF)


def join_row(tail):
    return jnp.sum(tail.astype(F32), axis=0, keepdims=True)


def half_gradient(core, which, chips, tile_ref, grad, out_ref, piece):
    chip = lax.div(lax.axis_index("dst"), 2)
    for i, m in enumerate(which):
        start = pl.multiple_of((core * chips + (chip ^ m)) * piece, 16)
        out_ref[i * piece : (i + 1) * piece] = jnp.dot(
            tile_ref[pl.ds(start, piece)], grad, preferred_element_type=F32
        ).astype(out_ref.dtype)


def backward_first(chips, tile_ref, *refs):
    *grads, send_ref, bias_ref, grad_ref = refs
    block = grads[0].shape[0]
    z = lax.axis_index("src")
    grads = dict(zip((0, *GRAD), grads))
    for m, piece in grads.items():
        grad_ref[pl.ds(pl.multiple_of((z ^ m) * block, 16), block)] = piece[...]
    rows = [
        jnp.sum(grads[m][...].astype(F32), axis=0, keepdims=True) for m in range(len(grads))
    ]
    tail = split_row(tree(rows))
    bias_ref[...] = jnp.broadcast_to(join_row(tail), bias_ref.shape)
    piece = (send_ref.shape[0] - TAIL) // len(FIRST)
    send_ref[pl.ds(piece * len(FIRST), TAIL)] = tail
    other = 1 - lax.rem(lax.axis_index("dst"), 2)
    half_gradient(other, FIRST, chips, tile_ref, grad_ref[...], send_ref, piece)


def backward_rest(chips, tile_ref, grad_ref, send_ref):
    other = 1 - lax.rem(lax.axis_index("dst"), 2)
    piece = send_ref.shape[0] // len(REST)
    half_gradient(other, REST, chips, tile_ref, grad_ref[...], send_ref, piece)


def backward_keep(chips, tile_ref, grad_ref, keep_ref):
    core = lax.rem(lax.axis_index("dst"), 2)
    piece = keep_ref.shape[0] // chips
    half_gradient(core, range(chips), chips, tile_ref, grad_ref[...], keep_ref, piece)


def add_first(keep_ref, bias_ref, received_ref, total_ref, *sends):
    piece = sends[0].shape[0] - TAIL
    tail = split_row(bias_ref[0:1] + join_row(received_ref[pl.ds(piece * len(FIRST), TAIL)]))
    total_ref[...] = jnp.broadcast_to(join_row(tail), total_ref.shape)
    for i, m in enumerate(FIRST):
        both = keep_ref[pl.ds(m * piece, piece)]
        both = both + received_ref[pl.ds(i * piece, piece)].astype(F32)
        sends[i][0:piece] = both.astype(BF)
        sends[i][piece : piece + TAIL] = tail


def add_rest(keep_ref, total_ref, received_ref, own_ref, *sends):
    piece = own_ref.shape[0]
    for i, m in enumerate(REST):
        both = keep_ref[pl.ds(m * piece, piece)]
        both = both + received_ref[pl.ds(i * piece, piece)].astype(F32)
        if m == 0:
            own_ref[...] = both
        else:
            sends[i][0:piece] = both.astype(BF)
            sends[i][piece : piece + TAIL] = split_row(total_ref[0:1])


def add_chips(own_ref, bias_ref, *refs):
    *received, sum_ref, total_ref = refs
    received = [received[SUMS.index(m)] for m in range(1, len(received) + 1)]
    piece = own_ref.shape[0]
    tails = [join_row(other[pl.ds(piece, TAIL)]) for other in received]
    total_ref[...] = jnp.broadcast_to(tree([bias_ref[0:1]] + tails), total_ref.shape)
    parts = [other[0:piece].astype(F32) for other in received]
    sum_ref[...] = tree([own_ref[...]] + parts).astype(BF)


def add_bands(*refs):
    *parts, out_ref = refs
    out_ref[...] = tree([part[...].astype(F32) for part in parts]).astype(BF)


def spread(which, chunks, out_ref, wide, sems, copies=()):
    me = lax.axis_index("dst")
    rows = chunks[0].shape[0]
    copies = list(copies)
    half = out_ref.shape[0] // 2
    for i, (core, chip) in enumerate(which):
        wide[i] = chunks[i][...].astype(F32)
        start = (lax.rem(me, 2) ^ core) * half + (lax.div(me, 2) ^ chip) * rows
        target = out_ref.at[pl.ds(pl.multiple_of(start, 16), rows)]
        copies.append(pltpu.make_async_copy(wide.at[i], target, sems.at[i]))
        copies[-1].start()
    for copy in copies:
        copy.wait()


def spread_first(which, bias_ref, pre_ref, *refs):
    *chunks, out_ref, row_ref, output_ref, wide, active, sems = refs
    pre = pre_ref[...]
    active[...] = (pre * jax.nn.sigmoid(pre)).astype(BF)
    copies = [
        pltpu.make_async_copy(bias_ref.at[pl.ds(0, 1)], row_ref, sems.at[len(which)]),
        pltpu.make_async_copy(active, output_ref, sems.at[len(which) + 1]),
    ]
    for copy in copies:
        copy.start()
    spread(which, chunks, out_ref, wide, sems, copies)


def spread_last(which, *refs):
    *chunks, _, out_ref, wide, sems = refs
    spread(which, chunks, out_ref, wide, sems)


def swap(x, axis, n, mask):
    return lax.ppermute(x, axis, [(i, i ^ mask) for i in range(n)])


def on_device(features, relation_weight, bias, block_values, block_list, block_count, cotangent):
    n_dst, n_src = lax.axis_size("dst"), lax.axis_size("src")
    own_rows, width = features.shape
    relations, hidden = relation_weight.shape[1:]
    block_size = block_values.shape[5]
    tile_columns = own_rows * n_dst
    block = cotangent.shape[0]
    band_rows = block * n_src
    few = n_dst == 8 and n_src == 4 and (relations * width) % (8 * 16) == 0
    weight = relation_weight.transpose(1, 0, 2).reshape(relations * width, hidden)
    dense, zero = call(
        functools.partial(assemble, band_rows),
        [shape((relations * band_rows, tile_columns), BF), shape(features.shape, BF)],
        (SMEM, SMEM, VMEM),
        block_list.reshape(relations, -1),
        block_count.reshape(-1),
        block_values.reshape(-1, block_size, block_size),
        flops=10**8,
        moved=4 * 2**20,
    )
    if few:
        return few_devices(features, weight, bias, dense, zero, cotangent, relations)
    gathered = lax.all_gather(features, "dst", axis=0, tiled=True)
    tile = jnp.dot(dense, gathered, preferred_element_type=F32).astype(BF)
    tile = tile.reshape(relations, band_rows, width)
    partial = jnp.einsum(
        "rnd,rdh->nh",
        tile,
        weight.reshape(relations, width, hidden),
        preferred_element_type=F32,
    )
    pre = lax.psum_scatter(partial, "src", scatter_dimension=0, tiled=True)
    pre = pre + bias.astype(F32)
    sigma = jax.nn.sigmoid(pre)
    output = (pre * sigma).astype(BF)
    grad = (cotangent.astype(F32) * sigma * (1.0 + pre * (1.0 - sigma))).astype(BF)
    band_grad = lax.all_gather(grad, "src", axis=0, tiled=True)
    weight_term = jnp.einsum("rnd,nh->rdh", tile, band_grad, preferred_element_type=F32)
    weight_grad, bias_grad = lax.psum(
        (weight_term, jnp.sum(grad.astype(F32), axis=0)), ("dst", "src")
    )
    return output, weight_grad.transpose(1, 0, 2), bias_grad


def few_devices(features, weight, bias, dense, zero, cotangent, relations):
    n_dst, n_src = lax.axis_size("dst"), lax.axis_size("src")
    chips = n_dst // 2
    own_rows, width = features.shape
    block, hidden = cotangent.shape
    band_rows = block * n_src
    total_rows = weight.shape[0]
    piece = total_rows // n_dst
    half = n_dst // 2

    def over_chips(x, m):
        return swap(x, "dst", n_dst, 2 * m)

    def over_core(x):
        return swap(x, "dst", n_dst, 1)

    def over_src(x, m):
        return swap(x, "src", n_src, m)

    near = [features] + [over_chips(features, m) for m in range(1, chips)]
    near[1] = near[1] + zero
    far = [over_core(x) for x in near]
    pieces = [x for pair in zip(near, far) for x in pair]
    half = n_dst // 2
    half_shape = shape((own_rows * half, width), BF)
    message_near, features_near = call(
        forward_near,
        [shape((band_rows, hidden), F32), half_shape],
        [VMEM] * (2 + half),
        dense,
        weight,
        *pieces[:half],
        flops=10**9,
        moved=2**20,
    )
    features_far, own, *sends = call(
        functools.partial(forward, half),
        [half_shape, shape((block, hidden), F32)] + [shape((block, hidden), BF)] * (n_src - 1),
        [VMEM] * (3 + half),
        dense,
        weight,
        message_near,
        *[x for m in FAR for x in (near[m], far[m])],
        scratch=[pltpu.VMEM((band_rows, hidden), F32)],
        flops=10**9,
        moved=2**20,
    )
    received = [over_src(x, m + 1) for m, x in enumerate(sends)]
    turned = call(
        functools.partial(tile_turned, half),
        shape((total_rows, band_rows), BF),
        [VMEM] * 3,
        dense,
        features_near,
        features_far,
        scratch=[pltpu.VMEM((own_rows * n_dst, width), BF)],
        flops=2 * 10**9,
        moved=4 * 2**20,
    )
    pre, grad = call(
        activate,
        [shape((block, hidden), F32), shape((block, hidden), BF)],
        [VMEM] * (2 + n_src),
        bias.reshape(1, hidden),
        cotangent,
        own,
        *[received[m - 1] for m in MESSAGE],
    )
    first, bias_part, band_grad = call(
        functools.partial(backward_first, chips),
        [
            shape((piece * len(FIRST) + TAIL, hidden), BF),
            shape((8, hidden), F32),
            shape((band_rows, hidden), BF),
        ],
        [VMEM] * (1 + n_src),
        turned,
        grad,
        *[over_src(grad, m) for m in GRAD],
    )
    rest = call(
        functools.partial(backward_rest, chips),
        shape((piece * len(REST), hidden), BF),
        [VMEM] * 2,
        turned,
        band_grad,
        flops=3 * 10**8,
        moved=2**20,
    )
    keep = call(
        functools.partial(backward_keep, chips),
        shape((piece * chips, hidden), F32),
        [VMEM] * 2,
        turned,
        band_grad,
        flops=3 * 10**8,
        moved=2**20,
    )
    sent = shape((piece + TAIL, hidden), BF)
    bias_part, *sends = call(
        add_first,
        [shape((8, hidden), F32)] + [sent] * len(FIRST),
        [VMEM] * 3,
        keep,
        bias_part,
        over_core(first),
    )
    own, *others = call(
        add_rest,
        [shape((piece, hidden), F32)] + [sent] * (len(REST) - 1),
        [VMEM] * 3,
        keep,
        bias_part,
        over_core(rest),
    )
    sends = dict(zip(FIRST, sends)) | dict(zip(REST, others))
    received = {m: over_chips(x, m) for m, x in sends.items()}
    part, bias_sum = call(
        add_chips,
        [shape((piece, hidden), BF), shape((8, hidden), F32)],
        [VMEM] * (1 + chips),
        own,
        bias_part,
        *[received[m] for m in SUMS],
    )
    chunk = part
    for m in (1, 3):
        chunk = call(
            add_bands, shape((piece, hidden), BF), [VMEM] * 2, chunk, over_src(chunk, m)
        )
    near = [chunk] + [over_chips(chunk, m) for m in range(1, chips)]
    far = [over_core(x) for x in near]
    chunks = {(0, m): x for m, x in enumerate(near)} | {(1, m): x for m, x in enumerate(far)}
    last = [(0, CHUNKS[-1]), (1, CHUNKS[-1])]
    first = [(core, m) for core in range(2) for m in (0, *CHUNKS[:-1])]
    whole = shape((total_rows, hidden), F32)

    weight_grad, bias_grad, output = call(
        functools.partial(spread_first, first),
        [whole, shape((1, hidden), F32), shape((block, hidden), BF)],
        [VMEM] * (2 + len(first)),
        bias_sum,
        pre,
        *[chunks[w] for w in first],
        scratch=[
            pltpu.VMEM((len(first), piece, hidden), F32),
            pltpu.VMEM((block, hidden), BF),
            pltpu.SemaphoreType.DMA((len(first) + 2,)),
        ],
        out_specs=[ANY] * 3,
    )
    weight_grad = call(
        functools.partial(spread_last, last),
        whole,
        [VMEM] * len(last) + [ANY],
        *[chunks[w] for w in last],
        weight_grad,
        scratch=[
            pltpu.VMEM((len(last), piece, hidden), F32),
            pltpu.SemaphoreType.DMA((len(last),)),
        ],
        aliases={len(last): 0},
        out_specs=ANY,
    )
    weight_grad = weight_grad.reshape(relations, width, hidden).transpose(1, 0, 2)
    return output, weight_grad, bias_grad.reshape(hidden)


def solution(mesh):
    in_specs = (
        P(("src", "dst"), None),
        P(),
        P(),
        P("dst", "src", None, None, None, None),
        P("dst", "src", None, None),
        P("dst", "src", None),
        P(("dst", "src"), None),
    )
    out_specs = (P(("dst", "src"), None), P(), P())
    return jax.shard_map(
        on_device, mesh=mesh, in_specs=in_specs, out_specs=out_specs, check_vma=False
    )
```

time: 73 us -> 67.8 us (0.929)
  waiting for transfers between devices: 24.4 us -> 20.2 us
  starting transfers between devices: 35.2 us -> 33.8 us
  Pallas kernels: 8.98 us -> 9.93 us
    ppermute x27, waiting for transfers between devices: 24.4 us -> 20.2 us  [swap(): return lax.ppermute(x, axis, [(i, i ^ mask) for i in range(n)])]
    ppermute x27, starting transfers between devices: 35.2 us -> 33.8 us  [swap(): return lax.ppermute(x, axis, [(i, i ^ mask) for i in range(n)])]
    pallas_call x10 -> x15, Pallas kernels: 8.98 us -> 9.93 us  [call(): pl.pallas_call(body, out_shape=out, in_specs=list(specs), out_specs=out_s...]
  transfers between devices with their start and end apart: 27 -> 27, of which waited for: 11 -> 9; matrix products, arithmetic and copies ran while one was open for 1% -> 1% of each run, Pallas kernels for 6% -> 11%
where the time goes in v4:
time: 67.8 us; the launch traced here: 67.6 us
  starting transfers between devices  33.8 us (50%)
  waiting for transfers between devices  20.2 us (30%)
  Pallas kernels  9.93 us (15%)
  local copies, waits for them, and re-layouts  2.77 us (4%)
  between operations  0.83 us (1%)
    ppermute x27, starting transfers between devices, swap(): return lax.ppermute(x, axis, [(i, i ^ mask) for i in range(n)])  33.8 us
    ppermute x27, waiting for transfers between devices, swap(): return lax.ppermute(x, axis, [(i, i ^ mask) for i in range(n)])  20.2 us
    pallas_call x15, Pallas kernels, call(): pl.pallas_call(body, out_shape=out, in_specs=list(specs), out_specs=out_s...  9.93 us
    unnamed x13, local copies, waits for them, and re-layouts  2.76 us
  transfers between devices with their start and end apart: 27, of which 9 were waited for; matrix products, arithmetic and copies ran while one was open for 1% of the time, Pallas kernels for 11%

profile of v4, /device:TPU:1, one launch (start us, length us, event | category | flops | bytes accessed | tf_op | source)
XLA Modules:
  0.0 67.6 jit_solution(9610965451420714801)
XLA Ops:
  0.6 2.1 %collective-permute-start.1 = (bf16[96,768]{1,0:T(8,128)(2,1)}, bf16[96,768]{1,0:T(8,128)(2,1)S(1)}, u32[]{:S(2)}, u32[]{:S(2)}) collective-permute-start(bf16[96,768]{1,0:T(8,128)(2,1)} %refs_0_.1), channel_id=1, source_target_pairs={{0,8},{4,12},{8,0},{12,4},{16,24},{20,28},{24,16},{28,20},{1,9},{5... | collective-permute-start | bytes 442376 | tf_op jit(solution)/shard_map/ppermute | solution.py:270
  2.7 1.2 %collective-permute-start.5 = (bf16[96,768]{1,0:T(8,128)(2,1)}, bf16[96,768]{1,0:T(8,128)(2,1)S(1)}, u32[]{:S(2)}, u32[]{:S(2)}) collective-permute-start(bf16[96,768]{1,0:T(8,128)(2,1)} %refs_0_.1), channel_id=1, source_target_pairs={{0,16},{4,20},{8,24},{12,28},{16,0},{20,4},{24,8},{28,12},{1,17},{... | collective-permute-start | bytes 442376 | tf_op jit(solution)/shard_map/ppermute | solution.py:270
  4.0 1.2 %collective-permute-start = (bf16[96,768]{1,0:T(8,128)(2,1)}, bf16[96,768]{1,0:T(8,128)(2,1)S(1)}, u32[]{:S(2)}, u32[]{:S(2)}) collective-permute-start(bf16[96,768]{1,0:T(8,128)(2,1)} %refs_0_.1), channel_id=1, source_target_pairs={{0,4},{4,0},{8,12},{12,8},{16,20},{20,16},{24,28},{28,24},{1,5},{5... | collective-permute-start | bytes 442376 | tf_op jit(solution)/shard_map/ppermute | solution.py:270
  5.9 1.4 %copy-done = bf16[1,1,3,16,128,128]{5,4,3,2,1,0:T(8,128)(2,1)S(1)} copy-done((bf16[1,1,3,16,128,128]{5,4,3,2,1,0:T(8,128)(2,1)S(1)}, bf16[1,1,3,16,128,128]{5,4,3,2,1,0:T(8,128)(2,1)}, u32[]{:S(2)}) %copy-start) | copy-done | bytes 1572888
  8.0 1.9 %shard_map.94 = (bf16[1152,768]{1,0:T(8,128)(2,1)S(1)}, bf16[96,768]{1,0:T(8,128)(2,1)S(1)}) custom-call(s32[3,16]{1,0:T(4,128)S(1)} %bitcast.15, s32[3]{0:T(128)S(1)} %bitcast.16, bf16[48,128,128]{2,1,0:T(8,128)(2,1)S(1)} %bitcast.12), custom_call_target="tpu_custom_call" | custom-call | flops 100000000 | bytes 4194304 | tf_op jit(solution)/shard_map/pallas_call | solution.py:29
  10.3 2.1 %collective-permute-start.6 = (bf16[96,768]{1,0:T(8,128)(2,1)S(1)}, bf16[96,768]{1,0:T(8,128)(2,1)S(1)}, u32[]{:S(2)}, u32[]{:S(2)}) collective-permute-start(bf16[96,768]{1,0:T(8,128)(2,1)S(1)} %collective-permute-done.5.refs_2_), channel_id=1, source_target_pairs={{0,4},{4,0},{8,12},{12,8},{16,20},{20,16},{24,28},{28,24},{1,5},{5... | collective-permute-start | bytes 442376 | tf_op jit(solution)/shard_map/ppermute | solution.py:270
  12.4 1.3 %shard_map.95 = (f32[384,256]{1,0:T(8,128)S(1)}, bf16[384,768]{1,0:T(8,128)(2,1)S(1)}) custom-call(bf16[1152,768]{1,0:T(8,128)(2,1)S(1)} %get-tuple-element.27.dense_ref, bf16[2304,256]{1,0:T(8,128)(2,1)S(1)} %bitcast.13, bf16[96,768]{1,0:T(8,128)(2,1)S(1)} %copy-done.4, bf16[96,768]{1,0:T(8,128)(2,1)S(1)} %collective-permute-done.refs_1_, ...), custom_call_target="tpu_custom_call" | custom-call | flops 1000000000 | bytes 1048576 | tf_op jit(solution)/shard_map/pallas_call | solution.py:29
  13.8 1.4 %shard_map.96 = (bf16[384,768]{1,0:T(8,128)(2,1)S(1)}, f32[96,256]{1,0:T(8,128)S(1)}, bf16[96,256]{1,0:T(8,128)(2,1)S(1)}, bf16[96,256]{1,0:T(8,128)(2,1)S(1)}, bf16[96,256]{1,0:T(8,128)(2,1)S(1)}) custom-call(bf16[1152,768]{1,0:T(8,128)(2,1)S(1)} %get-tuple-element.27.dense_ref, bf16[2304,256]{1,0:T(8,128)(2,1)S(1)} %bitcast.14, ...), custom_call_target="tpu_custom_call" | custom-call | flops 1000000000 | bytes 1048576 | tf_op jit(solution)/shard_map/pallas_call | solution.py:29
  15.2 3.4 %collective-permute-start.7 = (bf16[96,256]{1,0:T(8,128)(2,1)S(1)}, bf16[96,256]{1,0:T(8,128)(2,1)S(1)}, u32[]{:S(2)}, u32[]{:S(2)}) collective-permute-start(bf16[96,256]{1,0:T(8,128)(2,1)S(1)} %get-tuple-element.33), channel_id=1, source_target_pairs={{0,3},{1,2},{2,1},{3,0},{4,7},{5,6},{6,5},{7,4},{8,11},{9,10},{10,... | collective-permute-start | bytes 147464 | tf_op jit(solution)/shard_map/ppermute | solution.py:270
  19.0 1.2 %collective-permute-done.7.refs_0_ = bf16[96,256]{1,0:T(8,128)(2,1)S(1)} collective-permute-done((bf16[96,256]{1,0:T(8,128)(2,1)S(1)}, bf16[96,256]{1,0:T(8,128)(2,1)S(1)}, u32[]{:S(2)}, u32[]{:S(2)}) %collective-permute-start.7) | collective-permute-done | bytes 49184 | tf_op jit(solution)/shard_map/ppermute | solution.py:270
  20.1 2.9 %collective-permute-done.8.refs_1_ = bf16[96,256]{1,0:T(8,128)(2,1)S(1)} collective-permute-done((bf16[96,256]{1,0:T(8,128)(2,1)S(1)}, bf16[96,256]{1,0:T(8,128)(2,1)S(1)}, u32[]{:S(2)}, u32[]{:S(2)}) %collective-permute-start.8) | collective-permute-done | bytes 49184 | tf_op jit(solution)/shard_map/ppermute | solution.py:270
  23.1 1.4 %collective-permute-start.12 = (bf16[96,256]{1,0:T(8,128)(2,1)S(1)}, bf16[96,256]{1,0:T(8,128)(2,1)S(1)}, u32[]{:S(2)}, u32[]{:S(2)}) collective-permute-start(bf16[96,256]{1,0:T(8,128)(2,1)S(1)} %get-tuple-element.36.refs_0_), channel_id=1, source_target_pairs={{0,3},{1,2},{2,1},{3,0},{4,7},{5,6},{6,5},{7,4},{8,11},{9,10},{10,... | collective-permute-start | bytes 147464 | tf_op jit(solution)/shard_map/ppermute | solution.py:270
  24.6 2.1 %collective-permute-start.10 = (bf16[96,256]{1,0:T(8,128)(2,1)S(1)}, bf16[96,256]{1,0:T(8,128)(2,1)S(1)}, u32[]{:S(2)}, u32[]{:S(2)}) collective-permute-start(bf16[96,256]{1,0:T(8,128)(2,1)S(1)} %get-tuple-element.36.refs_0_), channel_id=1, source_target_pairs={{0,1},{1,0},{2,3},{3,2},{4,5},{5,4},{6,7},{7,6},{8,9},{9,8},{10,11... | collective-permute-start | bytes 147464 | tf_op jit(solution)/shard_map/ppermute | solution.py:270
  26.7 1.7 %shard_map.97.tile_ref = bf16[2304,384]{1,0:T(8,128)(2,1)S(1)} custom-call(bf16[1152,768]{1,0:T(8,128)(2,1)S(1)} %get-tuple-element.27.dense_ref, bf16[384,768]{1,0:T(8,128)(2,1)S(1)} %get-tuple-element.29.near_ref, bf16[384,768]{1,0:T(8,128)(2,1)S(1)} %get-tuple-element.31.far_ref), custom_call_target="tpu_custom_call" | custom-call | flops 2000000000 | bytes 4194304 | tf_op jit(solution)/shard_map/pallas_call | solution.py:29
  28.4 1.6 %collective-permute-done.11.refs_2_ = bf16[96,256]{1,0:T(8,128)(2,1)S(1)} collective-permute-done((bf16[96,256]{1,0:T(8,128)(2,1)S(1)}, bf16[96,256]{1,0:T(8,128)(2,1)S(1)}, u32[]{:S(2)}, u32[]{:S(2)}) %collective-permute-start.11) | collective-permute-done | bytes 49184 | tf_op jit(solution)/shard_map/ppermute | solution.py:270
  30.4 2.1 %collective-permute-start.13 = (bf16[592,256]{1,0:T(8,128)(2,1)S(1)}, bf16[592,256]{1,0:T(8,128)(2,1)S(1)}, u32[]{:S(2)}, u32[]{:S(2)}) collective-permute-start(bf16[592,256]{1,0:T(8,128)(2,1)S(1)} %get-tuple-element.39), channel_id=1, source_target_pairs={{0,4},{4,0},{8,12},{12,8},{16,20},{20,16},{24,28},{28,24},{1,5},{5... | collective-permute-start | bytes 909320 | tf_op jit(solution)/shard_map/ppermute | solution.py:270
  33.7 0.7 %collective-permute-start.15 = (bf16[304,256]{1,0:T(8,128)(2,1)S(1)}, bf16[304,256]{1,0:T(8,128)(2,1)S(1)}, u32[]{:S(2)}, u32[]{:S(2)}) collective-permute-start(bf16[304,256]{1,0:T(8,128)(2,1)S(1)} %get-tuple-element.42), channel_id=1, source_target_pairs={{0,8},{4,12},{8,0},{12,4},{16,24},{20,28},{24,16},{28,20},{1,9},{5... | collective-permute-start | bytes 466952 | tf_op jit(solution)/shard_map/ppermute | solution.py:270
  34.5 1.3 %collective-permute-start.16 = (bf16[304,256]{1,0:T(8,128)(2,1)S(1)}, bf16[304,256]{1,0:T(8,128)(2,1)S(1)}, u32[]{:S(2)}, u32[]{:S(2)}) collective-permute-start(bf16[304,256]{1,0:T(8,128)(2,1)S(1)} %get-tuple-element.43), channel_id=1, source_target_pairs={{0,16},{4,20},{8,24},{12,28},{16,0},{20,4},{24,8},{28,12},{1,17},{... | collective-permute-start | bytes 466952 | tf_op jit(solution)/shard_map/ppermute | solution.py:270
  35.8 0.7 %collective-permute-start.17 = (bf16[304,256]{1,0:T(8,128)(2,1)S(1)}, bf16[304,256]{1,0:T(8,128)(2,1)S(1)}, u32[]{:S(2)}, u32[]{:S(2)}) collective-permute-start(bf16[304,256]{1,0:T(8,128)(2,1)S(1)} %get-tuple-element.44), channel_id=1, source_target_pairs={{0,24},{4,28},{8,16},{12,20},{16,8},{20,12},{24,0},{28,4},{1,25},{... | collective-permute-start | bytes 466952 | tf_op jit(solution)/shard_map/ppermute | solution.py:270
  36.6 2.4 %collective-permute-done.15.refs_0_ = bf16[304,256]{1,0:T(8,128)(2,1)S(1)} collective-permute-done((bf16[304,256]{1,0:T(8,128)(2,1)S(1)}, bf16[304,256]{1,0:T(8,128)(2,1)S(1)}, u32[]{:S(2)}, u32[]{:S(2)}) %collective-permute-start.15) | collective-permute-done | bytes 155680 | tf_op jit(solution)/shard_map/ppermute | solution.py:270
  39.4 3.9 %collective-permute-done.17.refs_2_ = bf16[304,256]{1,0:T(8,128)(2,1)S(1)} collective-permute-done((bf16[304,256]{1,0:T(8,128)(2,1)S(1)}, bf16[304,256]{1,0:T(8,128)(2,1)S(1)}, u32[]{:S(2)}, u32[]{:S(2)}) %collective-permute-start.17) | collective-permute-done | bytes 155680 | tf_op jit(solution)/shard_map/ppermute | solution.py:270
  43.4 0.7 %collective-permute-start.18 = (bf16[288,256]{1,0:T(8,128)(2,1)S(1)}, bf16[288,256]{1,0:T(8,128)(2,1)S(1)}, u32[]{:S(2)}, u32[]{:S(2)}) collective-permute-start(bf16[288,256]{1,0:T(8,128)(2,1)S(1)} %get-tuple-element.47.refs_0_), channel_id=1, source_target_pairs={{0,1},{1,0},{2,3},{3,2},{4,5},{5,4},{6,7},{7,6},{8,9},{9,8},{10,11... | collective-permute-start | bytes 442376 | tf_op jit(solution)/shard_map/ppermute | solution.py:270
  44.1 3.3 %collective-permute-done.18.refs_1_ = bf16[288,256]{1,0:T(8,128)(2,1)S(1)} collective-permute-done((bf16[288,256]{1,0:T(8,128)(2,1)S(1)}, bf16[288,256]{1,0:T(8,128)(2,1)S(1)}, u32[]{:S(2)}, u32[]{:S(2)}) %collective-permute-start.18) | collective-permute-done | bytes 147488 | tf_op jit(solution)/shard_map/ppermute | solution.py:270
  47.5 1.8 %collective-permute-start.19 = (bf16[288,256]{1,0:T(8,128)(2,1)S(1)}, bf16[288,256]{1,0:T(8,128)(2,1)S(1)}, u32[]{:S(2)}, u32[]{:S(2)}) collective-permute-start(bf16[288,256]{1,0:T(8,128)(2,1)S(1)} %shard_map.105.refs_0_), channel_id=1, source_target_pairs={{0,3},{1,2},{2,1},{3,0},{4,7},{5,6},{6,5},{7,4},{8,11},{9,10},{10,... | collective-permute-start | bytes 442376 | tf_op jit(solution)/shard_map/ppermute | solution.py:270
  49.3 4.1 %collective-permute-done.19.refs_1_ = bf16[288,256]{1,0:T(8,128)(2,1)S(1)} collective-permute-done((bf16[288,256]{1,0:T(8,128)(2,1)S(1)}, bf16[288,256]{1,0:T(8,128)(2,1)S(1)}, u32[]{:S(2)}, u32[]{:S(2)}) %collective-permute-start.19) | collective-permute-done | bytes 147488 | tf_op jit(solution)/shard_map/ppermute | solution.py:270
  54.5 1.7 %collective-permute-start.25 = (bf16[288,256]{1,0:T(8,128)(2,1)S(1)}, bf16[288,256]{1,0:T(8,128)(2,1)S(1)}, u32[]{:S(2)}, u32[]{:S(2)}) collective-permute-start(bf16[288,256]{1,0:T(8,128)(2,1)S(1)} %shard_map.106.refs_0_), channel_id=1, source_target_pairs={{0,24},{4,28},{8,16},{12,20},{16,8},{20,12},{24,0},{28,4},{1,25},{... | collective-permute-start | bytes 442376 | tf_op jit(solution)/shard_map/ppermute | solution.py:270
  56.2 4.3 %collective-permute-start.22 = (bf16[288,256]{1,0:T(8,128)(2,1)S(1)}, bf16[288,256]{1,0:T(8,128)(2,1)S(1)}, u32[]{:S(2)}, u32[]{:S(2)}) collective-permute-start(bf16[288,256]{1,0:T(8,128)(2,1)S(1)} %shard_map.106.refs_0_), channel_id=1, source_target_pairs={{0,4},{4,0},{8,12},{12,8},{16,20},{20,16},{24,28},{28,24},{1,5},{5... | collective-permute-start | bytes 442376 | tf_op jit(solution)/shard_map/ppermute | solution.py:270
  60.6 2.0 %collective-permute-start.24 = (bf16[288,256]{1,0:T(8,128)(2,1)S(1)}, bf16[288,256]{1,0:T(8,128)(2,1)S(1)}, u32[]{:S(2)}, u32[]{:S(2)}) collective-permute-start(bf16[288,256]{1,0:T(8,128)(2,1)S(1)} %collective-permute-done.21.refs_2_), channel_id=1, source_target_pairs={{0,4},{4,0},{8,12},{12,8},{16,20},{20,16},{24,28},{28,24},{1,5},{5... | collective-permute-start | bytes 442376 | tf_op jit(solution)/shard_map/ppermute | solution.py:270
  62.6 0.8 %collective-permute-start.23 = (bf16[288,256]{1,0:T(8,128)(2,1)S(1)}, bf16[288,256]{1,0:T(8,128)(2,1)S(1)}, u32[]{:S(2)}, u32[]{:S(2)}) collective-permute-start(bf16[288,256]{1,0:T(8,128)(2,1)S(1)} %collective-permute-done.20.refs_1_), channel_id=1, source_target_pairs={{0,4},{4,0},{8,12},{12,8},{16,20},{20,16},{24,28},{28,24},{1,5},{5... | collective-permute-start | bytes 442376 | tf_op jit(solution)/shard_map/ppermute | solution.py:270
  63.4 2.0 %collective-permute-start.26 = (bf16[288,256]{1,0:T(8,128)(2,1)S(1)}, bf16[288,256]{1,0:T(8,128)(2,1)S(1)}, u32[]{:S(2)}, u32[]{:S(2)}) collective-permute-start(bf16[288,256]{1,0:T(8,128)(2,1)S(1)} %collective-permute-done.25.refs_0_), channel_id=1, source_target_pairs={{0,4},{4,0},{8,12},{12,8},{16,20},{20,16},{24,28},{28,24},{1,5},{5... | collective-permute-start | bytes 442376 | tf_op jit(solution)/shard_map/ppermute | solution.py:270
  65.4 1.3 %shard_map.107 = (f32[2304,256]{1,0:T(8,128)}, f32[1,256]{1,0:T(1,128)}, bf16[96,256]{1,0:T(8,128)(2,1)}) custom-call(f32[8,256]{1,0:T(8,128)S(1)} %get-tuple-element.45.bias_ref, f32[96,256]{1,0:T(8,128)S(1)} %get-tuple-element.46.pre_ref, bf16[288,256]{1,0:T(8,128)(2,1)S(1)} %shard_map.106.refs_0_, bf16[288,256]{1,0:T(8,128)(2,1)S(1)} %collective-permute-done.20.refs_1_, ...), custom_call_target="tpu_custom_call" | custom-call | tf_op jit(solution)/shard_map/pallas_call | solution.py:29
  66.8 0.9 %shard_map.108 = f32[2304,256]{1,0:T(8,128)} custom-call(bf16[288,256]{1,0:T(8,128)(2,1)S(1)} %collective-permute-done.25.refs_0_, bf16[288,256]{1,0:T(8,128)(2,1)S(1)} %collective-permute-done.26.refs_1_, f32[2304,256]{1,0:T(8,128)} %get-tuple-element.49.refs_2_), custom_call_target="tpu_custom_call", output_to_operand_aliasing={{}: (2, {})} | custom-call | tf_op jit(solution)/shard_map/pallas_call | solution.py:29
  (52 shorter events, 5.5 us)
Async XLA Ops:
  0.6 9.3 %collective-permute-start.1 = (bf16[96,768]{1,0:T(8,128)(2,1)}, bf16[96,768]{1,0:T(8,128)(2,1)S(1)}, u32[]{:S(2)}, u32[]{:S(2)}) collective-permute-start(bf16[96,768]{1,0:T(8,128)(2,1)} %refs_0_.1), channel_id=1, source_target_pairs={{0,8},{4,12},{8,0},{12,4},{16,24},{20,28},{24,16},{28,20},{1,9},{5... | collective-permute-start | bytes 442376 | tf_op jit(solution)/shard_map/ppermute | solution.py:270
  2.7 7.6 %collective-permute-start.5 = (bf16[96,768]{1,0:T(8,128)(2,1)}, bf16[96,768]{1,0:T(8,128)(2,1)S(1)}, u32[]{:S(2)}, u32[]{:S(2)}) collective-permute-start(bf16[96,768]{1,0:T(8,128)(2,1)} %refs_0_.1), channel_id=1, source_target_pairs={{0,16},{4,20},{8,24},{12,28},{16,0},{20,4},{24,8},{28,12},{1,17},{... | collective-permute-start | bytes 442376 | tf_op jit(solution)/shard_map/ppermute | solution.py:270
  4.0 8.4 %collective-permute-start.3 = (bf16[96,768]{1,0:T(8,128)(2,1)}, bf16[96,768]{1,0:T(8,128)(2,1)S(1)}, u32[]{:S(2)}, u32[]{:S(2)}) collective-permute-start(bf16[96,768]{1,0:T(8,128)(2,1)} %refs_0_.1), channel_id=1, source_target_pairs={{0,24},{4,28},{8,16},{12,20},{16,8},{20,12},{24,0},{28,4},{1,25},{... | collective-permute-start | bytes 442376 | tf_op jit(solution)/shard_map/ppermute | solution.py:270
  4.0 8.4 %collective-permute-start = (bf16[96,768]{1,0:T(8,128)(2,1)}, bf16[96,768]{1,0:T(8,128)(2,1)S(1)}, u32[]{:S(2)}, u32[]{:S(2)}) collective-permute-start(bf16[96,768]{1,0:T(8,128)(2,1)} %refs_0_.1), channel_id=1, source_target_pairs={{0,4},{4,0},{8,12},{12,8},{16,20},{20,16},{24,28},{28,24},{1,5},{5... | collective-permute-start | bytes 442376 | tf_op jit(solution)/shard_map/ppermute | solution.py:270
  5.9 1.4 %copy-start = (bf16[1,1,3,16,128,128]{5,4,3,2,1,0:T(8,128)(2,1)S(1)}, bf16[1,1,3,16,128,128]{5,4,3,2,1,0:T(8,128)(2,1)}, u32[]{:S(2)}) copy-start(bf16[1,1,3,16,128,128]{5,4,3,2,1,0:T(8,128)(2,1)} %param.10) | copy-start | bytes 4718596
  8.0 4.4 %copy-start.1 = (bf16[768,3,256]{2,0,1:T(8,128)(2,1)S(1)}, bf16[768,3,256]{2,0,1:T(8,128)(2,1)}, u32[]{:S(2)}) copy-start(bf16[768,3,256]{2,0,1:T(8,128)(2,1)} %param.8) | copy-start | bytes 3538948
  8.0 4.4 %copy-start.4 = (bf16[96,768]{1,0:T(8,128)(2,1)S(1)}, bf16[96,768]{1,0:T(8,128)(2,1)}, u32[]{:S(2)}) copy-start(bf16[96,768]{1,0:T(8,128)(2,1)} %refs_0_.1) | copy-start | bytes 442372
  9.9 2.4 %collective-permute-start.2 = (bf16[96,768]{1,0:T(8,128)(2,1)S(1)}, bf16[96,768]{1,0:T(8,128)(2,1)S(1)}, u32[]{:S(2)}, u32[]{:S(2)}) collective-permute-start(bf16[96,768]{1,0:T(8,128)(2,1)S(1)} %add.3.refs_2_), channel_id=1, source_target_pairs={{0,4},{4,0},{8,12},{12,8},{16,20},{20,16},{24,28},{28,24},{1,5},{5... | collective-permute-start | bytes 442376 | tf_op jit(solution)/shard_map/ppermute | solution.py:270
  10.3 3.5 %collective-permute-start.6 = (bf16[96,768]{1,0:T(8,128)(2,1)S(1)}, bf16[96,768]{1,0:T(8,128)(2,1)S(1)}, u32[]{:S(2)}, u32[]{:S(2)}) collective-permute-start(bf16[96,768]{1,0:T(8,128)(2,1)S(1)} %collective-permute-done.5.refs_2_), channel_id=1, source_target_pairs={{0,4},{4,0},{8,12},{12,8},{16,20},{20,16},{24,28},{28,24},{1,5},{5... | collective-permute-start | bytes 442376 | tf_op jit(solution)/shard_map/ppermute | solution.py:270
  12.4 1.4 %collective-permute-start.4 = (bf16[96,768]{1,0:T(8,128)(2,1)S(1)}, bf16[96,768]{1,0:T(8,128)(2,1)S(1)}, u32[]{:S(2)}, u32[]{:S(2)}) collective-permute-start(bf16[96,768]{1,0:T(8,128)(2,1)S(1)} %collective-permute-done.3.refs_0_), channel_id=1, source_target_pairs={{0,4},{4,0},{8,12},{12,8},{16,20},{20,16},{24,28},{28,24},{1,5},{5... | collective-permute-start | bytes 442376 | tf_op jit(solution)/shard_map/ppermute | solution.py:270
  13.8 5.2 %copy-start.5 = (bf16[256]{0:T(256)(128)(2,1)S(1)}, bf16[256]{0:T(256)(128)(2,1)}, u32[]{:S(2)}) copy-start(bf16[256]{0:T(256)(128)(2,1)} %param.9) | copy-start | bytes 1540
  13.8 9.2 %copy-start.2 = (bf16[96,256]{1,0:T(8,128)(2,1)S(1)}, bf16[96,256]{1,0:T(8,128)(2,1)}, u32[]{:S(2)}) copy-start(bf16[96,256]{1,0:T(8,128)(2,1)} %cotangent_ref.1) | copy-start | bytes 147460
  15.2 4.9 %collective-permute-start.7 = (bf16[96,256]{1,0:T(8,128)(2,1)S(1)}, bf16[96,256]{1,0:T(8,128)(2,1)S(1)}, u32[]{:S(2)}, u32[]{:S(2)}) collective-permute-start(bf16[96,256]{1,0:T(8,128)(2,1)S(1)} %get-tuple-element.33), channel_id=1, source_target_pairs={{0,3},{1,2},{2,1},{3,0},{4,7},{5,6},{6,5},{7,4},{8,11},{9,10},{10,... | collective-permute-start | bytes 147464 | tf_op jit(solution)/shard_map/ppermute | solution.py:270
  18.6 4.4 %collective-permute-start.8 = (bf16[96,256]{1,0:T(8,128)(2,1)S(1)}, bf16[96,256]{1,0:T(8,128)(2,1)S(1)}, u32[]{:S(2)}, u32[]{:S(2)}) collective-permute-start(bf16[96,256]{1,0:T(8,128)(2,1)S(1)} %get-tuple-element.34), channel_id=1, source_target_pairs={{0,2},{1,3},{2,0},{3,1},{4,6},{5,7},{6,4},{7,5},{8,10},{9,11},{10,... | collective-permute-start | bytes 147464 | tf_op jit(solution)/shard_map/ppermute | solution.py:270
  18.6 4.4 %collective-permute-start.9 = (bf16[96,256]{1,0:T(8,128)(2,1)S(1)}, bf16[96,256]{1,0:T(8,128)(2,1)S(1)}, u32[]{:S(2)}, u32[]{:S(2)}) collective-permute-start(bf16[96,256]{1,0:T(8,128)(2,1)S(1)} %get-tuple-element.35), channel_id=1, source_target_pairs={{0,1},{1,0},{2,3},{3,2},{4,5},{5,4},{6,7},{7,6},{8,9},{9,8},{10,11... | collective-permute-start | bytes 147464 | tf_op jit(solution)/shard_map/ppermute | solution.py:270
  23.1 5.3 %collective-permute-start.12 = (bf16[96,256]{1,0:T(8,128)(2,1)S(1)}, bf16[96,256]{1,0:T(8,128)(2,1)S(1)}, u32[]{:S(2)}, u32[]{:S(2)}) collective-permute-start(bf16[96,256]{1,0:T(8,128)(2,1)S(1)} %get-tuple-element.36.refs_0_), channel_id=1, source_target_pairs={{0,3},{1,2},{2,1},{3,0},{4,7},{5,6},{6,5},{7,4},{8,11},{9,10},{10,... | collective-permute-start | bytes 147464 | tf_op jit(solution)/shard_map/ppermute | solution.py:270
  24.5 5.5 %collective-permute-start.11 = (bf16[96,256]{1,0:T(8,128)(2,1)S(1)}, bf16[96,256]{1,0:T(8,128)(2,1)S(1)}, u32[]{:S(2)}, u32[]{:S(2)}) collective-permute-start(bf16[96,256]{1,0:T(8,128)(2,1)S(1)} %get-tuple-element.36.refs_0_), channel_id=1, source_target_pairs={{0,2},{1,3},{2,0},{3,1},{4,6},{5,7},{6,4},{7,5},{8,10},{9,11},{10,... | collective-permute-start | bytes 147464 | tf_op jit(solution)/shard_map/ppermute | solution.py:270
  24.6 5.5 %collective-permute-start.10 = (bf16[96,256]{1,0:T(8,128)(2,1)S(1)}, bf16[96,256]{1,0:T(8,128)(2,1)S(1)}, u32[]{:S(2)}, u32[]{:S(2)}) collective-permute-start(bf16[96,256]{1,0:T(8,128)(2,1)S(1)} %get-tuple-element.36.refs_0_), channel_id=1, source_target_pairs={{0,1},{1,0},{2,3},{3,2},{4,5},{5,4},{6,7},{7,6},{8,9},{9,8},{10,11... | collective-permute-start | bytes 147464 | tf_op jit(solution)/shard_map/ppermute | solution.py:270
  30.4 3.3 %collective-permute-start.13 = (bf16[592,256]{1,0:T(8,128)(2,1)S(1)}, bf16[592,256]{1,0:T(8,128)(2,1)S(1)}, u32[]{:S(2)}, u32[]{:S(2)}) collective-permute-start(bf16[592,256]{1,0:T(8,128)(2,1)S(1)} %get-tuple-element.39), channel_id=1, source_target_pairs={{0,4},{4,0},{8,12},{12,8},{16,20},{20,16},{24,28},{28,24},{1,5},{5... | collective-permute-start | bytes 909320 | tf_op jit(solution)/shard_map/ppermute | solution.py:270
  32.8 3.0 %collective-permute-start.14 = (bf16[576,256]{1,0:T(8,128)(2,1)S(1)}, bf16[576,256]{1,0:T(8,128)(2,1)S(1)}, u32[]{:S(2)}, u32[]{:S(2)}) collective-permute-start(bf16[576,256]{1,0:T(8,128)(2,1)S(1)} %shard_map.102), channel_id=1, source_target_pairs={{0,4},{4,0},{8,12},{12,8},{16,20},{20,16},{24,28},{28,24},{1,5},{5... | collective-permute-start | bytes 884744 | tf_op jit(solution)/shard_map/ppermute | solution.py:270
  33.7 5.3 %collective-permute-start.15 = (bf16[304,256]{1,0:T(8,128)(2,1)S(1)}, bf16[304,256]{1,0:T(8,128)(2,1)S(1)}, u32[]{:S(2)}, u32[]{:S(2)}) collective-permute-start(bf16[304,256]{1,0:T(8,128)(2,1)S(1)} %get-tuple-element.42), channel_id=1, source_target_pairs={{0,8},{4,12},{8,0},{12,4},{16,24},{20,28},{24,16},{28,20},{1,9},{5... | collective-permute-start | bytes 466952 | tf_op jit(solution)/shard_map/ppermute | solution.py:270
  34.5 4.9 %collective-permute-start.16 = (bf16[304,256]{1,0:T(8,128)(2,1)S(1)}, bf16[304,256]{1,0:T(8,128)(2,1)S(1)}, u32[]{:S(2)}, u32[]{:S(2)}) collective-permute-start(bf16[304,256]{1,0:T(8,128)(2,1)S(1)} %get-tuple-element.43), channel_id=1, source_target_pairs={{0,16},{4,20},{8,24},{12,28},{16,0},{20,4},{24,8},{28,12},{1,17},{... | collective-permute-start | bytes 466952 | tf_op jit(solution)/shard_map/ppermute | solution.py:270
  35.8 7.5 %collective-permute-start.17 = (bf16[304,256]{1,0:T(8,128)(2,1)S(1)}, bf16[304,256]{1,0:T(8,128)(2,1)S(1)}, u32[]{:S(2)}, u32[]{:S(2)}) collective-permute-start(bf16[304,256]{1,0:T(8,128)(2,1)S(1)} %get-tuple-element.44), channel_id=1, source_target_pairs={{0,24},{4,28},{8,16},{12,20},{16,8},{20,12},{24,0},{28,4},{1,25},{... | collective-permute-start | bytes 466952 | tf_op jit(solution)/shard_map/ppermute | solution.py:270
  43.4 4.1 %collective-permute-start.18 = (bf16[288,256]{1,0:T(8,128)(2,1)S(1)}, bf16[288,256]{1,0:T(8,128)(2,1)S(1)}, u32[]{:S(2)}, u32[]{:S(2)}) collective-permute-start(bf16[288,256]{1,0:T(8,128)(2,1)S(1)} %get-tuple-element.47.refs_0_), channel_id=1, source_target_pairs={{0,1},{1,0},{2,3},{3,2},{4,5},{5,4},{6,7},{7,6},{8,9},{9,8},{10,11... | collective-permute-start | bytes 442376 | tf_op jit(solution)/shard_map/ppermute | solution.py:270
  47.5 6.0 %collective-permute-start.19 = (bf16[288,256]{1,0:T(8,128)(2,1)S(1)}, bf16[288,256]{1,0:T(8,128)(2,1)S(1)}, u32[]{:S(2)}, u32[]{:S(2)}) collective-permute-start(bf16[288,256]{1,0:T(8,128)(2,1)S(1)} %shard_map.105.refs_0_), channel_id=1, source_target_pairs={{0,3},{1,2},{2,1},{3,0},{4,7},{5,6},{6,5},{7,4},{8,11},{9,10},{10,... | collective-permute-start | bytes 442376 | tf_op jit(solution)/shard_map/ppermute | solution.py:270
  53.5 7.1 %collective-permute-start.21 = (bf16[288,256]{1,0:T(8,128)(2,1)S(1)}, bf16[288,256]{1,0:T(8,128)(2,1)S(1)}, u32[]{:S(2)}, u32[]{:S(2)}) collective-permute-start(bf16[288,256]{1,0:T(8,128)(2,1)S(1)} %shard_map.106.refs_0_), channel_id=1, source_target_pairs={{0,16},{4,20},{8,24},{12,28},{16,0},{20,4},{24,8},{28,12},{1,17},{... | collective-permute-start | bytes 442376 | tf_op jit(solution)/shard_map/ppermute | solution.py:270
  53.8 8.8 %collective-permute-start.20 = (bf16[288,256]{1,0:T(8,128)(2,1)S(1)}, bf16[288,256]{1,0:T(8,128)(2,1)S(1)}, u32[]{:S(2)}, u32[]{:S(2)}) collective-permute-start(bf16[288,256]{1,0:T(8,128)(2,1)S(1)} %shard_map.106.refs_0_), channel_id=1, source_target_pairs={{0,8},{4,12},{8,0},{12,4},{16,24},{20,28},{24,16},{28,20},{1,9},{5... | collective-permute-start | bytes 442376 | tf_op jit(solution)/shard_map/ppermute | solution.py:270
  54.5 8.9 %collective-permute-start.25 = (bf16[288,256]{1,0:T(8,128)(2,1)S(1)}, bf16[288,256]{1,0:T(8,128)(2,1)S(1)}, u32[]{:S(2)}, u32[]{:S(2)}) collective-permute-start(bf16[288,256]{1,0:T(8,128)(2,1)S(1)} %shard_map.106.refs_0_), channel_id=1, source_target_pairs={{0,24},{4,28},{8,16},{12,20},{16,8},{20,12},{24,0},{28,4},{1,25},{... | collective-permute-start | bytes 442376 | tf_op jit(solution)/shard_map/ppermute | solution.py:270
  56.2 9.2 %collective-permute-start.22 = (bf16[288,256]{1,0:T(8,128)(2,1)S(1)}, bf16[288,256]{1,0:T(8,128)(2,1)S(1)}, u32[]{:S(2)}, u32[]{:S(2)}) collective-permute-start(bf16[288,256]{1,0:T(8,128)(2,1)S(1)} %shard_map.106.refs_0_), channel_id=1, source_target_pairs={{0,4},{4,0},{8,12},{12,8},{16,20},{20,16},{24,28},{28,24},{1,5},{5... | collective-permute-start | bytes 442376 | tf_op jit(solution)/shard_map/ppermute | solution.py:270
  60.6 4.9 %collective-permute-start.24 = (bf16[288,256]{1,0:T(8,128)(2,1)S(1)}, bf16[288,256]{1,0:T(8,128)(2,1)S(1)}, u32[]{:S(2)}, u32[]{:S(2)}) collective-permute-start(bf16[288,256]{1,0:T(8,128)(2,1)S(1)} %collective-permute-done.21.refs_2_), channel_id=1, source_target_pairs={{0,4},{4,0},{8,12},{12,8},{16,20},{20,16},{24,28},{28,24},{1,5},{5... | collective-permute-start | bytes 442376 | tf_op jit(solution)/shard_map/ppermute | solution.py:270
  62.6 2.8 %collective-permute-start.23 = (bf16[288,256]{1,0:T(8,128)(2,1)S(1)}, bf16[288,256]{1,0:T(8,128)(2,1)S(1)}, u32[]{:S(2)}, u32[]{:S(2)}) collective-permute-start(bf16[288,256]{1,0:T(8,128)(2,1)S(1)} %collective-permute-done.20.refs_1_), channel_id=1, source_target_pairs={{0,4},{4,0},{8,12},{12,8},{16,20},{20,16},{24,28},{28,24},{1,5},{5... | collective-permute-start | bytes 442376 | tf_op jit(solution)/shard_map/ppermute | solution.py:270
  63.4 3.3 %collective-permute-start.26 = (bf16[288,256]{1,0:T(8,128)(2,1)S(1)}, bf16[288,256]{1,0:T(8,128)(2,1)S(1)}, u32[]{:S(2)}, u32[]{:S(2)}) collective-permute-start(bf16[288,256]{1,0:T(8,128)(2,1)S(1)} %collective-permute-done.25.refs_0_), channel_id=1, source_target_pairs={{0,4},{4,0},{8,12},{12,8},{16,20},{20,16},{24,28},{28,24},{1,5},{5... | collective-permute-start | bytes 442376 | tf_op jit(solution)/shard_map/ppermute | solution.py:270
  (1 other events, 0.7 us)

commit v5 on v4

--- a/solution.py
+++ b/solution.py
@@ -9,11 +9,11 @@
 
 BF = jnp.bfloat16
 F32 = jnp.float32
-MESSAGE = (3, 2, 1)
+MESSAGE = (2, 3, 1)
 GRAD = (1, 2, 3)
 SUMS = (1, 2, 3)
 CHUNKS = (1, 2, 3)
-FIRST, REST = (1, 2), (3, 0)
+FIRST, REST = (2, 1), (3, 0)
 FAR = (3, 2)
 TAIL = 16
 ANY = pl.BlockSpec(memory_space=pl.ANY)
@@ -249,11 +249,12 @@
 
 
 def spread_first(which, bias_ref, pre_ref, *refs):
-    *chunks, out_ref, row_ref, output_ref, wide, active, sems = refs
+    *chunks, out_ref, row_ref, output_ref, wide, active, row, sems = refs
+    row[...] = bias_ref[0:1]
     pre = pre_ref[...]
     active[...] = (pre * jax.nn.sigmoid(pre)).astype(BF)
     copies = [
-        pltpu.make_async_copy(bias_ref.at[pl.ds(0, 1)], row_ref, sems.at[len(which)]),
+        pltpu.make_async_copy(row, row_ref, sems.at[len(which)]),
         pltpu.make_async_copy(active, output_ref, sems.at[len(which) + 1]),
     ]
     for copy in copies:
@@ -461,6 +462,7 @@
         scratch=[
             pltpu.VMEM((len(first), piece, hidden), F32),
             pltpu.VMEM((block, hidden), BF),
+            pltpu.VMEM((1, hidden), F32),
             pltpu.SemaphoreType.DMA((len(first) + 2,)),
         ],
         out_specs=[ANY] * 3,

time: 67.8 us -> 67.7 us (level)
  no operation moved by 1% of the time
where the time goes in v5:
time: 67.7 us; the launch traced here: 67.5 us
  starting transfers between devices  33.2 us (49%)
  waiting for transfers between devices  20.7 us (31%)
  Pallas kernels  9.98 us (15%)
  local copies, waits for them, and re-layouts  2.77 us (4%)
  between operations  0.83 us (1%)
    ppermute x27, starting transfers between devices, swap(): return lax.ppermute(x, axis, [(i, i ^ mask) for i in range(n)])  33.2 us
    ppermute x27, waiting for transfers between devices, swap(): return lax.ppermute(x, axis, [(i, i ^ mask) for i in range(n)])  20.7 us
    pallas_call x15, Pallas kernels, call(): pl.pallas_call(body, out_shape=out, in_specs=list(specs), out_specs=out_s...  9.98 us
    unnamed x13, local copies, waits for them, and re-layouts  2.76 us
  transfers between devices with their start and end apart: 27, of which 9 were waited for; matrix products, arithmetic and copies ran while one was open for 1% of the time, Pallas kernels for 11%

profile of v5, /device:TPU:1, one launch (start us, length us, event | category | flops | bytes accessed | tf_op | source)
XLA Modules:
  0.0 67.5 jit_solution(2993215161306228945)
XLA Ops:
  0.6 2.1 %collective-permute-start.1 = (bf16[96,768]{1,0:T(8,128)(2,1)}, bf16[96,768]{1,0:T(8,128)(2,1)S(1)}, u32[]{:S(2)}, u32[]{:S(2)}) collective-permute-start(bf16[96,768]{1,0:T(8,128)(2,1)} %refs_0_.1), channel_id=1, source_target_pairs={{0,8},{4,12},{8,0},{12,4},{16,24},{20,28},{24,16},{28,20},{1,9},{5... | collective-permute-start | bytes 442376 | tf_op jit(solution)/shard_map/ppermute | solution.py:271
  2.7 1.2 %collective-permute-start.5 = (bf16[96,768]{1,0:T(8,128)(2,1)}, bf16[96,768]{1,0:T(8,128)(2,1)S(1)}, u32[]{:S(2)}, u32[]{:S(2)}) collective-permute-start(bf16[96,768]{1,0:T(8,128)(2,1)} %refs_0_.1), channel_id=1, source_target_pairs={{0,16},{4,20},{8,24},{12,28},{16,0},{20,4},{24,8},{28,12},{1,17},{... | collective-permute-start | bytes 442376 | tf_op jit(solution)/shard_map/ppermute | solution.py:271
  4.0 1.2 %collective-permute-start = (bf16[96,768]{1,0:T(8,128)(2,1)}, bf16[96,768]{1,0:T(8,128)(2,1)S(1)}, u32[]{:S(2)}, u32[]{:S(2)}) collective-permute-start(bf16[96,768]{1,0:T(8,128)(2,1)} %refs_0_.1), channel_id=1, source_target_pairs={{0,4},{4,0},{8,12},{12,8},{16,20},{20,16},{24,28},{28,24},{1,5},{5... | collective-permute-start | bytes 442376 | tf_op jit(solution)/shard_map/ppermute | solution.py:271
  5.9 1.4 %copy-done = bf16[1,1,3,16,128,128]{5,4,3,2,1,0:T(8,128)(2,1)S(1)} copy-done((bf16[1,1,3,16,128,128]{5,4,3,2,1,0:T(8,128)(2,1)S(1)}, bf16[1,1,3,16,128,128]{5,4,3,2,1,0:T(8,128)(2,1)}, u32[]{:S(2)}) %copy-start) | copy-done | bytes 1572888
  8.0 1.9 %shard_map.94 = (bf16[1152,768]{1,0:T(8,128)(2,1)S(1)}, bf16[96,768]{1,0:T(8,128)(2,1)S(1)}) custom-call(s32[3,16]{1,0:T(4,128)S(1)} %bitcast.15, s32[3]{0:T(128)S(1)} %bitcast.16, bf16[48,128,128]{2,1,0:T(8,128)(2,1)S(1)} %bitcast.12), custom_call_target="tpu_custom_call" | custom-call | flops 100000000 | bytes 4194304 | tf_op jit(solution)/shard_map/pallas_call | solution.py:29
  10.2 2.1 %collective-permute-start.6 = (bf16[96,768]{1,0:T(8,128)(2,1)S(1)}, bf16[96,768]{1,0:T(8,128)(2,1)S(1)}, u32[]{:S(2)}, u32[]{:S(2)}) collective-permute-start(bf16[96,768]{1,0:T(8,128)(2,1)S(1)} %collective-permute-done.5.refs_2_), channel_id=1, source_target_pairs={{0,4},{4,0},{8,12},{12,8},{16,20},{20,16},{24,28},{28,24},{1,5},{5... | collective-permute-start | bytes 442376 | tf_op jit(solution)/shard_map/ppermute | solution.py:271
  12.4 1.3 %shard_map.95 = (f32[384,256]{1,0:T(8,128)S(1)}, bf16[384,768]{1,0:T(8,128)(2,1)S(1)}) custom-call(bf16[1152,768]{1,0:T(8,128)(2,1)S(1)} %get-tuple-element.27.dense_ref, bf16[2304,256]{1,0:T(8,128)(2,1)S(1)} %bitcast.13, bf16[96,768]{1,0:T(8,128)(2,1)S(1)} %copy-done.4, bf16[96,768]{1,0:T(8,128)(2,1)S(1)} %collective-permute-done.refs_1_, ...), custom_call_target="tpu_custom_call" | custom-call | flops 1000000000 | bytes 1048576 | tf_op jit(solution)/shard_map/pallas_call | solution.py:29
  13.8 1.4 %shard_map.96 = (bf16[384,768]{1,0:T(8,128)(2,1)S(1)}, f32[96,256]{1,0:T(8,128)S(1)}, bf16[96,256]{1,0:T(8,128)(2,1)S(1)}, bf16[96,256]{1,0:T(8,128)(2,1)S(1)}, bf16[96,256]{1,0:T(8,128)(2,1)S(1)}) custom-call(bf16[1152,768]{1,0:T(8,128)(2,1)S(1)} %get-tuple-element.27.dense_ref, bf16[2304,256]{1,0:T(8,128)(2,1)S(1)} %bitcast.14, ...), custom_call_target="tpu_custom_call" | custom-call | flops 1000000000 | bytes 1048576 | tf_op jit(solution)/shard_map/pallas_call | solution.py:29
  15.2 2.4 %collective-permute-start.7 = (bf16[96,256]{1,0:T(8,128)(2,1)S(1)}, bf16[96,256]{1,0:T(8,128)(2,1)S(1)}, u32[]{:S(2)}, u32[]{:S(2)}) collective-permute-start(bf16[96,256]{1,0:T(8,128)(2,1)S(1)} %get-tuple-element.33), channel_id=1, source_target_pairs={{0,2},{1,3},{2,0},{3,1},{4,6},{5,7},{6,4},{7,5},{8,10},{9,11},{10,... | collective-permute-start | bytes 147464 | tf_op jit(solution)/shard_map/ppermute | solution.py:271
  17.6 1.1 %collective-permute-start.8 = (bf16[96,256]{1,0:T(8,128)(2,1)S(1)}, bf16[96,256]{1,0:T(8,128)(2,1)S(1)}, u32[]{:S(2)}, u32[]{:S(2)}) collective-permute-start(bf16[96,256]{1,0:T(8,128)(2,1)S(1)} %get-tuple-element.34), channel_id=1, source_target_pairs={{0,3},{1,2},{2,1},{3,0},{4,7},{5,6},{6,5},{7,4},{8,11},{9,10},{10,... | collective-permute-start | bytes 147464 | tf_op jit(solution)/shard_map/ppermute | solution.py:271
  19.1 3.2 %collective-permute-done.8.refs_1_ = bf16[96,256]{1,0:T(8,128)(2,1)S(1)} collective-permute-done((bf16[96,256]{1,0:T(8,128)(2,1)S(1)}, bf16[96,256]{1,0:T(8,128)(2,1)S(1)}, u32[]{:S(2)}, u32[]{:S(2)}) %collective-permute-start.8) | collective-permute-done | bytes 49184 | tf_op jit(solution)/shard_map/ppermute | solution.py:271
  22.4 3.4 %collective-permute-start.12 = (bf16[96,256]{1,0:T(8,128)(2,1)S(1)}, bf16[96,256]{1,0:T(8,128)(2,1)S(1)}, u32[]{:S(2)}, u32[]{:S(2)}) collective-permute-start(bf16[96,256]{1,0:T(8,128)(2,1)S(1)} %get-tuple-element.36.refs_0_), channel_id=1, source_target_pairs={{0,3},{1,2},{2,1},{3,0},{4,7},{5,6},{6,5},{7,4},{8,11},{9,10},{10,... | collective-permute-start | bytes 147464 | tf_op jit(solution)/shard_map/ppermute | solution.py:271
  26.1 1.7 %shard_map.97.tile_ref = bf16[2304,384]{1,0:T(8,128)(2,1)S(1)} custom-call(bf16[1152,768]{1,0:T(8,128)(2,1)S(1)} %get-tuple-element.27.dense_ref, bf16[384,768]{1,0:T(8,128)(2,1)S(1)} %get-tuple-element.29.near_ref, bf16[384,768]{1,0:T(8,128)(2,1)S(1)} %get-tuple-element.31.far_ref), custom_call_target="tpu_custom_call" | custom-call | flops 2000000000 | bytes 4194304 | tf_op jit(solution)/shard_map/pallas_call | solution.py:29
  27.9 2.7 %collective-permute-done.11.refs_2_ = bf16[96,256]{1,0:T(8,128)(2,1)S(1)} collective-permute-done((bf16[96,256]{1,0:T(8,128)(2,1)S(1)}, bf16[96,256]{1,0:T(8,128)(2,1)S(1)}, u32[]{:S(2)}, u32[]{:S(2)}) %collective-permute-start.11) | collective-permute-done | bytes 49184 | tf_op jit(solution)/shard_map/ppermute | solution.py:271
  30.9 1.4 %collective-permute-start.13 = (bf16[592,256]{1,0:T(8,128)(2,1)S(1)}, bf16[592,256]{1,0:T(8,128)(2,1)S(1)}, u32[]{:S(2)}, u32[]{:S(2)}) collective-permute-start(bf16[592,256]{1,0:T(8,128)(2,1)S(1)} %get-tuple-element.39), channel_id=1, source_target_pairs={{0,4},{4,0},{8,12},{12,8},{16,20},{20,16},{24,28},{28,24},{1,5},{5... | collective-permute-start | bytes 909320 | tf_op jit(solution)/shard_map/ppermute | solution.py:271
  33.6 1.2 %collective-permute-start.15 = (bf16[304,256]{1,0:T(8,128)(2,1)S(1)}, bf16[304,256]{1,0:T(8,128)(2,1)S(1)}, u32[]{:S(2)}, u32[]{:S(2)}) collective-permute-start(bf16[304,256]{1,0:T(8,128)(2,1)S(1)} %get-tuple-element.42), channel_id=1, source_target_pairs={{0,8},{4,12},{8,0},{12,4},{16,24},{20,28},{24,16},{28,20},{1,9},{5... | collective-permute-start | bytes 466952 | tf_op jit(solution)/shard_map/ppermute | solution.py:271
  34.8 1.0 %collective-permute-start.16 = (bf16[304,256]{1,0:T(8,128)(2,1)S(1)}, bf16[304,256]{1,0:T(8,128)(2,1)S(1)}, u32[]{:S(2)}, u32[]{:S(2)}) collective-permute-start(bf16[304,256]{1,0:T(8,128)(2,1)S(1)} %get-tuple-element.43), channel_id=1, source_target_pairs={{0,16},{4,20},{8,24},{12,28},{16,0},{20,4},{24,8},{28,12},{1,17},{... | collective-permute-start | bytes 466952 | tf_op jit(solution)/shard_map/ppermute | solution.py:271
  36.5 2.4 %collective-permute-done.15.refs_0_ = bf16[304,256]{1,0:T(8,128)(2,1)S(1)} collective-permute-done((bf16[304,256]{1,0:T(8,128)(2,1)S(1)}, bf16[304,256]{1,0:T(8,128)(2,1)S(1)}, u32[]{:S(2)}, u32[]{:S(2)}) %collective-permute-start.15) | collective-permute-done | bytes 155680 | tf_op jit(solution)/shard_map/ppermute | solution.py:271
  38.9 0.8 %collective-permute-done.16.refs_1_ = bf16[304,256]{1,0:T(8,128)(2,1)S(1)} collective-permute-done((bf16[304,256]{1,0:T(8,128)(2,1)S(1)}, bf16[304,256]{1,0:T(8,128)(2,1)S(1)}, u32[]{:S(2)}, u32[]{:S(2)}) %collective-permute-start.16) | collective-permute-done | bytes 155680 | tf_op jit(solution)/shard_map/ppermute | solution.py:271
  39.7 3.5 %collective-permute-done.17.refs_2_ = bf16[304,256]{1,0:T(8,128)(2,1)S(1)} collective-permute-done((bf16[304,256]{1,0:T(8,128)(2,1)S(1)}, bf16[304,256]{1,0:T(8,128)(2,1)S(1)}, u32[]{:S(2)}, u32[]{:S(2)}) %collective-permute-start.17) | collective-permute-done | bytes 155680 | tf_op jit(solution)/shard_map/ppermute | solution.py:271
  43.3 0.7 %collective-permute-start.18 = (bf16[288,256]{1,0:T(8,128)(2,1)S(1)}, bf16[288,256]{1,0:T(8,128)(2,1)S(1)}, u32[]{:S(2)}, u32[]{:S(2)}) collective-permute-start(bf16[288,256]{1,0:T(8,128)(2,1)S(1)} %get-tuple-element.47.refs_0_), channel_id=1, source_target_pairs={{0,1},{1,0},{2,3},{3,2},{4,5},{5,4},{6,7},{7,6},{8,9},{9,8},{10,11... | collective-permute-start | bytes 442376 | tf_op jit(solution)/shard_map/ppermute | solution.py:271
  44.1 3.3 %collective-permute-done.18.refs_1_ = bf16[288,256]{1,0:T(8,128)(2,1)S(1)} collective-permute-done((bf16[288,256]{1,0:T(8,128)(2,1)S(1)}, bf16[288,256]{1,0:T(8,128)(2,1)S(1)}, u32[]{:S(2)}, u32[]{:S(2)}) %collective-permute-start.18) | collective-permute-done | bytes 147488 | tf_op jit(solution)/shard_map/ppermute | solution.py:271
  47.4 2.0 %collective-permute-start.19 = (bf16[288,256]{1,0:T(8,128)(2,1)S(1)}, bf16[288,256]{1,0:T(8,128)(2,1)S(1)}, u32[]{:S(2)}, u32[]{:S(2)}) collective-permute-start(bf16[288,256]{1,0:T(8,128)(2,1)S(1)} %shard_map.105.refs_0_), channel_id=1, source_target_pairs={{0,3},{1,2},{2,1},{3,0},{4,7},{5,6},{6,5},{7,4},{8,11},{9,10},{10,... | collective-permute-start | bytes 442376 | tf_op jit(solution)/shard_map/ppermute | solution.py:271
  49.4 4.0 %collective-permute-done.19.refs_1_ = bf16[288,256]{1,0:T(8,128)(2,1)S(1)} collective-permute-done((bf16[288,256]{1,0:T(8,128)(2,1)S(1)}, bf16[288,256]{1,0:T(8,128)(2,1)S(1)}, u32[]{:S(2)}, u32[]{:S(2)}) %collective-permute-start.19) | collective-permute-done | bytes 147488 | tf_op jit(solution)/shard_map/ppermute | solution.py:271
  53.7 1.1 %collective-permute-start.20 = (bf16[288,256]{1,0:T(8,128)(2,1)S(1)}, bf16[288,256]{1,0:T(8,128)(2,1)S(1)}, u32[]{:S(2)}, u32[]{:S(2)}) collective-permute-start(bf16[288,256]{1,0:T(8,128)(2,1)S(1)} %shard_map.106.refs_0_), channel_id=1, source_target_pairs={{0,8},{4,12},{8,0},{12,4},{16,24},{20,28},{24,16},{28,20},{1,9},{5... | collective-permute-start | bytes 442376 | tf_op jit(solution)/shard_map/ppermute | solution.py:271
  54.8 1.4 %collective-permute-start.25 = (bf16[288,256]{1,0:T(8,128)(2,1)S(1)}, bf16[288,256]{1,0:T(8,128)(2,1)S(1)}, u32[]{:S(2)}, u32[]{:S(2)}) collective-permute-start(bf16[288,256]{1,0:T(8,128)(2,1)S(1)} %shard_map.106.refs_0_), channel_id=1, source_target_pairs={{0,24},{4,28},{8,16},{12,20},{16,8},{20,12},{24,0},{28,4},{1,25},{... | collective-permute-start | bytes 442376 | tf_op jit(solution)/shard_map/ppermute | solution.py:271
  56.2 4.5 %collective-permute-start.22 = (bf16[288,256]{1,0:T(8,128)(2,1)S(1)}, bf16[288,256]{1,0:T(8,128)(2,1)S(1)}, u32[]{:S(2)}, u32[]{:S(2)}) collective-permute-start(bf16[288,256]{1,0:T(8,128)(2,1)S(1)} %shard_map.106.refs_0_), channel_id=1, source_target_pairs={{0,4},{4,0},{8,12},{12,8},{16,20},{20,16},{24,28},{28,24},{1,5},{5... | collective-permute-start | bytes 442376 | tf_op jit(solution)/shard_map/ppermute | solution.py:271
  60.6 1.9 %collective-permute-start.24 = (bf16[288,256]{1,0:T(8,128)(2,1)S(1)}, bf16[288,256]{1,0:T(8,128)(2,1)S(1)}, u32[]{:S(2)}, u32[]{:S(2)}) collective-permute-start(bf16[288,256]{1,0:T(8,128)(2,1)S(1)} %collective-permute-done.21.refs_2_), channel_id=1, source_target_pairs={{0,4},{4,0},{8,12},{12,8},{16,20},{20,16},{24,28},{28,24},{1,5},{5... | collective-permute-start | bytes 442376 | tf_op jit(solution)/shard_map/ppermute | solution.py:271
  62.5 0.9 %collective-permute-start.23 = (bf16[288,256]{1,0:T(8,128)(2,1)S(1)}, bf16[288,256]{1,0:T(8,128)(2,1)S(1)}, u32[]{:S(2)}, u32[]{:S(2)}) collective-permute-start(bf16[288,256]{1,0:T(8,128)(2,1)S(1)} %collective-permute-done.20.refs_1_), channel_id=1, source_target_pairs={{0,4},{4,0},{8,12},{12,8},{16,20},{20,16},{24,28},{28,24},{1,5},{5... | collective-permute-start | bytes 442376 | tf_op jit(solution)/shard_map/ppermute | solution.py:271
  63.5 1.9 %collective-permute-start.26 = (bf16[288,256]{1,0:T(8,128)(2,1)S(1)}, bf16[288,256]{1,0:T(8,128)(2,1)S(1)}, u32[]{:S(2)}, u32[]{:S(2)}) collective-permute-start(bf16[288,256]{1,0:T(8,128)(2,1)S(1)} %collective-permute-done.25.refs_0_), channel_id=1, source_target_pairs={{0,4},{4,0},{8,12},{12,8},{16,20},{20,16},{24,28},{28,24},{1,5},{5... | collective-permute-start | bytes 442376 | tf_op jit(solution)/shard_map/ppermute | solution.py:271
  65.4 1.3 %shard_map.107 = (f32[2304,256]{1,0:T(8,128)}, f32[1,256]{1,0:T(1,128)}, bf16[96,256]{1,0:T(8,128)(2,1)}) custom-call(f32[8,256]{1,0:T(8,128)S(1)} %get-tuple-element.45.bias_ref, f32[96,256]{1,0:T(8,128)S(1)} %get-tuple-element.46.pre_ref, bf16[288,256]{1,0:T(8,128)(2,1)S(1)} %shard_map.106.refs_0_, bf16[288,256]{1,0:T(8,128)(2,1)S(1)} %collective-permute-done.20.refs_1_, ...), custom_call_target="tpu_custom_call" | custom-call | tf_op jit(solution)/shard_map/pallas_call | solution.py:29
  66.7 0.9 %shard_map.108 = f32[2304,256]{1,0:T(8,128)} custom-call(bf16[288,256]{1,0:T(8,128)(2,1)S(1)} %collective-permute-done.25.refs_0_, bf16[288,256]{1,0:T(8,128)(2,1)S(1)} %collective-permute-done.26.refs_1_, f32[2304,256]{1,0:T(8,128)} %get-tuple-element.49.refs_2_), custom_call_target="tpu_custom_call", output_to_operand_aliasing={{}: (2, {})} | custom-call | tf_op jit(solution)/shard_map/pallas_call | solution.py:29
  (52 shorter events, 5.3 us)
Async XLA Ops:
  0.6 9.3 %collective-permute-start.1 = (bf16[96,768]{1,0:T(8,128)(2,1)}, bf16[96,768]{1,0:T(8,128)(2,1)S(1)}, u32[]{:S(2)}, u32[]{:S(2)}) collective-permute-start(bf16[96,768]{1,0:T(8,128)(2,1)} %refs_0_.1), channel_id=1, source_target_pairs={{0,8},{4,12},{8,0},{12,4},{16,24},{20,28},{24,16},{28,20},{1,9},{5... | collective-permute-start | bytes 442376 | tf_op jit(solution)/shard_map/ppermute | solution.py:271
  2.7 7.5 %collective-permute-start.5 = (bf16[96,768]{1,0:T(8,128)(2,1)}, bf16[96,768]{1,0:T(8,128)(2,1)S(1)}, u32[]{:S(2)}, u32[]{:S(2)}) collective-permute-start(bf16[96,768]{1,0:T(8,128)(2,1)} %refs_0_.1), channel_id=1, source_target_pairs={{0,16},{4,20},{8,24},{12,28},{16,0},{20,4},{24,8},{28,12},{1,17},{... | collective-permute-start | bytes 442376 | tf_op jit(solution)/shard_map/ppermute | solution.py:271
  4.0 8.4 %collective-permute-start.3 = (bf16[96,768]{1,0:T(8,128)(2,1)}, bf16[96,768]{1,0:T(8,128)(2,1)S(1)}, u32[]{:S(2)}, u32[]{:S(2)}) collective-permute-start(bf16[96,768]{1,0:T(8,128)(2,1)} %refs_0_.1), channel_id=1, source_target_pairs={{0,24},{4,28},{8,16},{12,20},{16,8},{20,12},{24,0},{28,4},{1,25},{... | collective-permute-start | bytes 442376 | tf_op jit(solution)/shard_map/ppermute | solution.py:271
  4.0 8.4 %collective-permute-start = (bf16[96,768]{1,0:T(8,128)(2,1)}, bf16[96,768]{1,0:T(8,128)(2,1)S(1)}, u32[]{:S(2)}, u32[]{:S(2)}) collective-permute-start(bf16[96,768]{1,0:T(8,128)(2,1)} %refs_0_.1), channel_id=1, source_target_pairs={{0,4},{4,0},{8,12},{12,8},{16,20},{20,16},{24,28},{28,24},{1,5},{5... | collective-permute-start | bytes 442376 | tf_op jit(solution)/shard_map/ppermute | solution.py:271
  5.9 1.4 %copy-start = (bf16[1,1,3,16,128,128]{5,4,3,2,1,0:T(8,128)(2,1)S(1)}, bf16[1,1,3,16,128,128]{5,4,3,2,1,0:T(8,128)(2,1)}, u32[]{:S(2)}) copy-start(bf16[1,1,3,16,128,128]{5,4,3,2,1,0:T(8,128)(2,1)} %param.10) | copy-start | bytes 4718596
  8.0 4.4 %copy-start.1 = (bf16[768,3,256]{2,0,1:T(8,128)(2,1)S(1)}, bf16[768,3,256]{2,0,1:T(8,128)(2,1)}, u32[]{:S(2)}) copy-start(bf16[768,3,256]{2,0,1:T(8,128)(2,1)} %param.8) | copy-start | bytes 3538948
  8.0 4.4 %copy-start.4 = (bf16[96,768]{1,0:T(8,128)(2,1)S(1)}, bf16[96,768]{1,0:T(8,128)(2,1)}, u32[]{:S(2)}) copy-start(bf16[96,768]{1,0:T(8,128)(2,1)} %refs_0_.1) | copy-start | bytes 442372
  10.0 2.4 %collective-permute-start.2 = (bf16[96,768]{1,0:T(8,128)(2,1)S(1)}, bf16[96,768]{1,0:T(8,128)(2,1)S(1)}, u32[]{:S(2)}, u32[]{:S(2)}) collective-permute-start(bf16[96,768]{1,0:T(8,128)(2,1)S(1)} %add.3.refs_2_), channel_id=1, source_target_pairs={{0,4},{4,0},{8,12},{12,8},{16,20},{20,16},{24,28},{28,24},{1,5},{5... | collective-permute-start | bytes 442376 | tf_op jit(solution)/shard_map/ppermute | solution.py:271
  10.2 3.5 %collective-permute-start.6 = (bf16[96,768]{1,0:T(8,128)(2,1)S(1)}, bf16[96,768]{1,0:T(8,128)(2,1)S(1)}, u32[]{:S(2)}, u32[]{:S(2)}) collective-permute-start(bf16[96,768]{1,0:T(8,128)(2,1)S(1)} %collective-permute-done.5.refs_2_), channel_id=1, source_target_pairs={{0,4},{4,0},{8,12},{12,8},{16,20},{20,16},{24,28},{28,24},{1,5},{5... | collective-permute-start | bytes 442376 | tf_op jit(solution)/shard_map/ppermute | solution.py:271
  12.4 1.4 %collective-permute-start.4 = (bf16[96,768]{1,0:T(8,128)(2,1)S(1)}, bf16[96,768]{1,0:T(8,128)(2,1)S(1)}, u32[]{:S(2)}, u32[]{:S(2)}) collective-permute-start(bf16[96,768]{1,0:T(8,128)(2,1)S(1)} %collective-permute-done.3.refs_0_), channel_id=1, source_target_pairs={{0,4},{4,0},{8,12},{12,8},{16,20},{20,16},{24,28},{28,24},{1,5},{5... | collective-permute-start | bytes 442376 | tf_op jit(solution)/shard_map/ppermute | solution.py:271
  13.8 5.1 %copy-start.5 = (bf16[256]{0:T(256)(128)(2,1)S(1)}, bf16[256]{0:T(256)(128)(2,1)}, u32[]{:S(2)}) copy-start(bf16[256]{0:T(256)(128)(2,1)} %param.9) | copy-start | bytes 1540
  13.8 8.5 %copy-start.2 = (bf16[96,256]{1,0:T(8,128)(2,1)S(1)}, bf16[96,256]{1,0:T(8,128)(2,1)}, u32[]{:S(2)}) copy-start(bf16[96,256]{1,0:T(8,128)(2,1)} %cotangent_ref.1) | copy-start | bytes 147460
  15.2 3.9 %collective-permute-start.7 = (bf16[96,256]{1,0:T(8,128)(2,1)S(1)}, bf16[96,256]{1,0:T(8,128)(2,1)S(1)}, u32[]{:S(2)}, u32[]{:S(2)}) collective-permute-start(bf16[96,256]{1,0:T(8,128)(2,1)S(1)} %get-tuple-element.33), channel_id=1, source_target_pairs={{0,2},{1,3},{2,0},{3,1},{4,6},{5,7},{6,4},{7,5},{8,10},{9,11},{10,... | collective-permute-start | bytes 147464 | tf_op jit(solution)/shard_map/ppermute | solution.py:271
  17.6 4.7 %collective-permute-start.8 = (bf16[96,256]{1,0:T(8,128)(2,1)S(1)}, bf16[96,256]{1,0:T(8,128)(2,1)S(1)}, u32[]{:S(2)}, u32[]{:S(2)}) collective-permute-start(bf16[96,256]{1,0:T(8,128)(2,1)S(1)} %get-tuple-element.34), channel_id=1, source_target_pairs={{0,3},{1,2},{2,1},{3,0},{4,7},{5,6},{6,5},{7,4},{8,11},{9,10},{10,... | collective-permute-start | bytes 147464 | tf_op jit(solution)/shard_map/ppermute | solution.py:271
  18.7 3.6 %collective-permute-start.9 = (bf16[96,256]{1,0:T(8,128)(2,1)S(1)}, bf16[96,256]{1,0:T(8,128)(2,1)S(1)}, u32[]{:S(2)}, u32[]{:S(2)}) collective-permute-start(bf16[96,256]{1,0:T(8,128)(2,1)S(1)} %get-tuple-element.35), channel_id=1, source_target_pairs={{0,1},{1,0},{2,3},{3,2},{4,5},{5,4},{6,7},{7,6},{8,9},{9,8},{10,11... | collective-permute-start | bytes 147464 | tf_op jit(solution)/shard_map/ppermute | solution.py:271
  22.4 5.5 %collective-permute-start.12 = (bf16[96,256]{1,0:T(8,128)(2,1)S(1)}, bf16[96,256]{1,0:T(8,128)(2,1)S(1)}, u32[]{:S(2)}, u32[]{:S(2)}) collective-permute-start(bf16[96,256]{1,0:T(8,128)(2,1)S(1)} %get-tuple-element.36.refs_0_), channel_id=1, source_target_pairs={{0,3},{1,2},{2,1},{3,0},{4,7},{5,6},{6,5},{7,4},{8,11},{9,10},{10,... | collective-permute-start | bytes 147464 | tf_op jit(solution)/shard_map/ppermute | solution.py:271
  25.8 4.8 %collective-permute-start.11 = (bf16[96,256]{1,0:T(8,128)(2,1)S(1)}, bf16[96,256]{1,0:T(8,128)(2,1)S(1)}, u32[]{:S(2)}, u32[]{:S(2)}) collective-permute-start(bf16[96,256]{1,0:T(8,128)(2,1)S(1)} %get-tuple-element.36.refs_0_), channel_id=1, source_target_pairs={{0,2},{1,3},{2,0},{3,1},{4,6},{5,7},{6,4},{7,5},{8,10},{9,11},{10,... | collective-permute-start | bytes 147464 | tf_op jit(solution)/shard_map/ppermute | solution.py:271
  25.8 4.8 %collective-permute-start.10 = (bf16[96,256]{1,0:T(8,128)(2,1)S(1)}, bf16[96,256]{1,0:T(8,128)(2,1)S(1)}, u32[]{:S(2)}, u32[]{:S(2)}) collective-permute-start(bf16[96,256]{1,0:T(8,128)(2,1)S(1)} %get-tuple-element.36.refs_0_), channel_id=1, source_target_pairs={{0,1},{1,0},{2,3},{3,2},{4,5},{5,4},{6,7},{7,6},{8,9},{9,8},{10,11... | collective-permute-start | bytes 147464 | tf_op jit(solution)/shard_map/ppermute | solution.py:271
  30.9 2.6 %collective-permute-start.13 = (bf16[592,256]{1,0:T(8,128)(2,1)S(1)}, bf16[592,256]{1,0:T(8,128)(2,1)S(1)}, u32[]{:S(2)}, u32[]{:S(2)}) collective-permute-start(bf16[592,256]{1,0:T(8,128)(2,1)S(1)} %get-tuple-element.39), channel_id=1, source_target_pairs={{0,4},{4,0},{8,12},{12,8},{16,20},{20,16},{24,28},{28,24},{1,5},{5... | collective-permute-start | bytes 909320 | tf_op jit(solution)/shard_map/ppermute | solution.py:271
  32.6 3.2 %collective-permute-start.14 = (bf16[576,256]{1,0:T(8,128)(2,1)S(1)}, bf16[576,256]{1,0:T(8,128)(2,1)S(1)}, u32[]{:S(2)}, u32[]{:S(2)}) collective-permute-start(bf16[576,256]{1,0:T(8,128)(2,1)S(1)} %shard_map.102), channel_id=1, source_target_pairs={{0,4},{4,0},{8,12},{12,8},{16,20},{20,16},{24,28},{28,24},{1,5},{5... | collective-permute-start | bytes 884744 | tf_op jit(solution)/shard_map/ppermute | solution.py:271
  33.6 5.3 %collective-permute-start.15 = (bf16[304,256]{1,0:T(8,128)(2,1)S(1)}, bf16[304,256]{1,0:T(8,128)(2,1)S(1)}, u32[]{:S(2)}, u32[]{:S(2)}) collective-permute-start(bf16[304,256]{1,0:T(8,128)(2,1)S(1)} %get-tuple-element.42), channel_id=1, source_target_pairs={{0,8},{4,12},{8,0},{12,4},{16,24},{20,28},{24,16},{28,20},{1,9},{5... | collective-permute-start | bytes 466952 | tf_op jit(solution)/shard_map/ppermute | solution.py:271
  34.8 4.9 %collective-permute-start.16 = (bf16[304,256]{1,0:T(8,128)(2,1)S(1)}, bf16[304,256]{1,0:T(8,128)(2,1)S(1)}, u32[]{:S(2)}, u32[]{:S(2)}) collective-permute-start(bf16[304,256]{1,0:T(8,128)(2,1)S(1)} %get-tuple-element.43), channel_id=1, source_target_pairs={{0,16},{4,20},{8,24},{12,28},{16,0},{20,4},{24,8},{28,12},{1,17},{... | collective-permute-start | bytes 466952 | tf_op jit(solution)/shard_map/ppermute | solution.py:271
  35.9 7.4 %collective-permute-start.17 = (bf16[304,256]{1,0:T(8,128)(2,1)S(1)}, bf16[304,256]{1,0:T(8,128)(2,1)S(1)}, u32[]{:S(2)}, u32[]{:S(2)}) collective-permute-start(bf16[304,256]{1,0:T(8,128)(2,1)S(1)} %get-tuple-element.44), channel_id=1, source_target_pairs={{0,24},{4,28},{8,16},{12,20},{16,8},{20,12},{24,0},{28,4},{1,25},{... | collective-permute-start | bytes 466952 | tf_op jit(solution)/shard_map/ppermute | solution.py:271
  43.3 4.1 %collective-permute-start.18 = (bf16[288,256]{1,0:T(8,128)(2,1)S(1)}, bf16[288,256]{1,0:T(8,128)(2,1)S(1)}, u32[]{:S(2)}, u32[]{:S(2)}) collective-permute-start(bf16[288,256]{1,0:T(8,128)(2,1)S(1)} %get-tuple-element.47.refs_0_), channel_id=1, source_target_pairs={{0,1},{1,0},{2,3},{3,2},{4,5},{5,4},{6,7},{7,6},{8,9},{9,8},{10,11... | collective-permute-start | bytes 442376 | tf_op jit(solution)/shard_map/ppermute | solution.py:271
  47.4 6.0 %collective-permute-start.19 = (bf16[288,256]{1,0:T(8,128)(2,1)S(1)}, bf16[288,256]{1,0:T(8,128)(2,1)S(1)}, u32[]{:S(2)}, u32[]{:S(2)}) collective-permute-start(bf16[288,256]{1,0:T(8,128)(2,1)S(1)} %shard_map.105.refs_0_), channel_id=1, source_target_pairs={{0,3},{1,2},{2,1},{3,0},{4,7},{5,6},{6,5},{7,4},{8,11},{9,10},{10,... | collective-permute-start | bytes 442376 | tf_op jit(solution)/shard_map/ppermute | solution.py:271
  53.4 7.2 %collective-permute-start.21 = (bf16[288,256]{1,0:T(8,128)(2,1)S(1)}, bf16[288,256]{1,0:T(8,128)(2,1)S(1)}, u32[]{:S(2)}, u32[]{:S(2)}) collective-permute-start(bf16[288,256]{1,0:T(8,128)(2,1)S(1)} %shard_map.106.refs_0_), channel_id=1, source_target_pairs={{0,16},{4,20},{8,24},{12,28},{16,0},{20,4},{24,8},{28,12},{1,17},{... | collective-permute-start | bytes 442376 | tf_op jit(solution)/shard_map/ppermute | solution.py:271
  53.7 8.8 %collective-permute-start.20 = (bf16[288,256]{1,0:T(8,128)(2,1)S(1)}, bf16[288,256]{1,0:T(8,128)(2,1)S(1)}, u32[]{:S(2)}, u32[]{:S(2)}) collective-permute-start(bf16[288,256]{1,0:T(8,128)(2,1)S(1)} %shard_map.106.refs_0_), channel_id=1, source_target_pairs={{0,8},{4,12},{8,0},{12,4},{16,24},{20,28},{24,16},{28,20},{1,9},{5... | collective-permute-start | bytes 442376 | tf_op jit(solution)/shard_map/ppermute | solution.py:271
  54.8 8.7 %collective-permute-start.25 = (bf16[288,256]{1,0:T(8,128)(2,1)S(1)}, bf16[288,256]{1,0:T(8,128)(2,1)S(1)}, u32[]{:S(2)}, u32[]{:S(2)}) collective-permute-start(bf16[288,256]{1,0:T(8,128)(2,1)S(1)} %shard_map.106.refs_0_), channel_id=1, source_target_pairs={{0,24},{4,28},{8,16},{12,20},{16,8},{20,12},{24,0},{28,4},{1,25},{... | collective-permute-start | bytes 442376 | tf_op jit(solution)/shard_map/ppermute | solution.py:271
  56.2 9.2 %collective-permute-start.22 = (bf16[288,256]{1,0:T(8,128)(2,1)S(1)}, bf16[288,256]{1,0:T(8,128)(2,1)S(1)}, u32[]{:S(2)}, u32[]{:S(2)}) collective-permute-start(bf16[288,256]{1,0:T(8,128)(2,1)S(1)} %shard_map.106.refs_0_), channel_id=1, source_target_pairs={{0,4},{4,0},{8,12},{12,8},{16,20},{20,16},{24,28},{28,24},{1,5},{5... | collective-permute-start | bytes 442376 | tf_op jit(solution)/shard_map/ppermute | solution.py:271
  60.6 4.7 %collective-permute-start.24 = (bf16[288,256]{1,0:T(8,128)(2,1)S(1)}, bf16[288,256]{1,0:T(8,128)(2,1)S(1)}, u32[]{:S(2)}, u32[]{:S(2)}) collective-permute-start(bf16[288,256]{1,0:T(8,128)(2,1)S(1)} %collective-permute-done.21.refs_2_), channel_id=1, source_target_pairs={{0,4},{4,0},{8,12},{12,8},{16,20},{20,16},{24,28},{28,24},{1,5},{5... | collective-permute-start | bytes 442376 | tf_op jit(solution)/shard_map/ppermute | solution.py:271
  62.5 2.8 %collective-permute-start.23 = (bf16[288,256]{1,0:T(8,128)(2,1)S(1)}, bf16[288,256]{1,0:T(8,128)(2,1)S(1)}, u32[]{:S(2)}, u32[]{:S(2)}) collective-permute-start(bf16[288,256]{1,0:T(8,128)(2,1)S(1)} %collective-permute-done.20.refs_1_), channel_id=1, source_target_pairs={{0,4},{4,0},{8,12},{12,8},{16,20},{20,16},{24,28},{28,24},{1,5},{5... | collective-permute-start | bytes 442376 | tf_op jit(solution)/shard_map/ppermute | solution.py:271
  63.5 3.2 %collective-permute-start.26 = (bf16[288,256]{1,0:T(8,128)(2,1)S(1)}, bf16[288,256]{1,0:T(8,128)(2,1)S(1)}, u32[]{:S(2)}, u32[]{:S(2)}) collective-permute-start(bf16[288,256]{1,0:T(8,128)(2,1)S(1)} %collective-permute-done.25.refs_0_), channel_id=1, source_target_pairs={{0,4},{4,0},{8,12},{12,8},{16,20},{20,16},{24,28},{28,24},{1,5},{5... | collective-permute-start | bytes 442376 | tf_op jit(solution)/shard_map/ppermute | solution.py:271
  (1 other events, 0.7 us)
